TPU v7x, 256 devices: a whole 4x4x8 slice. The times are simulated.
256 devices in a mesh: group: 8 (over x, core), rows: 32 (over y, z).
Axes of the slice: x: 4, y: 4, z: 8, core: 2. Of those that a mesh axis runs over, the one named last changes fastest.
Arguments:
- embeddings: float32 [131072, 4096], P(('group', 'rows')), may hold values from -600 to 600, as said below
- sketch_matrix: float32 [4096, 256], replicated, may hold values from -0.09375 to 0.09375
Outputs:
- left_basis: float32 [131072, 256], P(('group', 'rows'))
- right_basis: float32 [4096, 256], P('rows')
Inputs may be any that keep to these rules, and one draw needn't show every extreme that they name: `embeddings`: Real-valued entries.
All inputs are finite; a program needn't handle non-finite values.
Results may differ from a plain program's by a relative error of at most 0.00023.
Values sent between devices are 32-bit elements; how exact they have to be, the bound alone decides.
No kernel may reach another device: no remote copies, remote signals or barrier semaphores. Data moves between devices by JAX's collectives and lax.ppermute only.
A program may use at most 64 MiB of HBM per device.

v0:
```python
import math

import jax
import jax.numpy as jnp
from jax import lax
from jax.sharding import PartitionSpec as P

PSTEPS = 6


HIGHEST_PRECISION = lax.Precision.HIGHEST


def from_partner(block, axis, stride):
    count = lax.axis_size(axis)
    route = []
    for low in range(count):
        high = low | 1 << stride
        if high != low and high < count:
            route += [(low, high), (high, low)]
    return lax.ppermute(block, axis, route)


def matmul(left_side, right_side):
    return jnp.dot(
        left_side, right_side, precision=HIGHEST_PRECISION, preferred_element_type=jnp.float32
    )


def inner_rows(left_side, right_side):
    return lax.dot_general(
        left_side,
        right_side,
        (((0,), (0,)), ((), ())),
        precision=HIGHEST_PRECISION,
        preferred_element_type=jnp.float32,
    )


def upper_inverse(lower, identity):
    return jax.scipy.linalg.solve_triangular(lower, identity, lower=True).T


def per_device(embeddings, sketch_matrix):
    rows_here = embeddings.shape[0]
    width_total = embeddings.shape[1]
    sketch = matmul(embeddings, sketch_matrix)
    identity = jnp.eye(sketch.shape[1], dtype=jnp.float32)
    total_rows = rows_here * lax.axis_size("group") * lax.axis_size("rows")
    share_width = width_total // lax.axis_size("rows")
    gram_matrix = inner_rows(sketch, sketch)
    for level_bit in range(lax.axis_size("rows").bit_length() - 1):
        partner = from_partner(gram_matrix, "rows", level_bit)
        gram_matrix = gram_matrix + partner
    for level_bit in range(lax.axis_size("group").bit_length() - 1):
        partner = from_partner(gram_matrix, "group", level_bit)
        gram_matrix = gram_matrix + partner
    lower = jnp.linalg.cholesky(gram_matrix)
    inverse_upper = upper_inverse(lower, identity)
    basis = matmul(sketch, inverse_upper)
    left_basis = basis * math.sqrt(total_rows)
    summed = lax.psum(inner_rows(embeddings, basis), ("group", "rows"))
    cross = inner_rows(summed, summed)
    own_rows = lax.dynamic_slice_in_dim(
        summed, lax.axis_index("rows") * share_width, share_width, 0
    )
    frob = jnp.sqrt(jnp.sum(cross * cross))
    current = cross / frob
    whitening = identity
    for turn_index in range(PSTEPS):
        middle = 1.5 * identity - 0.5 * matmul(whitening, current)
        current = matmul(current, middle)
        whitening = matmul(middle, whitening)
    right_basis = matmul(own_rows, whitening.T) * jnp.sqrt(width_total / frob)
    return (left_basis, right_basis)


def solution(mesh):
    placed = (P(("group", "rows"), None), P())
    return jax.shard_map(
        per_device,
        mesh=mesh,
        in_specs=placed,
        out_specs=(P(("group", "rows"), None), P("rows", None)),
        check_vma=False,
    )
```

profile of v0, /device:TPU:1, one launch (start us, length us, event | category | flops | bytes accessed | tf_op | source)
XLA Modules:
  0.0 464.6 jit_solution(3833203504527808654)
XLA Ops:
  7.2 9.8 %fusion.24 = f32[512,256]{1,0:T(8,128)S(1)} fusion(f32[512,4096]{1,0:T(8,128)} %param.2, f32[4096,256]{1,0:T(8,128)} %param.3), kind=kOutput, calls=%fused_computation.55 | convolution fusion | flops 6442450944 | bytes 13107200 | tf_op jit(solution)/shard_map/dot_general | solution.py:25
  17.0 1.0 fusion.25
  18.0 2.6 collective-permute-start
  20.6 5.0 %collective-permute-done = f32[256,256]{0,1:T(8,128)S(1)} collective-permute-done((f32[256,256]{0,1:T(8,128)S(1)}, f32[256,256]{0,1:T(8,128)S(1)}, u32[]{:S(2)}, u32[]{:S(2)}) %collective-permute-start) | collective-permute-done | bytes 262176 | tf_op jit(solution)/shard_map/ppermute | solution.py:21
  25.6 4.0 collective-permute-start.1
  29.6 11.3 %collective-permute-done.1 = f32[256,256]{0,1:T(8,128)S(1)} collective-permute-done((f32[256,256]{0,1:T(8,128)S(1)}, f32[256,256]{0,1:T(8,128)S(1)}, u32[]{:S(2)}, u32[]{:S(2)}) %collective-permute-start.1) | collective-permute-done | bytes 262176 | tf_op jit(solution)/shard_map/ppermute | solution.py:21
  41.0 6.5 %collective-permute-start.2 = (f32[256,256]{0,1:T(8,128)S(1)}, f32[256,256]{0,1:T(8,128)S(1)}, u32[]{:S(2)}, u32[]{:S(2)}) collective-permute-start(f32[256,256]{0,1:T(8,128)S(1)} %add.53), channel_id=1, source_target_pairs={{0,4},{4,0},{1,5},{5,1},{2,6},{6,2},{3,7},{7,3},{8,12},{12,8},{9,1... | collective-permute-start | bytes 786440 | tf_op jit(solution)/shard_map/ppermute | solution.py:21
  47.5 8.6 %collective-permute-done.2 = f32[256,256]{0,1:T(8,128)S(1)} collective-permute-done((f32[256,256]{0,1:T(8,128)S(1)}, f32[256,256]{0,1:T(8,128)S(1)}, u32[]{:S(2)}, u32[]{:S(2)}) %collective-permute-start.2) | collective-permute-done | bytes 262176 | tf_op jit(solution)/shard_map/ppermute | solution.py:21
  56.1 1.4 collective-permute-start.3
  57.5 3.9 collective-permute-done.3
  61.5 3.0 collective-permute-start.4
  64.5 6.2 %collective-permute-done.4 = f32[256,256]{0,1:T(8,128)S(1)} collective-permute-done((f32[256,256]{0,1:T(8,128)S(1)}, f32[256,256]{0,1:T(8,128)S(1)}, u32[]{:S(2)}, u32[]{:S(2)}) %collective-permute-start.4) | collective-permute-done | bytes 262176 | tf_op jit(solution)/shard_map/ppermute | solution.py:21
  70.8 5.8 %collective-permute-start.5 = (f32[256,256]{0,1:T(8,128)S(1)}, f32[256,256]{0,1:T(8,128)S(1)}, u32[]{:S(2)}, u32[]{:S(2)}) collective-permute-start(f32[256,256]{0,1:T(8,128)S(1)} %add.56), channel_id=1, source_target_pairs={{0,32},{32,0},{64,96},{96,64},{128,160},{160,128},{192,224},{224,1... | collective-permute-start | bytes 786440 | tf_op jit(solution)/shard_map/ppermute | solution.py:21
  76.6 1.2 collective-permute-done.5
  77.8 1.3 collective-permute-start.6
  79.1 6.3 %collective-permute-done.6 = f32[256,256]{0,1:T(8,128)S(1)} collective-permute-done((f32[256,256]{0,1:T(8,128)S(1)}, f32[256,256]{0,1:T(8,128)S(1)}, u32[]{:S(2)}, u32[]{:S(2)}) %collective-permute-start.6) | collective-permute-done | bytes 262176 | tf_op jit(solution)/shard_map/ppermute | solution.py:21
  85.4 3.0 collective-permute-start.7
  88.4 5.4 %collective-permute-done.7 = f32[256,256]{0,1:T(8,128)S(1)} collective-permute-done((f32[256,256]{0,1:T(8,128)S(1)}, f32[256,256]{0,1:T(8,128)S(1)}, u32[]{:S(2)}, u32[]{:S(2)}) %collective-permute-start.7) | collective-permute-done | bytes 262176 | tf_op jit(solution)/shard_map/ppermute | solution.py:21
  94.0 11.7 %cholesky.50 = f32[128,128]{1,0:T(8,128)S(1)} custom-call(f32[128,128]{1,0:T(8,128)S(1)} %cholesky.118), custom_call_target="Cholesky" | custom-call | tf_op jit(solution)/shard_map/jit(cholesky)/cholesky | solution.py:58
  105.8 9.8 %custom-call.15 = f32[1,128,128]{1,2,0:T(8,128)S(1)} custom-call(f32[1,128,128]{2,1,0:T(8,128)S(1)} %get-tuple-element.23), custom_call_target="InvertDiagBlocksLowerTriangular" | custom-call | tf_op jit(solution)/shard_map/jit(cholesky)/cholesky | solution.py:58
  116.1 11.7 %cholesky.105 = f32[128,128]{1,0:T(8,128)S(1)} custom-call(f32[128,128]{1,0:T(8,128)S(1)} %slice_subtract_fusion), custom_call_target="Cholesky" | custom-call | tf_op jit(solution)/shard_map/jit(cholesky)/cholesky | solution.py:58
  127.8 0.7 compare_reduce_fusion
  129.9 4.2 while.1
  130.1 0.6 fusion.80
  130.7 1.4 bitcast_dynamic-update-slice_fusion.2
  132.1 0.6 fusion.80
  132.7 1.4 bitcast_dynamic-update-slice_fusion.2
  134.1 19.7 %custom-call.16 = f32[2,128,128]{1,2,0:T(8,128)S(1)} custom-call(f32[2,128,128]{2,1,0:T(8,128)S(1)} %get-tuple-element.9), custom_call_target="InvertDiagBlocksLowerTriangular" | custom-call | tf_op jit(solution)/shard_map/jit(_solve_triangular)/triangular_solve | solution.py:41
  154.6 1.4 broadcast_multiply_fusion
  156.0 10.8 %convolution_bitcast_fusion = f32[4096,256]{0,1:T(8,128)} fusion(f32[512,256]{1,0:T(8,128)S(1)} %get-tuple-element.27, f32[512,4096]{1,0:T(8,128)} %param.2), kind=kOutput, calls=%fused_computation.2 | convolution fusion | flops 6442450944 | bytes 13107200 | tf_op jit(solution)/shard_map/dot_general | solution.py:31
  166.9 268.5 %all-reduce.3.cloned.1.call-done = f32[4096,256]{0,1:T(8,128)} async-done(((f32[4096,256]{0,1:T(8,128)}), f32[4096,256]{0,1:T(8,128)}) %all-reduce.3.cloned.1.call-update) | async-done | bytes 4194320 | tf_op jit(solution)/shard_map/psum | solution.py:62
  435.3 12.8 %multiply_reduce_fusion = (f32[]{:T(128)}, f32[256,256]{1,0:T(8,128)S(1)}) fusion(f32[4096,256]{0,1:T(8,128)} %all-reduce.3.cloned.1.call-done), kind=kOutput, calls=%fused_computation.24 | convolution fusion | flops 3221356544 | bytes 4456452 | tf_op jit(solution)/shard_map/dot_general | solution.py:31
  449.4 0.4 fusion.15
  449.8 0.4 fusion.4
  450.2 0.4 fusion.26
  450.6 0.4 fusion.27
  451.0 0.4 fusion.3
  451.3 0.4 fusion.28
  451.7 0.4 fusion.29
  452.1 0.4 fusion.2
  452.5 0.4 fusion.30
  452.9 0.4 fusion.31
  453.3 0.4 fusion.1
  453.7 0.4 fusion.32
  454.1 0.4 fusion.33
  454.4 0.4 fusion
  454.8 0.4 fusion.34
  455.3 2.0 convolution_multiply_fusion.6
  (30 shorter events, 2.6 us)
Async XLA Ops:
  7.2 428.2 %all-reduce.3.cloned.1.call-start = ((), (), s32[]{:S(2)}) async-start(), calls=%async_computation | async-start | bytes 8388608 | tf_op jit(solution)/shard_map/psum | solution.py:62
  18.0 7.5 %collective-permute-start = (f32[256,256]{0,1:T(8,128)S(1)}, f32[256,256]{0,1:T(8,128)S(1)}, u32[]{:S(2)}, u32[]{:S(2)}) collective-permute-start(f32[256,256]{0,1:T(8,128)S(1)} %fusion.25), channel_id=1, source_target_pairs={{0,1},{1,0},{2,3},{3,2},{4,5},{5,4},{6,7},{7,6},{8,9},{9,8},{10,11... | collective-permute-start | bytes 786440 | tf_op jit(solution)/shard_map/ppermute | solution.py:21
  25.6 15.3 %collective-permute-start.1 = (f32[256,256]{0,1:T(8,128)S(1)}, f32[256,256]{0,1:T(8,128)S(1)}, u32[]{:S(2)}, u32[]{:S(2)}) collective-permute-start(f32[256,256]{0,1:T(8,128)S(1)} %add.52), channel_id=1, source_target_pairs={{0,2},{2,0},{1,3},{3,1},{4,6},{6,4},{5,7},{7,5},{8,10},{10,8},{9,1... | collective-permute-start | bytes 786440 | tf_op jit(solution)/shard_map/ppermute | solution.py:21
  41.0 15.1 %collective-permute-start.2 = (f32[256,256]{0,1:T(8,128)S(1)}, f32[256,256]{0,1:T(8,128)S(1)}, u32[]{:S(2)}, u32[]{:S(2)}) collective-permute-start(f32[256,256]{0,1:T(8,128)S(1)} %add.53), channel_id=1, source_target_pairs={{0,4},{4,0},{1,5},{5,1},{2,6},{6,2},{3,7},{7,3},{8,12},{12,8},{9,1... | collective-permute-start | bytes 786440 | tf_op jit(solution)/shard_map/ppermute | solution.py:21
  56.1 5.3 %collective-permute-start.3 = (f32[256,256]{0,1:T(8,128)S(1)}, f32[256,256]{0,1:T(8,128)S(1)}, u32[]{:S(2)}, u32[]{:S(2)}) collective-permute-start(f32[256,256]{0,1:T(8,128)S(1)} %add.54), channel_id=1, source_target_pairs={{0,8},{8,0},{1,9},{9,1},{2,10},{10,2},{3,11},{11,3},{4,12},{12,4},... | collective-permute-start | bytes 786440 | tf_op jit(solution)/shard_map/ppermute | solution.py:21
  61.5 9.3 %collective-permute-start.4 = (f32[256,256]{0,1:T(8,128)S(1)}, f32[256,256]{0,1:T(8,128)S(1)}, u32[]{:S(2)}, u32[]{:S(2)}) collective-permute-start(f32[256,256]{0,1:T(8,128)S(1)} %add.55), channel_id=1, source_target_pairs={{0,16},{16,0},{1,17},{17,1},{2,18},{18,2},{3,19},{19,3},{4,20},{20... | collective-permute-start | bytes 786440 | tf_op jit(solution)/shard_map/ppermute | solution.py:21
  70.8 7.0 %collective-permute-start.5 = (f32[256,256]{0,1:T(8,128)S(1)}, f32[256,256]{0,1:T(8,128)S(1)}, u32[]{:S(2)}, u32[]{:S(2)}) collective-permute-start(f32[256,256]{0,1:T(8,128)S(1)} %add.56), channel_id=1, source_target_pairs={{0,32},{32,0},{64,96},{96,64},{128,160},{160,128},{192,224},{224,1... | collective-permute-start | bytes 786440 | tf_op jit(solution)/shard_map/ppermute | solution.py:21
  77.8 7.6 %collective-permute-start.6 = (f32[256,256]{0,1:T(8,128)S(1)}, f32[256,256]{0,1:T(8,128)S(1)}, u32[]{:S(2)}, u32[]{:S(2)}) collective-permute-start(f32[256,256]{0,1:T(8,128)S(1)} %add.57), channel_id=1, source_target_pairs={{0,64},{64,0},{32,96},{96,32},{128,192},{192,128},{160,224},{224,1... | collective-permute-start | bytes 786440 | tf_op jit(solution)/shard_map/ppermute | solution.py:21
  85.4 8.4 %collective-permute-start.7 = (f32[256,256]{0,1:T(8,128)S(1)}, f32[256,256]{0,1:T(8,128)S(1)}, u32[]{:S(2)}, u32[]{:S(2)}) collective-permute-start(f32[256,256]{0,1:T(8,128)S(1)} %add.58), channel_id=1, source_target_pairs={{0,128},{128,0},{32,160},{160,32},{64,192},{192,64},{96,224},{224,... | collective-permute-start | bytes 786440 | tf_op jit(solution)/shard_map/ppermute | solution.py:21
Sparse Core Ops, SparseCore 0:
  167.0 268.2 all-reduce.2
where the time goes:
time: 472 us; the launch traced here: 465 us
  waiting for transfers between devices  316 us (67%)
  other arithmetic  54 us (11%)
  matrix products  45.3 us (10%)
  starting transfers between devices  27.6 us (6%)
  between operations  16.8 us (4%)
    psum x1, waiting for transfers between devices, per_device(): summed = lax.psum(inner_rows(embeddings, basis), ('group', 'rows'))  268 us
    ppermute x8, waiting for transfers between devices, from_partner(): return lax.ppermute(block, axis, route)  47.9 us
    another operation x6, other arithmetic, per_device(): lower = jnp.linalg.cholesky(gram_matrix)  34 us
    ppermute x8, starting transfers between devices, from_partner(): return lax.ppermute(block, axis, route)  27.5 us
    dot_general x3, matrix products, inner_rows(): lax.dot_general(left_side, right_side, (((0,), (0,)), ((), ())), precisio...  24.6 us
    another operation x3, other arithmetic, upper_inverse(): return jax.scipy.linalg.solve_triangular(lower, identity, lower=True).T  19.7 us
    dot_general x20, matrix products, matmul(): jnp.dot(left_side, right_side, precision=HIGHEST_PRECISION, preferred_ele...  19.4 us
  transfers between devices with their start and end apart: 9, of which 9 were waited for; matrix products, arithmetic and copies ran while one was open for 0% of the time, Pallas kernels for 0%

commit v1 on v0

v1 whole, which is shorter than its diff:
```python
import functools
import math

import jax
import jax.numpy as jnp
from jax import lax
from jax.experimental import pallas as pl
from jax.experimental.pallas import tpu as pltpu
from jax.sharding import Mesh
from jax.sharding import PartitionSpec as P

PSTEPS = 6
NX, NC, NY, NZ = 4, 2, 4, 8
AXES = ("x", "c", "y", "z")
CHIPS = ("x", "y", "z")
PANEL, GROUP, LANES = 32, 8, 128
HIGHEST = lax.Precision.HIGHEST
VMEM_LIMIT = 48 * 2**20


def dot(a, b, dims, precision=None):
    return lax.dot_general(
        a, b, (dims, ((), ())), precision=precision, preferred_element_type=jnp.float32
    )


def nn(a, b):
    return dot(a, b, ((1,), (0,)), HIGHEST)


def tn(a, b):
    return dot(a, b, ((0,), (0,)), HIGHEST)


def nt(a, b):
    return dot(a, b, ((1,), (1,)), HIGHEST)


def split(value):
    high = value.astype(jnp.bfloat16)
    return high, (value - high.astype(jnp.float32)).astype(jnp.bfloat16)


def three(a, b, dims):
    return dot(a[0], b[0], dims) + (dot(a[0], b[1], dims) + dot(a[1], b[0], dims))


def products_kernel(
    core_ref, emb_ref, matrix_ref, sketch_ref, keep_ref, send_ref, high, low, gram, s_high, s_low
):
    step = pl.program_id(0)
    rank = matrix_ref.shape[1]

    @pl.when(step < NY)
    def _():
        parts = split(emb_ref[...])
        high[step], low[step] = parts
        term = three(parts, split(matrix_ref[...]), ((1,), (0,)))

        @pl.when(step == 0)
        def _():
            sketch_ref[...] = term

        @pl.when(step > 0)
        def _():
            sketch_ref[...] += term

    @pl.when(step == NY)
    def _():
        sketch = sketch_ref[...]
        s_high[...], s_low[...] = split(sketch)
        gram[...] = tn(sketch, sketch)

    @pl.when(step >= NY)
    def _():
        y = step - NY
        product = three((high[y], low[y]), (s_high[...], s_low[...]), ((0,), (0,)))
        product = product.reshape(NZ, NX, NC, -1, rank)
        first = core_ref[0] == 0
        for x in range(NX):
            halves = [product[:, x, c].reshape(-1, rank) for c in range(NC)]
            extra = [
                gram[pl.ds(pl.multiple_of(NZ * ((c * NX + x) * NY + y), NZ), NZ), :]
                for c in range(NC)
            ]
            size = halves[0].shape[0]
            keep_ref[0, x, :size, :] = jnp.where(first, halves[0], halves[1])
            send_ref[0, x, :size, :] = jnp.where(first, halves[1], halves[0])
            keep_ref[0, x, size:, :] = jnp.where(first, extra[0], extra[1])
            send_ref[0, x, size:, :] = jnp.where(first, extra[1], extra[0])


def products(core, embeddings, matrix):
    rows, width = embeddings.shape
    rank = matrix.shape[1]
    wide = width // NY
    piece = wide // (NX * NC) + NZ
    blocks = jax.ShapeDtypeStruct((NY, NX, piece, rank), jnp.float32)
    spec = pl.BlockSpec((1, NX, piece, rank), lambda i: (jnp.maximum(i - NY, 0), 0, 0, 0))
    return pl.pallas_call(
        products_kernel,
        grid=(2 * NY,),
        out_shape=(jax.ShapeDtypeStruct((rows, rank), jnp.float32), blocks, blocks),
        in_specs=[
            pl.BlockSpec(memory_space=pltpu.SMEM),
            pl.BlockSpec((rows, wide), lambda i: (0, jnp.minimum(i, NY - 1))),
            pl.BlockSpec((wide, rank), lambda i: (jnp.minimum(i, NY - 1), 0)),
        ],
        out_specs=(pl.BlockSpec((rows, rank), lambda i: (0, 0)), spec, spec),
        scratch_shapes=[
            pltpu.VMEM((NY, rows, wide), jnp.bfloat16),
            pltpu.VMEM((NY, rows, wide), jnp.bfloat16),
            pltpu.VMEM((rank, rank), jnp.float32),
            pltpu.VMEM((rows, rank), jnp.bfloat16),
            pltpu.VMEM((rows, rank), jnp.bfloat16),
        ],
        compiler_params=pltpu.CompilerParams(vmem_limit_bytes=VMEM_LIMIT),
        cost_estimate=pl.CostEstimate(
            flops=12 * rows * width * rank, bytes_accessed=24 * 2**20, transcendentals=0
        ),
    )(core, embeddings, matrix)


def join(core_ref, mine_ref, other_ref, out_ref):
    half = mine_ref.shape[0]
    first = core_ref[0] == 0
    out_ref[:half, :] = jnp.where(first, mine_ref[...], other_ref[...])
    out_ref[half:, :] = jnp.where(first, other_ref[...], mine_ref[...])


def eliminate(out_ref, left, right):
    order = left.shape[0]
    sub = lax.broadcasted_iota(jnp.int32, (GROUP, LANES), 0)
    halves = order // LANES
    for start in range(0, order, PANEL):
        home = start // LANES
        rows = pl.ds(start, PANEL)
        left_at = list(range(home, halves))
        right_at = list(range(0, home + 1))
        tiles = [left[rows, pl.ds(h * LANES, LANES)] for h in left_at]
        tiles += [right[rows, pl.ds(h * LANES, LANES)] for h in right_at]
        done = [[] for _ in tiles]
        pivots = []
        for group in range(0, PANEL, GROUP):
            lane = start + group - home * LANES
            tall = tiles[0].shape[0]
            cols = [
                jnp.broadcast_to(tiles[0][:, lane + m : lane + m + 1], (tall, LANES))
                for m in range(GROUP)
            ]
            for j in range(GROUP):
                pivot = cols[j][j : j + 1, :]
                pivots.append(pivot)
                factor = cols[j] * (1.0 / pivot)
                top = jnp.where(sub > j, factor[:GROUP], 0.0)
                factor = top if tall == GROUP else jnp.concatenate([top, factor[GROUP:]], axis=0)
                tiles = [t - factor * t[j : j + 1, :] for t in tiles]
                cols = [
                    q if m <= j else q - factor * q[j : j + 1, :] for m, q in enumerate(cols)
                ]
            for i, t in enumerate(tiles):
                done[i].append(t[:GROUP])
            tiles = [t[GROUP:] for t in tiles]
        scale = lax.rsqrt(jnp.concatenate(pivots, axis=0))
        full = [jnp.concatenate(d, axis=0) * scale for d in done]
        for h, t in zip(right_at, full[len(left_at) :]):
            out_ref[rows, pl.ds(h * LANES, LANES)] = t
        below = start + PANEL
        for i, h in enumerate(left_at):
            first = max(below, h * LANES)
            if first >= (h + 1) * LANES:
                continue
            target = pl.ds(first, (h + 1) * LANES - first)
            flipped = full[i].T[first - h * LANES :]
            for k, g in enumerate(left_at):
                if g >= h:
                    left[target, pl.ds(g * LANES, LANES)] -= nn(flipped, full[k])
            for k, g in enumerate(right_at):
                right[target, pl.ds(g * LANES, LANES)] -= nn(flipped, full[len(left_at) + k])


def basis_kernel(
    scale, core_ref, mine_ref, other_ref, sketch_ref, rows_ref, inverse_ref, basis_ref, out_ref,
    left, right,
):
    order = left.shape[0]
    join(core_ref, mine_ref, other_ref, left)
    across = lax.broadcasted_iota(jnp.int32, (order, order), 1)
    down = lax.broadcasted_iota(jnp.int32, (order, order), 0)
    right[...] = jnp.where(across == down, 1.0, 0.0)
    inverse_ref[...] = jnp.zeros_like(inverse_ref)
    eliminate(inverse_ref, left, right)
    inverse = inverse_ref[...]
    basis_ref[...] = nt(sketch_ref[...], inverse) * scale
    out_ref[...] = nt(rows_ref[...], inverse)


def basis(core, mine, other, sketch, block_rows, scale):
    order = sketch.shape[1]
    return pl.pallas_call(
        functools.partial(basis_kernel, scale),
        out_shape=(
            jax.ShapeDtypeStruct((order, order), jnp.float32),
            jax.ShapeDtypeStruct(sketch.shape, jnp.float32),
            jax.ShapeDtypeStruct(block_rows.shape, jnp.float32),
        ),
        in_specs=[pl.BlockSpec(memory_space=pltpu.SMEM)]
        + [pl.BlockSpec(memory_space=pltpu.VMEM)] * 4,
        scratch_shapes=[pltpu.VMEM((order, order), jnp.float32)] * 2,
        cost_estimate=pl.CostEstimate(flops=10**10, bytes_accessed=2**21, transcendentals=0),
    )(core, mine, other, sketch, block_rows)


def whiten_kernel(width, core_ref, mine_ref, other_ref, inverse_ref, rows_ref, out_ref, inner):
    join(core_ref, mine_ref, other_ref, inner)
    inverse = inverse_ref[...]
    order = inverse.shape[0]
    across = lax.broadcasted_iota(jnp.int32, (order, order), 1)
    down = lax.broadcasted_iota(jnp.int32, (order, order), 0)
    diagonal = jnp.where(across == down, 1.5, 0.0)
    cross = nt(nn(inverse, inner[...]), inverse)
    squares = jnp.sum(cross * cross, axis=0, keepdims=True)
    frob = jnp.sqrt(jnp.sum(squares, axis=1, keepdims=True))
    now = cross / frob
    projected = rows_ref[...] * jnp.sqrt(width / frob)
    for step in range(PSTEPS):
        middle = diagonal - 0.5 * now
        projected = nn(projected, middle)
        if step < PSTEPS - 1:
            now = nn(nn(middle, now), middle)
    out_ref[...] = projected


def whiten(core, mine, other, inverse, block_rows, width):
    order = inverse.shape[0]
    return pl.pallas_call(
        functools.partial(whiten_kernel, width),
        out_shape=jax.ShapeDtypeStruct(block_rows.shape, jnp.float32),
        in_specs=[pl.BlockSpec(memory_space=pltpu.SMEM)]
        + [pl.BlockSpec(memory_space=pltpu.VMEM)] * 4,
        scratch_shapes=[pltpu.VMEM((order, order), jnp.float32)],
        cost_estimate=pl.CostEstimate(flops=10**10, bytes_accessed=2**20, transcendentals=0),
    )(core, mine, other, inverse, block_rows)


def to_core(block):
    return lax.ppermute(block, "c", [(0, 1), (1, 0)])


def along_x(block, flip):
    return lax.ppermute(block, "x", [(x, x ^ flip) for x in range(NX)])


def exchange(blocks, axes):
    return lax.all_to_all(blocks, axes, 0, 0, tiled=True)


def per_device(embeddings, sketch_matrix):
    rank = sketch_matrix.shape[1]
    width = embeddings.shape[1]
    share = width // (NX * NC * NY * NZ)
    total_rows = embeddings.shape[0] * NX * NC * NY * NZ
    chips = NX * NY * NZ
    x, c = lax.axis_index("x"), lax.axis_index("c")
    first_core = c == 0
    core = c.reshape(1).astype(jnp.int32)

    sketch, keep, send = products(core, embeddings, sketch_matrix)
    chip = (keep + to_core(send)).reshape(NY * NX, -1, rank)
    line = jnp.sum(exchange(chip, ("y", "x")), axis=0)
    size = NZ * share
    line = jnp.concatenate([line[:size].reshape(NZ, share, rank), line[size:][:, None]], axis=1)
    own = jnp.sum(exchange(line, "z"), axis=0)
    own_product, own_gram = own[:share], own[share:]

    from_core = to_core(own_product)
    pair = jnp.concatenate(
        [
            jnp.where(first_core, own_product, from_core),
            jnp.where(first_core, from_core, own_product),
        ]
    )
    around = jnp.stack([pair] + [along_x(pair, r) for r in (1, 2, 3)])
    block_rows = jnp.concatenate(
        [lax.dynamic_index_in_dim(around, x ^ r, 0, keepdims=False) for r in range(NX)]
    )

    half = jnp.where(first_core, pair[:, :chips], pair[:, chips:])
    inner = tn(half, pair)
    packet = jnp.concatenate([inner, jnp.broadcast_to(own_gram, inner.shape)], axis=1)
    packet = exchange(packet, CHIPS)
    gram = packet[:, rank:]
    inner_row = jnp.sum(packet[:, :rank], axis=0, keepdims=True)
    inner = exchange(jnp.broadcast_to(inner_row, inner.shape), CHIPS)

    inverse, left_basis, projected = basis(
        core, gram, to_core(gram), sketch, block_rows, math.sqrt(total_rows)
    )
    right_basis = whiten(core, inner, to_core(inner), inverse, projected, width)
    return (left_basis, right_basis)


def solution(mesh):
    fine = Mesh(mesh.devices.reshape(NX, NC, NY, NZ), AXES)
    return jax.shard_map(
        per_device,
        mesh=fine,
        in_specs=(P(AXES, None), P()),
        out_specs=(P(AXES, None), P(("y", "z"), None)),
        check_vma=False,
    )
```

time: 472 us -> 139 us (0.29); the launches traced: 465 us -> 139 us
  waiting for transfers between devices: 316 us -> 24.2 us
  other arithmetic: 54 us -> 1.2 us
  blocking collectives: 0 us -> 50.7 us
  matrix products: 45.3 us -> 0.31 us
  Pallas kernels: 0 us -> 31.6 us
  between operations: 16.8 us -> 0.84 us
    psum x1 -> x0, waiting for transfers between devices: 268 us -> none  [per_device(): summed = lax.psum(inner_rows(embeddings, basis), ('group', 'rows'))]
    another operation x9 -> x2, other arithmetic: 53.7 us -> 0.02 us  [per_device(): around = jnp.stack([pair] + [along_x(pair, r) for r in (1, 2, 3)])]
    all_to_all x0 -> x2, blocking collectives: none -> 50.7 us  [exchange(): return lax.all_to_all(blocks, axes, 0, 0, tiled=True)]
    dot_general x23 -> x1, matrix products: 44 us -> 0.31 us  [dot(): lax.dot_general(a, b, (dims, ((), ())), precision=precision, preferred_el...]
    ppermute x8 -> x7, waiting for transfers between devices: 47.9 us -> 4.81 us  [the longest x4 4.81 us: to_core(): return lax.ppermute(block, 'c', [(0, 1), (1, 0)])]
    pallas_call x0 -> x3, Pallas kernels: none -> 31.6 us  [the longest x1 12.3 us: products(): pl.pallas_call(products_kernel, grid=(2 * NY,), out_shape=(jax.ShapeDtype...]
    all_to_all x0 -> x2, waiting for transfers between devices: none -> 19.4 us  [exchange(): return lax.all_to_all(blocks, axes, 0, 0, tiled=True)]
    ppermute x8 -> x7, starting transfers between devices: 27.5 us -> 14.7 us  [the longest x4 10.7 us: to_core(): return lax.ppermute(block, 'c', [(0, 1), (1, 0)])]
  transfers between devices with their start and end apart: 9 -> 9, of which waited for: 9 -> 4; matrix products, arithmetic and copies ran while one was open for 0% -> 1% of each run, Pallas kernels for 0% -> 8%
where the time goes in v1:
time: 139 us
  blocking collectives  50.7 us (36%)
  Pallas kernels  31.6 us (23%)
  starting transfers between devices  27 us (19%)
  waiting for transfers between devices  24.2 us (17%)
  local copies, waits for them, and re-layouts  3.08 us (2%)
    all_to_all x2, blocking collectives, exchange(): return lax.all_to_all(blocks, axes, 0, 0, tiled=True)  50.7 us
    all_to_all x2, waiting for transfers between devices, exchange(): return lax.all_to_all(blocks, axes, 0, 0, tiled=True)  19.4 us
    all_to_all x2, starting transfers between devices, exchange(): return lax.all_to_all(blocks, axes, 0, 0, tiled=True)  12.3 us
    pallas_call x1, Pallas kernels, products(): pl.pallas_call(products_kernel, grid=(2 * NY,), out_shape=(jax.ShapeDtype...  12.3 us
    pallas_call x1, Pallas kernels, basis(): pl.pallas_call(functools.partial(basis_kernel, scale), out_shape=(jax.Sha...  10.9 us
    ppermute x4, starting transfers between devices, to_core(): return lax.ppermute(block, 'c', [(0, 1), (1, 0)])  10.7 us
    pallas_call x1, Pallas kernels, whiten(): pl.pallas_call(functools.partial(whiten_kernel, width), out_shape=jax.Sha...  8.34 us
    ppermute x4, waiting for transfers between devices, to_core(): return lax.ppermute(block, 'c', [(0, 1), (1, 0)])  4.81 us
  transfers between devices with their start and end apart: 9, of which 4 were waited for; matrix products, arithmetic and copies ran while one was open for 1% of the time, Pallas kernels for 8%

profile of v1, /device:TPU:1, one launch (start us, length us, event | category | flops | bytes accessed | tf_op | source)
XLA Modules:
  0.0 139.0 jit_solution(1542882727877723744)
XLA Ops:
  0.6 12.3 %shard_map.41 = (f32[512,256]{1,0:T(8,128)S(1)}, f32[4,4,136,256]{3,2,1,0:T(8,128)S(1)}, f32[4,4,136,256]{3,2,1,0:T(8,128)S(1)}) custom-call(s32[1]{0:T(128)} %bitcast.core_ref, f32[512,4096]{1,0:T(8,128)} %emb_ref.1, f32[4096,256]{1,0:T(8,128)} %matrix_ref.1), custom_call_target="tpu_custom_call" | custom-call | flops 6442450944 | bytes 25165824 | tf_op jit(solution)/shard_map/pallas_call | solution.py:100
  13.0 0.0 copy-start
  13.0 3.3 %collective-permute-start = (f32[4,4,136,256]{3,2,1,0:T(8,128)S(1)}, f32[4,4,136,256]{3,2,1,0:T(8,128)S(1)}, u32[]{:S(2)}, u32[]{:S(2)}) collective-permute-start(f32[4,4,136,256]{3,2,1,0:T(8,128)S(1)} %get-tuple-element.9), channel_id=1, source_target_pairs={{0,32},{32,0},{1,33},{33,1},{2,34},{34,2},{3,35},{35,3},{4,36},{36... | collective-permute-start | bytes 6684680 | tf_op jit(solution)/shard_map/ppermute | solution.py:247
  16.3 4.0 %collective-permute-done = f32[4,4,136,256]{3,2,1,0:T(8,128)S(1)} collective-permute-done((f32[4,4,136,256]{3,2,1,0:T(8,128)S(1)}, f32[4,4,136,256]{3,2,1,0:T(8,128)S(1)}, u32[]{:S(2)}, u32[]{:S(2)}) %collective-permute-start) | collective-permute-done | bytes 2228256 | tf_op jit(solution)/shard_map/ppermute | solution.py:247
  20.3 0.3 add.16
  20.6 0.0 copy-done
  20.6 34.1 %all_to_all.30 = f32[16,136,256]{2,1,0:T(8,128)S(1)} all-to-all(f32[16,136,256]{2,1,0:T(8,128)S(1)} %bitcast.25), channel_id=1, replica_groups=mesh['x'=4,'c'=2,'y'=4,'z'=8] {'y','x'}, dimensions={0} | all-to-all | bytes 4456448 | tf_op jit(solution)/shard_map/all_to_all | solution.py:255
  54.7 0.1 reduce_sum.27
  54.9 16.6 %all_to_all.31 = f32[8,17,256]{2,1,0:T(8,128)S(1)} all-to-all(f32[8,17,256]{2,1,0:T(8,128)S(1)} %pad_maximum_fusion), channel_id=1, replica_groups=mesh['x'=4,'c'=2,'y'=4,'z'=8] {'z'}, dimensions={0} | all-to-all | bytes 278528 | tf_op jit(solution)/shard_map/all_to_all | solution.py:255
  71.5 3.0 %collective-permute-start.1 = (f32[16,256]{1,0:T(8,128)S(1)}, f32[16,256]{1,0:T(8,128)S(1)}, u32[]{:S(2)}, u32[]{:S(2)}) collective-permute-start(f32[16,256]{1,0:T(8,128)S(1)} %slice.34), channel_id=1, source_target_pairs={{0,32},{32,0},{1,33},{33,1},{2,34},{34,2},{3,35},{35,3},{4,36},{36... | collective-permute-start | bytes 49160 | tf_op jit(solution)/shard_map/ppermute | solution.py:247
  74.5 0.8 collective-permute-done.1
  75.4 0.3 fusion.2
  75.7 1.0 copy.10
  76.7 6.2 %all-to-all-start.2 = ((f32[128,1,512]{2,1,0:T(1,128)}), f32[128,1,512]{2,1,0:T(1,128)S(1)}, u32[]{:S(2)}, u32[]{:S(2)}) async-start(f32[128,1,512]{2,1,0:T(1,128)} %copy.10), calls=%async_computation.2 | async-start | bytes 524288 | tf_op jit(solution)/shard_map/all_to_all | solution.py:255
  82.9 0.8 collective-permute-start.3
  83.7 2.8 %collective-permute-start.4 = (f32[32,256]{1,0:T(8,128)S(1)}, f32[32,256]{1,0:T(8,128)S(1)}, u32[]{:S(2)}, u32[]{:S(2)}) collective-permute-start(f32[32,256]{1,0:T(8,128)S(1)} %get-tuple-element.23), channel_id=1, source_target_pairs={{0,128},{64,192},{128,0},{192,64},{1,129},{65,193},{129,1},{193,65... | collective-permute-start | bytes 98312 | tf_op jit(solution)/shard_map/ppermute | solution.py:251
  86.5 0.4 collective-permute-start.5
  86.8 10.4 %all-to-all-done.2 = f32[128,1,512]{2,1,0:T(1,128)S(1)} async-done(((f32[128,1,512]{2,1,0:T(1,128)}), f32[128,1,512]{2,1,0:T(1,128)S(1)}, u32[]{:S(2)}, u32[]{:S(2)}) %all-to-all-start.2) | async-done | bytes 262176 | tf_op jit(solution)/shard_map/all_to_all | solution.py:255
  97.3 0.0 copy-start.1
  97.4 0.7 broadcast_in_dim.19
  98.1 6.2 %all-to-all-start.3 = ((f32[128,1,256]{2,1,0:T(1,128)}), f32[128,1,256]{2,1,0:T(1,128)S(1)}, u32[]{:S(2)}, u32[]{:S(2)}) async-start(f32[128,1,256]{2,1,0:T(1,128)} %broadcast_in_dim.19), calls=%async_computation.3 | async-start | bytes 262144 | tf_op jit(solution)/shard_map/all_to_all | solution.py:255
  104.3 0.0 collective-permute-done.3
  104.3 0.0 collective-permute-done.4
  104.3 0.0 collective-permute-done.5
  104.3 1.7 %collective-permute-start.2 = (f32[128,256]{1,0:T(8,128)S(1)}, f32[128,256]{1,0:T(8,128)S(1)}, u32[]{:S(2)}, u32[]{:S(2)}) collective-permute-start(f32[128,256]{1,0:T(8,128)S(1)} %get-tuple-element.15.mine_ref), channel_id=1, source_target_pairs={{0,32},{32,0},{1,33},{33,1},{2,34},{34,2},{3,35},{35,3},{4,36},{36... | collective-permute-start | bytes 393224 | tf_op jit(solution)/shard_map/ppermute | solution.py:247
  106.0 0.7 pad_maximum_fusion.2.rows_ref
  106.7 9.0 %all-to-all-done.3 = f32[128,1,256]{2,1,0:T(1,128)S(1)} async-done(((f32[128,1,256]{2,1,0:T(1,128)}), f32[128,1,256]{2,1,0:T(1,128)S(1)}, u32[]{:S(2)}, u32[]{:S(2)}) %all-to-all-start.3) | async-done | bytes 131104 | tf_op jit(solution)/shard_map/all_to_all | solution.py:255
  115.7 0.0 copy-start.2
  115.7 2.7 %collective-permute-start.6 = (f32[128,256]{1,0:T(8,128)S(1)}, f32[128,256]{1,0:T(8,128)S(1)}, u32[]{:S(2)}, u32[]{:S(2)}) collective-permute-start(f32[128,256]{1,0:T(8,128)S(1)} %bitcast.28), channel_id=1, source_target_pairs={{0,32},{32,0},{1,33},{33,1},{2,34},{34,2},{3,35},{35,3},{4,36},{36... | collective-permute-start | bytes 393224 | tf_op jit(solution)/shard_map/ppermute | solution.py:247
  118.4 0.0 collective-permute-done.2.other_ref
  118.4 0.0 copy-start.3
  118.4 0.0 copy-done.1
  118.4 0.6 copy-done.3
  119.1 10.9 %shard_map.42 = (f32[256,256]{1,0:T(8,128)}, f32[512,256]{1,0:T(8,128)}, f32[128,256]{1,0:T(8,128)}) custom-call(s32[1]{0:T(128)} %bitcast.core_ref, f32[128,256]{1,0:T(8,128)} %copy-done.1, f32[128,256]{1,0:T(8,128)} %copy-done.3, f32[512,256]{1,0:T(8,128)} %copy-done, f32[128,256]{1,0:T(8,128)} %pad_maximum_fusion.2.rows_ref), custom_call_target="tpu_custom_call" | custom-call | flops 10000000000 | bytes 2097152 | tf_op jit(solution)/shard_map/pallas_call | solution.py:200
  130.0 0.0 copy-done.2
  130.0 0.0 collective-permute-done.6.other_ref
  130.0 0.0 copy-start.4
  130.0 0.6 copy-done.4
  130.6 8.3 %shard_map.43 = f32[128,256]{1,0:T(8,128)} custom-call(s32[1]{0:T(128)} %bitcast.core_ref, f32[128,256]{1,0:T(8,128)} %bitcast.29, f32[128,256]{1,0:T(8,128)} %copy-done.4, f32[256,256]{1,0:T(8,128)} %get-tuple-element.12.inverse_ref, f32[128,256]{1,0:T(8,128)} %get-tuple-element.13.rows_ref), custom_call_target="tpu_custom_call" | custom-call | flops 10000000000 | bytes 1048576 | tf_op jit(solution)/shard_map/pallas_call | solution.py:236
  (16 shorter events, 0.2 us)
Async XLA Ops:
  13.0 7.6 %copy-start = (f32[512,256]{1,0:T(8,128)}, f32[512,256]{1,0:T(8,128)S(1)}, u32[]{:S(2)}) copy-start(f32[512,256]{1,0:T(8,128)S(1)} %get-tuple-element.10.sketch_ref) | copy-start | bytes 1572868
  13.0 7.3 %collective-permute-start = (f32[4,4,136,256]{3,2,1,0:T(8,128)S(1)}, f32[4,4,136,256]{3,2,1,0:T(8,128)S(1)}, u32[]{:S(2)}, u32[]{:S(2)}) collective-permute-start(f32[4,4,136,256]{3,2,1,0:T(8,128)S(1)} %get-tuple-element.9), channel_id=1, source_target_pairs={{0,32},{32,0},{1,33},{33,1},{2,34},{34,2},{3,35},{35,3},{4,36},{36... | collective-permute-start | bytes 6684680 | tf_op jit(solution)/shard_map/ppermute | solution.py:247
  71.5 3.8 %collective-permute-start.1 = (f32[16,256]{1,0:T(8,128)S(1)}, f32[16,256]{1,0:T(8,128)S(1)}, u32[]{:S(2)}, u32[]{:S(2)}) collective-permute-start(f32[16,256]{1,0:T(8,128)S(1)} %slice.34), channel_id=1, source_target_pairs={{0,32},{32,0},{1,33},{33,1},{2,34},{34,2},{3,35},{35,3},{4,36},{36... | collective-permute-start | bytes 49160 | tf_op jit(solution)/shard_map/ppermute | solution.py:247
  76.7 20.6 %all-to-all-start.2 = ((f32[128,1,512]{2,1,0:T(1,128)}), f32[128,1,512]{2,1,0:T(1,128)S(1)}, u32[]{:S(2)}, u32[]{:S(2)}) async-start(f32[128,1,512]{2,1,0:T(1,128)} %copy.10), calls=%async_computation.2 | async-start | bytes 524288 | tf_op jit(solution)/shard_map/all_to_all | solution.py:255
  82.9 21.4 %collective-permute-start.3 = (f32[32,256]{1,0:T(8,128)S(1)}, f32[32,256]{1,0:T(8,128)S(1)}, u32[]{:S(2)}, u32[]{:S(2)}) collective-permute-start(f32[32,256]{1,0:T(8,128)S(1)} %get-tuple-element.23), channel_id=1, source_target_pairs={{0,64},{64,0},{128,192},{192,128},{1,65},{65,1},{129,193},{193,129... | collective-permute-start | bytes 98312 | tf_op jit(solution)/shard_map/ppermute | solution.py:251
  83.7 20.6 %collective-permute-start.4 = (f32[32,256]{1,0:T(8,128)S(1)}, f32[32,256]{1,0:T(8,128)S(1)}, u32[]{:S(2)}, u32[]{:S(2)}) collective-permute-start(f32[32,256]{1,0:T(8,128)S(1)} %get-tuple-element.23), channel_id=1, source_target_pairs={{0,128},{64,192},{128,0},{192,64},{1,129},{65,193},{129,1},{193,65... | collective-permute-start | bytes 98312 | tf_op jit(solution)/shard_map/ppermute | solution.py:251
  86.5 17.8 %collective-permute-start.5 = (f32[32,256]{1,0:T(8,128)S(1)}, f32[32,256]{1,0:T(8,128)S(1)}, u32[]{:S(2)}, u32[]{:S(2)}) collective-permute-start(f32[32,256]{1,0:T(8,128)S(1)} %get-tuple-element.23), channel_id=1, source_target_pairs={{0,192},{64,128},{128,64},{192,0},{1,193},{65,129},{129,65},{193,1... | collective-permute-start | bytes 98312 | tf_op jit(solution)/shard_map/ppermute | solution.py:251
  97.3 21.1 %copy-start.1 = (f32[128,256]{1,0:T(8,128)}, f32[128,256]{1,0:T(8,128)S(1)}, u32[]{:S(2)}) copy-start(f32[128,256]{1,0:T(8,128)S(1)} %get-tuple-element.15.mine_ref) | copy-start | bytes 393220
  98.1 17.6 %all-to-all-start.3 = ((f32[128,1,256]{2,1,0:T(1,128)}), f32[128,1,256]{2,1,0:T(1,128)S(1)}, u32[]{:S(2)}, u32[]{:S(2)}) async-start(f32[128,1,256]{2,1,0:T(1,128)} %broadcast_in_dim.19), calls=%async_computation.3 | async-start | bytes 262144 | tf_op jit(solution)/shard_map/all_to_all | solution.py:255
  104.3 14.1 %collective-permute-start.2 = (f32[128,256]{1,0:T(8,128)S(1)}, f32[128,256]{1,0:T(8,128)S(1)}, u32[]{:S(2)}, u32[]{:S(2)}) collective-permute-start(f32[128,256]{1,0:T(8,128)S(1)} %get-tuple-element.15.mine_ref), channel_id=1, source_target_pairs={{0,32},{32,0},{1,33},{33,1},{2,34},{34,2},{3,35},{35,3},{4,36},{36... | collective-permute-start | bytes 393224 | tf_op jit(solution)/shard_map/ppermute | solution.py:247
  115.7 14.3 %copy-start.2 = (f32[128,1,256]{2,0,1:T(8,128)}, f32[128,1,256]{2,0,1:T(8,128)S(1)}, u32[]{:S(2)}) copy-start(f32[128,1,256]{2,0,1:T(8,128)S(1)} %copy.19) | copy-start | bytes 393220
  115.7 14.3 %collective-permute-start.6 = (f32[128,256]{1,0:T(8,128)S(1)}, f32[128,256]{1,0:T(8,128)S(1)}, u32[]{:S(2)}, u32[]{:S(2)}) collective-permute-start(f32[128,256]{1,0:T(8,128)S(1)} %bitcast.28), channel_id=1, source_target_pairs={{0,32},{32,0},{1,33},{33,1},{2,34},{34,2},{3,35},{35,3},{4,36},{36... | collective-permute-start | bytes 393224 | tf_op jit(solution)/shard_map/ppermute | solution.py:247
  118.4 0.7 copy-start.3
  130.0 0.7 copy-start.4

commit v2 on v1

--- a/solution.py
+++ b/solution.py
@@ -16,6 +16,7 @@
 PANEL, GROUP, LANES = 32, 8, 128
 HIGHEST = lax.Precision.HIGHEST
 VMEM_LIMIT = 48 * 2**20
+NN, TN, NT = ((1,), (0,)), ((0,), (0,)), ((1,), (1,))
 
 
 def dot(a, b, dims, precision=None):
@@ -218,16 +219,17 @@
     across = lax.broadcasted_iota(jnp.int32, (order, order), 1)
     down = lax.broadcasted_iota(jnp.int32, (order, order), 0)
     diagonal = jnp.where(across == down, 1.5, 0.0)
-    cross = nt(nn(inverse, inner[...]), inverse)
+    inverse = split(inverse)
+    cross = three(split(three(inverse, split(inner[...]), NN)), inverse, NT)
     squares = jnp.sum(cross * cross, axis=0, keepdims=True)
     frob = jnp.sqrt(jnp.sum(squares, axis=1, keepdims=True))
-    now = cross / frob
+    now = cross * (1.0 / frob)
     projected = rows_ref[...] * jnp.sqrt(width / frob)
     for step in range(PSTEPS):
-        middle = diagonal - 0.5 * now
-        projected = nn(projected, middle)
+        middle = split(diagonal - 0.5 * now)
         if step < PSTEPS - 1:
-            now = nn(nn(middle, now), middle)
+            now = three(split(three(middle, split(now), NN)), middle, NN)
+        projected = three(split(projected), middle, NN)
     out_ref[...] = projected
 
 
@@ -296,6 +298,7 @@
     inverse, left_basis, projected = basis(
         core, gram, to_core(gram), sketch, block_rows, math.sqrt(total_rows)
     )
+    inner, inverse = lax.optimization_barrier((inner, inverse))
     right_basis = whiten(core, inner, to_core(inner), inverse, projected, width)
     return (left_basis, right_basis)
 

time: 139 us -> 128 us (0.921)
  waiting for transfers between devices: 24.2 us -> 16.5 us
  Pallas kernels: 31.6 us -> 29 us
    all_to_all x2, waiting for transfers between devices: 19.4 us -> 6.49 us  [exchange(): return lax.all_to_all(blocks, axes, 0, 0, tiled=True)]
    ppermute x3, waiting for transfers between devices: 0.01 us -> 4.23 us  [along_x(): return lax.ppermute(block, 'x', [(x, x ^ flip) for x in range(NX)])]
    pallas_call x1, Pallas kernels: 8.34 us -> 5.71 us  [whiten(): pl.pallas_call(functools.partial(whiten_kernel, width), out_shape=jax.Sha...]
    ppermute x4, starting transfers between devices: 10.7 us -> 9.24 us  [to_core(): return lax.ppermute(block, 'c', [(0, 1), (1, 0)])]
  transfers between devices with their start and end apart: 9 -> 9, of which waited for: 4 -> 7; matrix products, arithmetic and copies ran while one was open for 1% -> 1% of each run, Pallas kernels for 8% -> 9%
where the time goes in v2:
time: 128 us; the launch traced here: 127 us
  blocking collectives  50.7 us (40%)
  Pallas kernels  29 us (23%)
  starting transfers between devices  25.7 us (20%)
  waiting for transfers between devices  16.5 us (13%)
  local copies, waits for them, and re-layouts  3.04 us (2%)
    all_to_all x2, blocking collectives, exchange(): return lax.all_to_all(blocks, axes, 0, 0, tiled=True)  50.7 us
    all_to_all x2, starting transfers between devices, exchange(): return lax.all_to_all(blocks, axes, 0, 0, tiled=True)  12.5 us
    pallas_call x1, Pallas kernels, products(): pl.pallas_call(products_kernel, grid=(2 * NY,), out_shape=(jax.ShapeDtype...  12.3 us
    pallas_call x1, Pallas kernels, basis(): pl.pallas_call(functools.partial(basis_kernel, scale), out_shape=(jax.Sha...  10.9 us
    ppermute x4, starting transfers between devices, to_core(): return lax.ppermute(block, 'c', [(0, 1), (1, 0)])  9.24 us
    all_to_all x2, waiting for transfers between devices, exchange(): return lax.all_to_all(blocks, axes, 0, 0, tiled=True)  6.49 us
    ppermute x4, waiting for transfers between devices, to_core(): return lax.ppermute(block, 'c', [(0, 1), (1, 0)])  5.79 us
    pallas_call x1, Pallas kernels, whiten(): pl.pallas_call(functools.partial(whiten_kernel, width), out_shape=jax.Sha...  5.71 us
  transfers between devices with their start and end apart: 9, of which 7 were waited for; matrix products, arithmetic and copies ran while one was open for 1% of the time, Pallas kernels for 9%

profile of v2, /device:TPU:1, one launch (start us, length us, event | category | flops | bytes accessed | tf_op | source)
XLA Modules:
  0.0 127.3 jit_solution(2229444551536059343)
XLA Ops:
  0.6 12.3 %shard_map.41 = (f32[512,256]{1,0:T(8,128)S(1)}, f32[4,4,136,256]{3,2,1,0:T(8,128)S(1)}, f32[4,4,136,256]{3,2,1,0:T(8,128)S(1)}) custom-call(s32[1]{0:T(128)} %bitcast.core_ref, f32[512,4096]{1,0:T(8,128)} %emb_ref.1, f32[4096,256]{1,0:T(8,128)} %matrix_ref.1), custom_call_target="tpu_custom_call" | custom-call | flops 6442450944 | bytes 25165824 | tf_op jit(solution)/shard_map/pallas_call | solution.py:101
  13.0 0.0 copy-start
  13.0 3.3 %collective-permute-start = (f32[4,4,136,256]{3,2,1,0:T(8,128)S(1)}, f32[4,4,136,256]{3,2,1,0:T(8,128)S(1)}, u32[]{:S(2)}, u32[]{:S(2)}) collective-permute-start(f32[4,4,136,256]{3,2,1,0:T(8,128)S(1)} %get-tuple-element.11), channel_id=1, source_target_pairs={{0,32},{32,0},{1,33},{33,1},{2,34},{34,2},{3,35},{35,3},{4,36},{36... | collective-permute-start | bytes 6684680 | tf_op jit(solution)/shard_map/ppermute | solution.py:249
  16.3 4.0 %collective-permute-done = f32[4,4,136,256]{3,2,1,0:T(8,128)S(1)} collective-permute-done((f32[4,4,136,256]{3,2,1,0:T(8,128)S(1)}, f32[4,4,136,256]{3,2,1,0:T(8,128)S(1)}, u32[]{:S(2)}, u32[]{:S(2)}) %collective-permute-start) | collective-permute-done | bytes 2228256 | tf_op jit(solution)/shard_map/ppermute | solution.py:249
  20.3 0.3 add.16
  20.6 0.0 copy-done
  20.6 34.1 %all_to_all.31 = f32[16,136,256]{2,1,0:T(8,128)S(1)} all-to-all(f32[16,136,256]{2,1,0:T(8,128)S(1)} %bitcast.25), channel_id=1, replica_groups=mesh['x'=4,'c'=2,'y'=4,'z'=8] {'y','x'}, dimensions={0} | all-to-all | bytes 4456448 | tf_op jit(solution)/shard_map/all_to_all | solution.py:257
  54.7 0.1 reduce_sum.27
  54.9 16.6 %all_to_all.32 = f32[8,17,256]{2,1,0:T(8,128)S(1)} all-to-all(f32[8,17,256]{2,1,0:T(8,128)S(1)} %pad_maximum_fusion), channel_id=1, replica_groups=mesh['x'=4,'c'=2,'y'=4,'z'=8] {'z'}, dimensions={0} | all-to-all | bytes 278528 | tf_op jit(solution)/shard_map/all_to_all | solution.py:257
  71.5 3.0 %collective-permute-start.1 = (f32[16,256]{1,0:T(8,128)S(1)}, f32[16,256]{1,0:T(8,128)S(1)}, u32[]{:S(2)}, u32[]{:S(2)}) collective-permute-start(f32[16,256]{1,0:T(8,128)S(1)} %slice.34), channel_id=1, source_target_pairs={{0,32},{32,0},{1,33},{33,1},{2,34},{34,2},{3,35},{35,3},{4,36},{36... | collective-permute-start | bytes 49160 | tf_op jit(solution)/shard_map/ppermute | solution.py:249
  74.5 0.8 collective-permute-done.1
  75.4 0.3 fusion.2
  75.7 1.0 copy.10
  76.7 6.2 %all-to-all-start.2 = ((f32[128,1,512]{2,1,0:T(1,128)}), f32[128,1,512]{2,1,0:T(1,128)S(1)}, u32[]{:S(2)}, u32[]{:S(2)}) async-start(f32[128,1,512]{2,1,0:T(1,128)} %copy.10), calls=%async_computation.2 | async-start | bytes 524288 | tf_op jit(solution)/shard_map/all_to_all | solution.py:257
  82.9 0.8 collective-permute-start.3
  83.6 2.8 %collective-permute-start.4 = (f32[32,256]{1,0:T(8,128)S(1)}, f32[32,256]{1,0:T(8,128)S(1)}, u32[]{:S(2)}, u32[]{:S(2)}) collective-permute-start(f32[32,256]{1,0:T(8,128)S(1)} %get-tuple-element.27), channel_id=1, source_target_pairs={{0,128},{64,192},{128,0},{192,64},{1,129},{65,193},{129,1},{193,65... | collective-permute-start | bytes 98312 | tf_op jit(solution)/shard_map/ppermute | solution.py:253
  86.5 0.4 collective-permute-start.5
  86.8 0.0 collective-permute-done.3
  86.8 1.9 %collective-permute-done.4 = f32[32,256]{1,0:T(8,128)S(1)} collective-permute-done((f32[32,256]{1,0:T(8,128)S(1)}, f32[32,256]{1,0:T(8,128)S(1)}, u32[]{:S(2)}, u32[]{:S(2)}) %collective-permute-start.4) | collective-permute-done | bytes 32800 | tf_op jit(solution)/shard_map/ppermute | solution.py:253
  88.8 2.3 %collective-permute-done.5 = f32[32,256]{1,0:T(8,128)S(1)} collective-permute-done((f32[32,256]{1,0:T(8,128)S(1)}, f32[32,256]{1,0:T(8,128)S(1)}, u32[]{:S(2)}, u32[]{:S(2)}) %collective-permute-start.5) | collective-permute-done | bytes 32800 | tf_op jit(solution)/shard_map/ppermute | solution.py:253
  91.1 6.2 %all-to-all-done.2 = f32[128,1,512]{2,1,0:T(1,128)S(1)} async-done(((f32[128,1,512]{2,1,0:T(1,128)}), f32[128,1,512]{2,1,0:T(1,128)S(1)}, u32[]{:S(2)}, u32[]{:S(2)}) %all-to-all-start.2) | async-done | bytes 262176 | tf_op jit(solution)/shard_map/all_to_all | solution.py:257
  97.3 0.0 copy-start.1
  97.4 1.7 %collective-permute-start.2 = (f32[128,256]{1,0:T(8,128)S(1)}, f32[128,256]{1,0:T(8,128)S(1)}, u32[]{:S(2)}, u32[]{:S(2)}) collective-permute-start(f32[128,256]{1,0:T(8,128)S(1)} %get-tuple-element.19.mine_ref), channel_id=1, source_target_pairs={{0,32},{32,0},{1,33},{33,1},{2,34},{34,2},{3,35},{35,3},{4,36},{36... | collective-permute-start | bytes 393224 | tf_op jit(solution)/shard_map/ppermute | solution.py:249
  99.1 0.7 pad_maximum_fusion.2.rows_ref
  99.7 0.7 broadcast_in_dim.19
  100.4 6.3 %all-to-all-start.3 = ((f32[128,1,256]{2,1,0:T(1,128)}), f32[128,1,256]{2,1,0:T(1,128)S(1)}, u32[]{:S(2)}, u32[]{:S(2)}) async-start(f32[128,1,256]{2,1,0:T(1,128)} %broadcast_in_dim.19), calls=%async_computation.3 | async-start | bytes 262144 | tf_op jit(solution)/shard_map/all_to_all | solution.py:257
  106.8 0.0 collective-permute-done.2.other_ref
  106.8 0.0 copy-start.3
  106.8 0.0 copy-done.1
  106.8 0.6 copy-done.3
  107.4 10.9 %shard_map.42 = (f32[256,256]{1,0:T(8,128)}, f32[512,256]{1,0:T(8,128)}, f32[128,256]{1,0:T(8,128)}) custom-call(s32[1]{0:T(128)} %bitcast.core_ref, f32[128,256]{1,0:T(8,128)} %copy-done.1, f32[128,256]{1,0:T(8,128)} %copy-done.3, f32[512,256]{1,0:T(8,128)} %copy-done, f32[128,256]{1,0:T(8,128)} %pad_maximum_fusion.2.rows_ref), custom_call_target="tpu_custom_call" | custom-call | flops 10000000000 | bytes 2097152 | tf_op jit(solution)/shard_map/pallas_call | solution.py:201
  118.4 0.3 all-to-all-done.3
  118.6 0.0 copy-start.2
  118.7 1.3 collective-permute-start.6
  119.9 1.0 collective-permute-done.6.other_ref
  120.9 0.0 copy-start.4
  120.9 0.0 copy-done.2
  120.9 0.6 copy-done.4
  121.5 5.7 %shard_map.43 = f32[128,256]{1,0:T(8,128)} custom-call(s32[1]{0:T(128)} %bitcast.core_ref, f32[128,256]{1,0:T(8,128)} %bitcast.29, f32[128,256]{1,0:T(8,128)} %copy-done.4, f32[256,256]{1,0:T(8,128)} %get-tuple-element.16.inverse_ref, f32[128,256]{1,0:T(8,128)} %get-tuple-element.17.rows_ref), custom_call_target="tpu_custom_call" | custom-call | flops 10000000000 | bytes 1048576 | tf_op jit(solution)/shard_map/pallas_call | solution.py:238
  (16 shorter events, 0.2 us)
Async XLA Ops:
  13.0 7.6 %copy-start = (f32[512,256]{1,0:T(8,128)}, f32[512,256]{1,0:T(8,128)S(1)}, u32[]{:S(2)}) copy-start(f32[512,256]{1,0:T(8,128)S(1)} %get-tuple-element.12.sketch_ref) | copy-start | bytes 1572868
  13.0 7.3 %collective-permute-start = (f32[4,4,136,256]{3,2,1,0:T(8,128)S(1)}, f32[4,4,136,256]{3,2,1,0:T(8,128)S(1)}, u32[]{:S(2)}, u32[]{:S(2)}) collective-permute-start(f32[4,4,136,256]{3,2,1,0:T(8,128)S(1)} %get-tuple-element.11), channel_id=1, source_target_pairs={{0,32},{32,0},{1,33},{33,1},{2,34},{34,2},{3,35},{35,3},{4,36},{36... | collective-permute-start | bytes 6684680 | tf_op jit(solution)/shard_map/ppermute | solution.py:249
  71.5 3.8 %collective-permute-start.1 = (f32[16,256]{1,0:T(8,128)S(1)}, f32[16,256]{1,0:T(8,128)S(1)}, u32[]{:S(2)}, u32[]{:S(2)}) collective-permute-start(f32[16,256]{1,0:T(8,128)S(1)} %slice.34), channel_id=1, source_target_pairs={{0,32},{32,0},{1,33},{33,1},{2,34},{34,2},{3,35},{35,3},{4,36},{36... | collective-permute-start | bytes 49160 | tf_op jit(solution)/shard_map/ppermute | solution.py:249
  76.7 20.6 %all-to-all-start.2 = ((f32[128,1,512]{2,1,0:T(1,128)}), f32[128,1,512]{2,1,0:T(1,128)S(1)}, u32[]{:S(2)}, u32[]{:S(2)}) async-start(f32[128,1,512]{2,1,0:T(1,128)} %copy.10), calls=%async_computation.2 | async-start | bytes 524288 | tf_op jit(solution)/shard_map/all_to_all | solution.py:257
  82.9 3.9 %collective-permute-start.3 = (f32[32,256]{1,0:T(8,128)S(1)}, f32[32,256]{1,0:T(8,128)S(1)}, u32[]{:S(2)}, u32[]{:S(2)}) collective-permute-start(f32[32,256]{1,0:T(8,128)S(1)} %get-tuple-element.27), channel_id=1, source_target_pairs={{0,64},{64,0},{128,192},{192,128},{1,65},{65,1},{129,193},{193,129... | collective-permute-start | bytes 98312 | tf_op jit(solution)/shard_map/ppermute | solution.py:253
  83.6 5.1 %collective-permute-start.4 = (f32[32,256]{1,0:T(8,128)S(1)}, f32[32,256]{1,0:T(8,128)S(1)}, u32[]{:S(2)}, u32[]{:S(2)}) collective-permute-start(f32[32,256]{1,0:T(8,128)S(1)} %get-tuple-element.27), channel_id=1, source_target_pairs={{0,128},{64,192},{128,0},{192,64},{1,129},{65,193},{129,1},{193,65... | collective-permute-start | bytes 98312 | tf_op jit(solution)/shard_map/ppermute | solution.py:253
  86.5 4.6 %collective-permute-start.5 = (f32[32,256]{1,0:T(8,128)S(1)}, f32[32,256]{1,0:T(8,128)S(1)}, u32[]{:S(2)}, u32[]{:S(2)}) collective-permute-start(f32[32,256]{1,0:T(8,128)S(1)} %get-tuple-element.27), channel_id=1, source_target_pairs={{0,192},{64,128},{128,64},{192,0},{1,193},{65,129},{129,65},{193,1... | collective-permute-start | bytes 98312 | tf_op jit(solution)/shard_map/ppermute | solution.py:253
  97.3 9.4 %copy-start.1 = (f32[128,256]{1,0:T(8,128)}, f32[128,256]{1,0:T(8,128)S(1)}, u32[]{:S(2)}) copy-start(f32[128,256]{1,0:T(8,128)S(1)} %get-tuple-element.19.mine_ref) | copy-start | bytes 393220
  97.4 9.4 %collective-permute-start.2 = (f32[128,256]{1,0:T(8,128)S(1)}, f32[128,256]{1,0:T(8,128)S(1)}, u32[]{:S(2)}, u32[]{:S(2)}) collective-permute-start(f32[128,256]{1,0:T(8,128)S(1)} %get-tuple-element.19.mine_ref), channel_id=1, source_target_pairs={{0,32},{32,0},{1,33},{33,1},{2,34},{34,2},{3,35},{35,3},{4,36},{36... | collective-permute-start | bytes 393224 | tf_op jit(solution)/shard_map/ppermute | solution.py:249
  100.4 18.2 %all-to-all-start.3 = ((f32[128,1,256]{2,1,0:T(1,128)}), f32[128,1,256]{2,1,0:T(1,128)S(1)}, u32[]{:S(2)}, u32[]{:S(2)}) async-start(f32[128,1,256]{2,1,0:T(1,128)} %broadcast_in_dim.19), calls=%async_computation.3 | async-start | bytes 262144 | tf_op jit(solution)/shard_map/all_to_all | solution.py:257
  106.8 0.7 copy-start.3
  118.6 2.3 %copy-start.2 = (f32[128,1,256]{2,0,1:T(8,128)}, f32[128,1,256]{2,0,1:T(8,128)S(1)}, u32[]{:S(2)}) copy-start(f32[128,1,256]{2,0,1:T(8,128)S(1)} %copy.19) | copy-start | bytes 393220
  118.7 2.2 %collective-permute-start.6 = (f32[128,256]{1,0:T(8,128)S(1)}, f32[128,256]{1,0:T(8,128)S(1)}, u32[]{:S(2)}, u32[]{:S(2)}) collective-permute-start(f32[128,256]{1,0:T(8,128)S(1)} %bitcast.28), channel_id=1, source_target_pairs={{0,32},{32,0},{1,33},{33,1},{2,34},{34,2},{3,35},{35,3},{4,36},{36... | collective-permute-start | bytes 393224 | tf_op jit(solution)/shard_map/ppermute | solution.py:249
  120.9 0.6 copy-start.4

commit v3 on v2

--- a/solution.py
+++ b/solution.py
@@ -47,7 +47,8 @@
 
 
 def products_kernel(
-    core_ref, emb_ref, matrix_ref, sketch_ref, keep_ref, send_ref, high, low, gram, s_high, s_low
+    slots_ref, emb_ref, matrix_ref, sketch_ref, keep_a, keep_b, send_a, send_b, high, low, gram,
+    s_high, s_low,
 ):
     step = pl.program_id(0)
     rank = matrix_ref.shape[1]
@@ -56,7 +57,7 @@
     def _():
         parts = split(emb_ref[...])
         high[step], low[step] = parts
-        term = three(parts, split(matrix_ref[...]), ((1,), (0,)))
+        term = three(parts, split(matrix_ref[...]), NN)
 
         @pl.when(step == 0)
         def _():
@@ -75,51 +76,77 @@
     @pl.when(step >= NY)
     def _():
         y = step - NY
-        product = three((high[y], low[y]), (s_high[...], s_low[...]), ((0,), (0,)))
+        product = three((high[y], low[y]), (s_high[...], s_low[...]), TN)
         product = product.reshape(NZ, NX, NC, -1, rank)
-        first = core_ref[0] == 0
+        first = slots_ref[0] == 0
         for x in range(NX):
             halves = [product[:, x, c].reshape(-1, rank) for c in range(NC)]
             extra = [
                 gram[pl.ds(pl.multiple_of(NZ * ((c * NX + x) * NY + y), NZ), NZ), :]
                 for c in range(NC)
             ]
-            size = halves[0].shape[0]
-            keep_ref[0, x, :size, :] = jnp.where(first, halves[0], halves[1])
-            send_ref[0, x, :size, :] = jnp.where(first, halves[1], halves[0])
-            keep_ref[0, x, size:, :] = jnp.where(first, extra[0], extra[1])
-            send_ref[0, x, size:, :] = jnp.where(first, extra[1], extra[0])
-
-
-def products(core, embeddings, matrix):
+            size = halves[0].shape[0] // 2
+            kept = jnp.where(first, halves[0], halves[1])
+            sent = jnp.where(first, halves[1], halves[0])
+            keep_x, send_x = slots_ref[1 + 2 * NY + x], slots_ref[1 + 2 * NY + NX + x]
+            keep_a[0, keep_x, :size, :] = kept[:size]
+            send_a[0, send_x, :size, :] = sent[:size]
+            keep_a[0, keep_x, size:, :] = jnp.where(first, extra[0], extra[1])
+            send_a[0, send_x, size:, :] = jnp.where(first, extra[1], extra[0])
+            keep_b[keep_x, 0] = kept[size:]
+            send_b[send_x, 0] = sent[size:]
+
+
+def products(slots, embeddings, matrix):
     rows, width = embeddings.shape
     rank = matrix.shape[1]
     wide = width // NY
-    piece = wide // (NX * NC) + NZ
-    blocks = jax.ShapeDtypeStruct((NY, NX, piece, rank), jnp.float32)
-    spec = pl.BlockSpec((1, NX, piece, rank), lambda i: (jnp.maximum(i - NY, 0), 0, 0, 0))
+    piece = wide // (NX * NC * 2)
+    part_a = jax.ShapeDtypeStruct((NY, NX, piece + NZ, rank), jnp.float32)
+    part_b = jax.ShapeDtypeStruct((NX, NY, piece, rank), jnp.float32)
+
+    def spec_a(base):
+        return pl.BlockSpec(
+            (1,) + part_a.shape[1:], lambda i, s: (s[base + jnp.maximum(i - NY, 0)], 0, 0, 0)
+        )
+
+    def spec_b(base):
+        return pl.BlockSpec(
+            (NX, 1) + part_b.shape[2:], lambda i, s: (0, s[base + jnp.maximum(i - NY, 0)], 0, 0)
+        )
+
     return pl.pallas_call(
         products_kernel,
-        grid=(2 * NY,),
-        out_shape=(jax.ShapeDtypeStruct((rows, rank), jnp.float32), blocks, blocks),
-        in_specs=[
-            pl.BlockSpec(memory_space=pltpu.SMEM),
-            pl.BlockSpec((rows, wide), lambda i: (0, jnp.minimum(i, NY - 1))),
-            pl.BlockSpec((wide, rank), lambda i: (jnp.minimum(i, NY - 1), 0)),
-        ],
-        out_specs=(pl.BlockSpec((rows, rank), lambda i: (0, 0)), spec, spec),
-        scratch_shapes=[
-            pltpu.VMEM((NY, rows, wide), jnp.bfloat16),
-            pltpu.VMEM((NY, rows, wide), jnp.bfloat16),
-            pltpu.VMEM((rank, rank), jnp.float32),
-            pltpu.VMEM((rows, rank), jnp.bfloat16),
-            pltpu.VMEM((rows, rank), jnp.bfloat16),
-        ],
+        grid_spec=pltpu.PrefetchScalarGridSpec(
+            num_scalar_prefetch=1,
+            grid=(2 * NY,),
+            in_specs=[
+                pl.BlockSpec((rows, wide), lambda i, s: (0, jnp.minimum(i, NY - 1))),
+                pl.BlockSpec((wide, rank), lambda i, s: (jnp.minimum(i, NY - 1), 0)),
+            ],
+            out_specs=(
+                pl.BlockSpec((rows, rank), lambda i, s: (0, 0)),
+                spec_a(1),
+                spec_b(1),
+                spec_a(1 + NY),
+                spec_b(1 + NY),
+            ),
+            scratch_shapes=[
+                pltpu.VMEM((NY, rows, wide), jnp.bfloat16),
+                pltpu.VMEM((NY, rows, wide), jnp.bfloat16),
+                pltpu.VMEM((rank, rank), jnp.float32),
+                pltpu.VMEM((rows, rank), jnp.bfloat16),
+                pltpu.VMEM((rows, rank), jnp.bfloat16),
+            ],
+        ),
+        out_shape=(
+            jax.ShapeDtypeStruct((rows, rank), jnp.float32), part_a, part_b, part_a, part_b
+        ),
         compiler_params=pltpu.CompilerParams(vmem_limit_bytes=VMEM_LIMIT),
         cost_estimate=pl.CostEstimate(
             flops=12 * rows * width * rank, bytes_accessed=24 * 2**20, transcendentals=0
         ),
-    )(core, embeddings, matrix)
+    )(slots, embeddings, matrix)
 
 
 def join(core_ref, mine_ref, other_ref, out_ref):
@@ -257,21 +284,59 @@
     return lax.all_to_all(blocks, axes, 0, 0, tiled=True)
 
 
+def ring_pairs(block, axis, turn):
+    pairs = []
+    for c in range(NC):
+        flip = 1 if turn == c else 3
+        pairs += [(c * 4 + i, c * 4 + (i ^ flip)) for i in range(4)]
+    if axis == "y":
+        return lax.ppermute(block, ("c", "y"), pairs)
+    pairs = [((i % 4) * NC + i // 4, (j % 4) * NC + j // 4) for i, j in pairs]
+    return lax.ppermute(block, ("x", "c"), pairs)
+
+
+def ring_slots(core, here):
+    apart = jnp.arange(4, dtype=jnp.int32) ^ here
+    return jnp.where((core == 1) & (apart % 2 == 1), 4 - apart, apart)
+
+
+def ring_sums(terms_a, terms_b, axis_a, axis_b):
+    def first(terms, slot):
+        return functools.reduce(lambda p, q: p + q, [t[slot] for t in terms])
+
+    out = []
+    sent = [sum(t[1:3] for t in terms) for terms in (terms_a, terms_b)]
+    got = [ring_pairs(v, axis, 0) for v, axis in zip(sent, (axis_a, axis_b))]
+    got = lax.optimization_barrier(tuple(got))
+    sent = [first(terms, 3) + g[1] for terms, g in zip((terms_a, terms_b), got)]
+    more = [ring_pairs(v, axis, 1) for v, axis in zip(sent, (axis_a, axis_b))]
+    more = lax.optimization_barrier(tuple(more))
+    for terms, g, m in zip((terms_a, terms_b), got, more):
+        out.append([first(terms, 0), g[0], m])
+    return out
+
+
 def per_device(embeddings, sketch_matrix):
     rank = sketch_matrix.shape[1]
     width = embeddings.shape[1]
     share = width // (NX * NC * NY * NZ)
     total_rows = embeddings.shape[0] * NX * NC * NY * NZ
     chips = NX * NY * NZ
-    x, c = lax.axis_index("x"), lax.axis_index("c")
+    x, c, y = (lax.axis_index(name).astype(jnp.int32) for name in ("x", "c", "y"))
     first_core = c == 0
-    core = c.reshape(1).astype(jnp.int32)
-
-    sketch, keep, send = products(core, embeddings, sketch_matrix)
-    chip = (keep + to_core(send)).reshape(NY * NX, -1, rank)
-    line = jnp.sum(exchange(chip, ("y", "x")), axis=0)
-    size = NZ * share
-    line = jnp.concatenate([line[:size].reshape(NZ, share, rank), line[size:][:, None]], axis=1)
+    core = c.reshape(1)
+
+    slots = jnp.concatenate(
+        [core] + [ring_slots(k, at) for at in (y, x) for k in (c, 1 - c)]
+    )
+    sketch, keep_a, keep_b, send_a, send_b = products(slots, embeddings, sketch_matrix)
+    got_a, got_b = to_core(send_a), to_core(send_b)
+    line_a, line_b = ring_sums([keep_a, got_a], [keep_b, got_b], "y", "x")
+    own_a, own_b = ring_sums(line_a, line_b, "x", "y")
+    own_a, own_b = sum(own_a), sum(own_b)
+    size = own_b.shape[0]
+    line = jnp.concatenate([own_a[:size], own_b]).reshape(NZ, share, rank)
+    line = jnp.concatenate([line, own_a[size:][:, None]], axis=1)
     own = jnp.sum(exchange(line, "z"), axis=0)
     own_product, own_gram = own[:share], own[share:]
 

time: 128 us -> 126 us (0.984)
  blocking collectives: 50.7 us -> 16.6 us
  waiting for transfers between devices: 16.5 us -> 34.9 us
  starting transfers between devices: 25.7 us -> 38.6 us
    all_to_all x2 -> x1, blocking collectives: 50.7 us -> 16.6 us  [exchange(): return lax.all_to_all(blocks, axes, 0, 0, tiled=True)]
    ppermute x0 -> x8, waiting for transfers between devices: none -> 18.9 us  [the longest x4 12.6 us: ring_pairs(): return lax.ppermute(block, ('x', 'c'), pairs)]
    ppermute x0 -> x8, starting transfers between devices: none -> 8.05 us  [the longest x4 4.69 us: ring_pairs(): return lax.ppermute(block, ('x', 'c'), pairs)]
    ppermute x4 -> x5, starting transfers between devices: 9.24 us -> 14.7 us  [to_core(): return lax.ppermute(block, 'c', [(0, 1), (1, 0)])]
    ppermute x4 -> x5, waiting for transfers between devices: 5.79 us -> 4.52 us  [to_core(): return lax.ppermute(block, 'c', [(0, 1), (1, 0)])]
  transfers between devices with their start and end apart: 9 -> 18, of which waited for: 7 -> 13; matrix products, arithmetic and copies ran while one was open for 1% -> 1% of each run, Pallas kernels for 9% -> 9%
where the time goes in v3:
time: 126 us
  starting transfers between devices  38.6 us (31%)
  waiting for transfers between devices  34.9 us (28%)
  Pallas kernels  29.8 us (24%)
  blocking collectives  16.6 us (13%)
  local copies, waits for them, and re-layouts  3.13 us (2%)
  other arithmetic  1.31 us (1%)
    all_to_all x1, blocking collectives, exchange(): return lax.all_to_all(blocks, axes, 0, 0, tiled=True)  16.6 us
    ppermute x5, starting transfers between devices, to_core(): return lax.ppermute(block, 'c', [(0, 1), (1, 0)])  14.7 us
    pallas_call x1, Pallas kernels, products(): pl.pallas_call(products_kernel, grid_spec=pltpu.PrefetchScalarGridSpec(nu...  13.2 us
    ppermute x4, waiting for transfers between devices, ring_pairs(): return lax.ppermute(block, ('x', 'c'), pairs)  12.6 us
    all_to_all x2, starting transfers between devices, exchange(): return lax.all_to_all(blocks, axes, 0, 0, tiled=True)  12.5 us
    pallas_call x1, Pallas kernels, basis(): pl.pallas_call(functools.partial(basis_kernel, scale), out_shape=(jax.Sha...  10.9 us
    all_to_all x2, waiting for transfers between devices, exchange(): return lax.all_to_all(blocks, axes, 0, 0, tiled=True)  7.61 us
    ppermute x4, waiting for transfers between devices, ring_pairs(): return lax.ppermute(block, ('c', 'y'), pairs)  6.3 us
  transfers between devices with their start and end apart: 18, of which 13 were waited for; matrix products, arithmetic and copies ran while one was open for 1% of the time, Pallas kernels for 9%

profile of v3, /device:TPU:1, one launch (start us, length us, event | category | flops | bytes accessed | tf_op | source)
XLA Modules:
  0.0 125.6 jit_solution(1822056190175556508)
XLA Ops:
  0.7 0.1 concatenate.18.slots_ref
  0.8 13.2 %shard_map.41 = (f32[512,256]{1,0:T(8,128)S(1)}, f32[4,4,72,256]{3,2,1,0:T(8,128)S(1)}, f32[4,4,64,256]{3,2,1,0:T(8,128)S(1)}, f32[4,4,72,256]{3,2,1,0:T(8,128)S(1)}, f32[4,4,64,256]{3,2,1,0:T(8,128)S(1)}) custom-call(s32[17]{0:T(128)S(1)} %concatenate.18.slots_ref, f32[512,4096]{1,0:T(8,128)} %emb_ref.1, f32[4096,256]{1,0:T(8,128)} %matrix_ref.1), custom_call_target="tpu_custom_call" | custom-call | flops 6442450944 | bytes 25165824 | tf_op jit(solution)/shard_map/pallas_call | solution.py:118
  14.0 3.3 %collective-permute-start = (f32[4,4,72,256]{3,2,1,0:T(8,128)S(1)}, f32[4,4,72,256]{3,2,1,0:T(8,128)S(1)}, u32[]{:S(2)}, u32[]{:S(2)}) collective-permute-start(f32[4,4,72,256]{3,2,1,0:T(8,128)S(1)} %get-tuple-element.21), channel_id=1, source_target_pairs={{0,32},{32,0},{1,33},{33,1},{2,34},{34,2},{3,35},{35,3},{4,36},{36... | collective-permute-start | bytes 3538952 | tf_op jit(solution)/shard_map/ppermute | solution.py:276
  17.3 0.1 collective-permute-start.2
  17.4 2.4 %collective-permute-done = f32[4,4,72,256]{3,2,1,0:T(8,128)S(1)} collective-permute-done((f32[4,4,72,256]{3,2,1,0:T(8,128)S(1)}, f32[4,4,72,256]{3,2,1,0:T(8,128)S(1)}, u32[]{:S(2)}, u32[]{:S(2)}) %collective-permute-start) | collective-permute-done | bytes 1179680 | tf_op jit(solution)/shard_map/ppermute | solution.py:276
  19.8 0.1 slice_add_fusion
  19.8 1.1 collective-permute-start.1
  20.9 0.3 collective-permute-done.2
  21.3 0.1 slice_add_fusion.1
  21.3 2.3 %collective-permute-start.3 = (f32[2,4,64,256]{3,2,1,0:T(8,128)S(1)}, f32[2,4,64,256]{3,2,1,0:T(8,128)S(1)}, u32[]{:S(2)}, u32[]{:S(2)}) collective-permute-start(f32[2,4,64,256]{3,2,1,0:T(8,128)S(1)} %slice_add_fusion.1), channel_id=1, source_target_pairs={{0,64},{64,0},{128,192},{192,128},{32,224},{96,160},{160,96},{224,... | collective-permute-start | bytes 1572872 | tf_op jit(solution)/shard_map/ppermute | solution.py:295
  23.6 7.1 %collective-permute-done.3 = f32[2,4,64,256]{3,2,1,0:T(8,128)S(1)} collective-permute-done((f32[2,4,64,256]{3,2,1,0:T(8,128)S(1)}, f32[2,4,64,256]{3,2,1,0:T(8,128)S(1)}, u32[]{:S(2)}, u32[]{:S(2)}) %collective-permute-start.3) | collective-permute-done | bytes 524320 | tf_op jit(solution)/shard_map/ppermute | solution.py:295
  30.7 0.1 fusion.1
  30.8 0.1 collective-permute-start.4
  30.9 0.1 slice_add_fusion.4
  31.0 0.1 collective-permute-start.5
  31.1 5.5 %collective-permute-done.5 = f32[4,64,256]{2,1,0:T(8,128)S(1)} collective-permute-done((f32[4,64,256]{2,1,0:T(8,128)S(1)}, f32[4,64,256]{2,1,0:T(8,128)S(1)}, u32[]{:S(2)}, u32[]{:S(2)}) %collective-permute-start.5) | collective-permute-done | bytes 262176 | tf_op jit(solution)/shard_map/ppermute | solution.py:295
  36.6 0.2 collective-permute-done.4
  36.8 2.3 %collective-permute-start.6 = (f32[2,72,256]{2,1,0:T(8,128)S(1)}, f32[2,72,256]{2,1,0:T(8,128)S(1)}, u32[]{:S(2)}, u32[]{:S(2)}) collective-permute-start(f32[2,72,256]{2,1,0:T(8,128)S(1)} %fusion.5), channel_id=1, source_target_pairs={{0,64},{64,0},{128,192},{192,128},{32,224},{96,160},{160,96},{224,... | collective-permute-start | bytes 442376 | tf_op jit(solution)/shard_map/ppermute | solution.py:295
  39.0 1.7 %collective-permute-start.7 = (f32[2,64,256]{2,1,0:T(8,128)S(1)}, f32[2,64,256]{2,1,0:T(8,128)S(1)}, u32[]{:S(2)}, u32[]{:S(2)}) collective-permute-start(f32[2,64,256]{2,1,0:T(8,128)S(1)} %fusion.7), channel_id=1, source_target_pairs={{0,8},{8,0},{16,24},{24,16},{32,56},{40,48},{48,40},{56,32},{1,9},... | collective-permute-start | bytes 393224 | tf_op jit(solution)/shard_map/ppermute | solution.py:293
  40.8 3.4 %collective-permute-done.7 = f32[2,64,256]{2,1,0:T(8,128)S(1)} collective-permute-done((f32[2,64,256]{2,1,0:T(8,128)S(1)}, f32[2,64,256]{2,1,0:T(8,128)S(1)}, u32[]{:S(2)}, u32[]{:S(2)}) %collective-permute-start.7) | collective-permute-done | bytes 131104 | tf_op jit(solution)/shard_map/ppermute | solution.py:293
  44.2 0.0 collective-permute-done.6
  44.2 0.1 collective-permute-start.8
  44.3 0.5 collective-permute-start.9
  44.8 2.7 %collective-permute-done.9 = f32[64,256]{1,0:T(8,128)S(1)} collective-permute-done((f32[64,256]{1,0:T(8,128)S(1)}, f32[64,256]{1,0:T(8,128)S(1)}, u32[]{:S(2)}, u32[]{:S(2)}) %collective-permute-start.9) | collective-permute-done | bytes 65568 | tf_op jit(solution)/shard_map/ppermute | solution.py:293
  47.7 16.6 %all_to_all.26 = f32[8,17,256]{2,1,0:T(8,128)S(1)} all-to-all(f32[8,17,256]{2,1,0:T(8,128)S(1)} %pad_maximum_fusion), channel_id=1, replica_groups=mesh['x'=4,'c'=2,'y'=4,'z'=8] {'z'}, dimensions={0} | all-to-all | bytes 278528 | tf_op jit(solution)/shard_map/all_to_all | solution.py:284
  64.3 8.3 %collective-permute-start.10 = (f32[16,256]{1,0:T(8,128)S(1)}, f32[16,256]{1,0:T(8,128)S(1)}, u32[]{:S(2)}, u32[]{:S(2)}) collective-permute-start(f32[16,256]{1,0:T(8,128)S(1)} %slice.210), channel_id=1, source_target_pairs={{0,32},{32,0},{1,33},{33,1},{2,34},{34,2},{3,35},{35,3},{4,36},{36... | collective-permute-start | bytes 49160 | tf_op jit(solution)/shard_map/ppermute | solution.py:276
  72.6 0.8 collective-permute-done.10
  73.5 0.3 fusion.24
  73.8 1.0 copy.6
  74.8 6.4 %all-to-all-start.1 = ((f32[128,1,512]{2,1,0:T(1,128)}), f32[128,1,512]{2,1,0:T(1,128)S(1)}, u32[]{:S(2)}, u32[]{:S(2)}) async-start(f32[128,1,512]{2,1,0:T(1,128)} %copy.6), calls=%async_computation.1 | async-start | bytes 524288 | tf_op jit(solution)/shard_map/all_to_all | solution.py:284
  81.2 2.4 %collective-permute-start.14 = (f32[32,256]{1,0:T(8,128)S(1)}, f32[32,256]{1,0:T(8,128)S(1)}, u32[]{:S(2)}, u32[]{:S(2)}) collective-permute-start(f32[32,256]{1,0:T(8,128)S(1)} %get-tuple-element.51), channel_id=1, source_target_pairs={{0,192},{64,128},{128,64},{192,0},{1,193},{65,129},{129,65},{193,1... | collective-permute-start | bytes 98312 | tf_op jit(solution)/shard_map/ppermute | solution.py:280
  83.6 0.2 collective-permute-start.13
  83.8 0.8 collective-permute-start.12
  84.5 1.2 collective-permute-done.14
  85.7 2.7 %collective-permute-done.13 = f32[32,256]{1,0:T(8,128)S(1)} collective-permute-done((f32[32,256]{1,0:T(8,128)S(1)}, f32[32,256]{1,0:T(8,128)S(1)}, u32[]{:S(2)}, u32[]{:S(2)}) %collective-permute-start.13) | collective-permute-done | bytes 32800 | tf_op jit(solution)/shard_map/ppermute | solution.py:280
  88.4 7.2 %all-to-all-done.1 = f32[128,1,512]{2,1,0:T(1,128)S(1)} async-done(((f32[128,1,512]{2,1,0:T(1,128)}), f32[128,1,512]{2,1,0:T(1,128)S(1)}, u32[]{:S(2)}, u32[]{:S(2)}) %all-to-all-start.1) | async-done | bytes 262176 | tf_op jit(solution)/shard_map/all_to_all | solution.py:284
  95.6 0.0 copy-start.1
  95.7 1.7 %collective-permute-start.11 = (f32[128,256]{1,0:T(8,128)S(1)}, f32[128,256]{1,0:T(8,128)S(1)}, u32[]{:S(2)}, u32[]{:S(2)}) collective-permute-start(f32[128,256]{1,0:T(8,128)S(1)} %get-tuple-element.43.mine_ref), channel_id=1, source_target_pairs={{0,32},{32,0},{1,33},{33,1},{2,34},{34,2},{3,35},{35,3},{4,36},{36... | collective-permute-start | bytes 393224 | tf_op jit(solution)/shard_map/ppermute | solution.py:276
  97.4 0.6 pad_maximum_fusion.3.rows_ref
  98.0 0.7 broadcast_in_dim.19
  98.7 6.2 %all-to-all-start.2 = ((f32[128,1,256]{2,1,0:T(1,128)}), f32[128,1,256]{2,1,0:T(1,128)S(1)}, u32[]{:S(2)}, u32[]{:S(2)}) async-start(f32[128,1,256]{2,1,0:T(1,128)} %broadcast_in_dim.19), calls=%async_computation.2 | async-start | bytes 262144 | tf_op jit(solution)/shard_map/all_to_all | solution.py:284
  104.9 0.6 copy-done.3
  105.6 10.9 %shard_map.42 = (f32[256,256]{1,0:T(8,128)}, f32[512,256]{1,0:T(8,128)}, f32[128,256]{1,0:T(8,128)}) custom-call(s32[1]{0:T(128)} %bitcast.core_ref, f32[128,256]{1,0:T(8,128)} %copy-done.1, f32[128,256]{1,0:T(8,128)} %copy-done.3, f32[512,256]{1,0:T(8,128)} %copy-done, f32[128,256]{1,0:T(8,128)} %pad_maximum_fusion.3.rows_ref), custom_call_target="tpu_custom_call" | custom-call | flops 10000000000 | bytes 2097152 | tf_op jit(solution)/shard_map/pallas_call | solution.py:228
  116.5 0.5 all-to-all-done.2
  117.0 1.3 %collective-permute-start.15 = (f32[128,256]{1,0:T(8,128)S(1)}, f32[128,256]{1,0:T(8,128)S(1)}, u32[]{:S(2)}, u32[]{:S(2)}) collective-permute-start(f32[128,256]{1,0:T(8,128)S(1)} %bitcast.84), channel_id=1, source_target_pairs={{0,32},{32,0},{1,33},{33,1},{2,34},{34,2},{3,35},{35,3},{4,36},{36... | collective-permute-start | bytes 393224 | tf_op jit(solution)/shard_map/ppermute | solution.py:276
  118.2 1.0 collective-permute-done.15.other_ref
  119.2 0.6 copy-done.4
  119.9 5.7 %shard_map.43 = f32[128,256]{1,0:T(8,128)} custom-call(s32[1]{0:T(128)} %bitcast.core_ref, f32[128,256]{1,0:T(8,128)} %bitcast.85, f32[128,256]{1,0:T(8,128)} %copy-done.4, f32[256,256]{1,0:T(8,128)} %get-tuple-element.36.inverse_ref, f32[128,256]{1,0:T(8,128)} %get-tuple-element.37.rows_ref), custom_call_target="tpu_custom_call" | custom-call | flops 10000000000 | bytes 1048576 | tf_op jit(solution)/shard_map/pallas_call | solution.py:265
  (36 shorter events, 0.4 us)
Async XLA Ops:
  13.9 7.4 %copy-start = (f32[512,256]{1,0:T(8,128)}, f32[512,256]{1,0:T(8,128)S(1)}, u32[]{:S(2)}) copy-start(f32[512,256]{1,0:T(8,128)S(1)} %get-tuple-element.32.sketch_ref) | copy-start | bytes 1572868
  14.0 5.8 %collective-permute-start = (f32[4,4,72,256]{3,2,1,0:T(8,128)S(1)}, f32[4,4,72,256]{3,2,1,0:T(8,128)S(1)}, u32[]{:S(2)}, u32[]{:S(2)}) collective-permute-start(f32[4,4,72,256]{3,2,1,0:T(8,128)S(1)} %get-tuple-element.21), channel_id=1, source_target_pairs={{0,32},{32,0},{1,33},{33,1},{2,34},{34,2},{3,35},{35,3},{4,36},{36... | collective-permute-start | bytes 3538952 | tf_op jit(solution)/shard_map/ppermute | solution.py:276
  17.3 4.0 %collective-permute-start.2 = (f32[4,4,64,256]{3,2,1,0:T(8,128)S(1)}, f32[4,4,64,256]{3,2,1,0:T(8,128)S(1)}, u32[]{:S(2)}, u32[]{:S(2)}) collective-permute-start(f32[4,4,64,256]{3,2,1,0:T(8,128)S(1)} %get-tuple-element.23), channel_id=1, source_target_pairs={{0,32},{32,0},{1,33},{33,1},{2,34},{34,2},{3,35},{35,3},{4,36},{36... | collective-permute-start | bytes 3145736 | tf_op jit(solution)/shard_map/ppermute | solution.py:276
  19.8 10.8 %collective-permute-start.1 = (f32[2,4,72,256]{3,2,1,0:T(8,128)S(1)}, f32[2,4,72,256]{3,2,1,0:T(8,128)S(1)}, u32[]{:S(2)}, u32[]{:S(2)}) collective-permute-start(f32[2,4,72,256]{3,2,1,0:T(8,128)S(1)} %slice_add_fusion), channel_id=1, source_target_pairs={{0,8},{8,0},{16,24},{24,16},{32,56},{40,48},{48,40},{56,32},{1,9},... | collective-permute-start | bytes 1769480 | tf_op jit(solution)/shard_map/ppermute | solution.py:293
  21.3 9.3 %collective-permute-start.3 = (f32[2,4,64,256]{3,2,1,0:T(8,128)S(1)}, f32[2,4,64,256]{3,2,1,0:T(8,128)S(1)}, u32[]{:S(2)}, u32[]{:S(2)}) collective-permute-start(f32[2,4,64,256]{3,2,1,0:T(8,128)S(1)} %slice_add_fusion.1), channel_id=1, source_target_pairs={{0,64},{64,0},{128,192},{192,128},{32,224},{96,160},{160,96},{224,... | collective-permute-start | bytes 1572872 | tf_op jit(solution)/shard_map/ppermute | solution.py:295
  30.8 6.0 %collective-permute-start.4 = (f32[4,72,256]{2,1,0:T(8,128)S(1)}, f32[4,72,256]{2,1,0:T(8,128)S(1)}, u32[]{:S(2)}, u32[]{:S(2)}) collective-permute-start(f32[4,72,256]{2,1,0:T(8,128)S(1)} %get-tuple-element.38), channel_id=1, source_target_pairs={{0,24},{8,16},{16,8},{24,0},{32,40},{40,32},{48,56},{56,48},{1,25}... | collective-permute-start | bytes 884744 | tf_op jit(solution)/shard_map/ppermute | solution.py:293
  31.0 5.6 %collective-permute-start.5 = (f32[4,64,256]{2,1,0:T(8,128)S(1)}, f32[4,64,256]{2,1,0:T(8,128)S(1)}, u32[]{:S(2)}, u32[]{:S(2)}) collective-permute-start(f32[4,64,256]{2,1,0:T(8,128)S(1)} %get-tuple-element.41), channel_id=1, source_target_pairs={{0,192},{64,128},{128,64},{192,0},{32,96},{96,32},{160,224},{224,1... | collective-permute-start | bytes 786440 | tf_op jit(solution)/shard_map/ppermute | solution.py:295
  36.8 7.4 %collective-permute-start.6 = (f32[2,72,256]{2,1,0:T(8,128)S(1)}, f32[2,72,256]{2,1,0:T(8,128)S(1)}, u32[]{:S(2)}, u32[]{:S(2)}) collective-permute-start(f32[2,72,256]{2,1,0:T(8,128)S(1)} %fusion.5), channel_id=1, source_target_pairs={{0,64},{64,0},{128,192},{192,128},{32,224},{96,160},{160,96},{224,... | collective-permute-start | bytes 442376 | tf_op jit(solution)/shard_map/ppermute | solution.py:295
  39.0 5.1 %collective-permute-start.7 = (f32[2,64,256]{2,1,0:T(8,128)S(1)}, f32[2,64,256]{2,1,0:T(8,128)S(1)}, u32[]{:S(2)}, u32[]{:S(2)}) collective-permute-start(f32[2,64,256]{2,1,0:T(8,128)S(1)} %fusion.7), channel_id=1, source_target_pairs={{0,8},{8,0},{16,24},{24,16},{32,56},{40,48},{48,40},{56,32},{1,9},... | collective-permute-start | bytes 393224 | tf_op jit(solution)/shard_map/ppermute | solution.py:293
  44.2 3.3 %collective-permute-start.8 = (f32[72,256]{1,0:T(8,128)S(1)}, f32[72,256]{1,0:T(8,128)S(1)}, u32[]{:S(2)}, u32[]{:S(2)}) collective-permute-start(f32[72,256]{1,0:T(8,128)S(1)} %fusion.10), channel_id=1, source_target_pairs={{0,192},{64,128},{128,64},{192,0},{32,96},{96,32},{160,224},{224,1... | collective-permute-start | bytes 221192 | tf_op jit(solution)/shard_map/ppermute | solution.py:295
  44.3 3.2 %collective-permute-start.9 = (f32[64,256]{1,0:T(8,128)S(1)}, f32[64,256]{1,0:T(8,128)S(1)}, u32[]{:S(2)}, u32[]{:S(2)}) collective-permute-start(f32[64,256]{1,0:T(8,128)S(1)} %fusion.21), channel_id=1, source_target_pairs={{0,24},{8,16},{16,8},{24,0},{32,40},{40,32},{48,56},{56,48},{1,25}... | collective-permute-start | bytes 196616 | tf_op jit(solution)/shard_map/ppermute | solution.py:293
  64.3 9.2 %collective-permute-start.10 = (f32[16,256]{1,0:T(8,128)S(1)}, f32[16,256]{1,0:T(8,128)S(1)}, u32[]{:S(2)}, u32[]{:S(2)}) collective-permute-start(f32[16,256]{1,0:T(8,128)S(1)} %slice.210), channel_id=1, source_target_pairs={{0,32},{32,0},{1,33},{33,1},{2,34},{34,2},{3,35},{35,3},{4,36},{36... | collective-permute-start | bytes 49160 | tf_op jit(solution)/shard_map/ppermute | solution.py:276
  74.8 20.8 %all-to-all-start.1 = ((f32[128,1,512]{2,1,0:T(1,128)}), f32[128,1,512]{2,1,0:T(1,128)S(1)}, u32[]{:S(2)}, u32[]{:S(2)}) async-start(f32[128,1,512]{2,1,0:T(1,128)} %copy.6), calls=%async_computation.1 | async-start | bytes 524288 | tf_op jit(solution)/shard_map/all_to_all | solution.py:284
  81.2 4.5 %collective-permute-start.14 = (f32[32,256]{1,0:T(8,128)S(1)}, f32[32,256]{1,0:T(8,128)S(1)}, u32[]{:S(2)}, u32[]{:S(2)}) collective-permute-start(f32[32,256]{1,0:T(8,128)S(1)} %get-tuple-element.51), channel_id=1, source_target_pairs={{0,192},{64,128},{128,64},{192,0},{1,193},{65,129},{129,65},{193,1... | collective-permute-start | bytes 98312 | tf_op jit(solution)/shard_map/ppermute | solution.py:280
  83.6 4.8 %collective-permute-start.13 = (f32[32,256]{1,0:T(8,128)S(1)}, f32[32,256]{1,0:T(8,128)S(1)}, u32[]{:S(2)}, u32[]{:S(2)}) collective-permute-start(f32[32,256]{1,0:T(8,128)S(1)} %get-tuple-element.51), channel_id=1, source_target_pairs={{0,128},{64,192},{128,0},{192,64},{1,129},{65,193},{129,1},{193,65... | collective-permute-start | bytes 98312 | tf_op jit(solution)/shard_map/ppermute | solution.py:280
  83.8 4.7 %collective-permute-start.12 = (f32[32,256]{1,0:T(8,128)S(1)}, f32[32,256]{1,0:T(8,128)S(1)}, u32[]{:S(2)}, u32[]{:S(2)}) collective-permute-start(f32[32,256]{1,0:T(8,128)S(1)} %get-tuple-element.51), channel_id=1, source_target_pairs={{0,64},{64,0},{128,192},{192,128},{1,65},{65,1},{129,193},{193,129... | collective-permute-start | bytes 98312 | tf_op jit(solution)/shard_map/ppermute | solution.py:280
  95.6 9.3 %copy-start.1 = (f32[128,256]{1,0:T(8,128)}, f32[128,256]{1,0:T(8,128)S(1)}, u32[]{:S(2)}) copy-start(f32[128,256]{1,0:T(8,128)S(1)} %get-tuple-element.43.mine_ref) | copy-start | bytes 393220
  95.7 9.3 %collective-permute-start.11 = (f32[128,256]{1,0:T(8,128)S(1)}, f32[128,256]{1,0:T(8,128)S(1)}, u32[]{:S(2)}, u32[]{:S(2)}) collective-permute-start(f32[128,256]{1,0:T(8,128)S(1)} %get-tuple-element.43.mine_ref), channel_id=1, source_target_pairs={{0,32},{32,0},{1,33},{33,1},{2,34},{34,2},{3,35},{35,3},{4,36},{36... | collective-permute-start | bytes 393224 | tf_op jit(solution)/shard_map/ppermute | solution.py:276
  98.7 18.2 %all-to-all-start.2 = ((f32[128,1,256]{2,1,0:T(1,128)}), f32[128,1,256]{2,1,0:T(1,128)S(1)}, u32[]{:S(2)}, u32[]{:S(2)}) async-start(f32[128,1,256]{2,1,0:T(1,128)} %broadcast_in_dim.19), calls=%async_computation.2 | async-start | bytes 262144 | tf_op jit(solution)/shard_map/all_to_all | solution.py:284
  104.9 0.6 copy-start.3
  117.0 2.3 %copy-start.2 = (f32[128,1,256]{2,0,1:T(8,128)}, f32[128,1,256]{2,0,1:T(8,128)S(1)}, u32[]{:S(2)}) copy-start(f32[128,1,256]{2,0,1:T(8,128)S(1)} %copy.12) | copy-start | bytes 393220
  117.0 2.3 %collective-permute-start.15 = (f32[128,256]{1,0:T(8,128)S(1)}, f32[128,256]{1,0:T(8,128)S(1)}, u32[]{:S(2)}, u32[]{:S(2)}) collective-permute-start(f32[128,256]{1,0:T(8,128)S(1)} %bitcast.84), channel_id=1, source_target_pairs={{0,32},{32,0},{1,33},{33,1},{2,34},{34,2},{3,35},{35,3},{4,36},{36... | collective-permute-start | bytes 393224 | tf_op jit(solution)/shard_map/ppermute | solution.py:276
  119.2 0.6 copy-start.4

commit v4 on v3

--- a/solution.py
+++ b/solution.py
@@ -11,9 +11,10 @@
 
 PSTEPS = 6
 NX, NC, NY, NZ = 4, 2, 4, 8
+LOADS = 2
 AXES = ("x", "c", "y", "z")
 CHIPS = ("x", "y", "z")
-PANEL, GROUP, LANES = 32, 8, 128
+PANEL, GROUP, LANES = 64, 16, 128
 HIGHEST = lax.Precision.HIGHEST
 VMEM_LIMIT = 48 * 2**20
 NN, TN, NT = ((1,), (0,)), ((0,), (0,)), ((1,), (1,))
@@ -52,11 +53,15 @@
 ):
     step = pl.program_id(0)
     rank = matrix_ref.shape[1]
-
-    @pl.when(step < NY)
+    wide = high.shape[2]
+
+    @pl.when(step < LOADS)
     def _():
         parts = split(emb_ref[...])
-        high[step], low[step] = parts
+        for k in range(NY // LOADS):
+            at = step * (NY // LOADS) + k
+            high[at] = parts[0][:, k * wide : (k + 1) * wide]
+            low[at] = parts[1][:, k * wide : (k + 1) * wide]
         term = three(parts, split(matrix_ref[...]), NN)
 
         @pl.when(step == 0)
@@ -67,15 +72,15 @@
         def _():
             sketch_ref[...] += term
 
-    @pl.when(step == NY)
+    @pl.when(step == LOADS)
     def _():
         sketch = sketch_ref[...]
         s_high[...], s_low[...] = split(sketch)
         gram[...] = tn(sketch, sketch)
 
-    @pl.when(step >= NY)
+    @pl.when(step >= LOADS)
     def _():
-        y = step - NY
+        y = step - LOADS
         product = three((high[y], low[y]), (s_high[...], s_low[...]), TN)
         product = product.reshape(NZ, NX, NC, -1, rank)
         first = slots_ref[0] == 0
@@ -107,22 +112,22 @@
 
     def spec_a(base):
         return pl.BlockSpec(
-            (1,) + part_a.shape[1:], lambda i, s: (s[base + jnp.maximum(i - NY, 0)], 0, 0, 0)
+            (1,) + part_a.shape[1:], lambda i, s: (s[base + jnp.maximum(i - LOADS, 0)], 0, 0, 0)
         )
 
     def spec_b(base):
         return pl.BlockSpec(
-            (NX, 1) + part_b.shape[2:], lambda i, s: (0, s[base + jnp.maximum(i - NY, 0)], 0, 0)
+            (NX, 1) + part_b.shape[2:], lambda i, s: (0, s[base + jnp.maximum(i - LOADS, 0)], 0, 0)
         )
 
     return pl.pallas_call(
         products_kernel,
         grid_spec=pltpu.PrefetchScalarGridSpec(
             num_scalar_prefetch=1,
-            grid=(2 * NY,),
+            grid=(LOADS + NY,),
             in_specs=[
-                pl.BlockSpec((rows, wide), lambda i, s: (0, jnp.minimum(i, NY - 1))),
-                pl.BlockSpec((wide, rank), lambda i, s: (jnp.minimum(i, NY - 1), 0)),
+                pl.BlockSpec((rows, width // LOADS), lambda i, s: (0, jnp.minimum(i, LOADS - 1))),
+                pl.BlockSpec((width // LOADS, rank), lambda i, s: (jnp.minimum(i, LOADS - 1), 0)),
             ],
             out_specs=(
                 pl.BlockSpec((rows, rank), lambda i, s: (0, 0)),
@@ -179,12 +184,13 @@
             for j in range(GROUP):
                 pivot = cols[j][j : j + 1, :]
                 pivots.append(pivot)
-                factor = cols[j] * (1.0 / pivot)
-                top = jnp.where(sub > j, factor[:GROUP], 0.0)
-                factor = top if tall == GROUP else jnp.concatenate([top, factor[GROUP:]], axis=0)
-                tiles = [t - factor * t[j : j + 1, :] for t in tiles]
+                low = jnp.where(sub > j, cols[j][:GROUP], 0.0)
+                if tall > GROUP:
+                    low = jnp.concatenate([low, cols[j][GROUP:]], axis=0)
+                pivot = 1.0 / pivot
+                tiles = [t - low * (t[j : j + 1, :] * pivot) for t in tiles]
                 cols = [
-                    q if m <= j else q - factor * q[j : j + 1, :] for m, q in enumerate(cols)
+                    q if m <= j else q - low * (q[j : j + 1, :] * pivot) for m, q in enumerate(cols)
                 ]
             for i, t in enumerate(tiles):
                 done[i].append(t[:GROUP])
@@ -208,45 +214,50 @@
 
 
 def basis_kernel(
-    scale, core_ref, mine_ref, other_ref, sketch_ref, rows_ref, inverse_ref, basis_ref, out_ref,
-    left, right,
+    scale, slots_ref, mine_ref, other_ref, sketch_ref, part_0, part_1, part_2, part_3, inverse_ref,
+    basis_ref, out_ref, left, right, rows,
 ):
     order = left.shape[0]
-    join(core_ref, mine_ref, other_ref, left)
+    join(slots_ref, mine_ref, other_ref, left)
+    for r, part in enumerate((part_0, part_1, part_2, part_3)):
+        size = part.shape[0]
+        at = pl.multiple_of((slots_ref[slots_ref.shape[0] - 1] ^ r) * size, size)
+        rows[pl.ds(at, size), :] = part[...]
     across = lax.broadcasted_iota(jnp.int32, (order, order), 1)
     down = lax.broadcasted_iota(jnp.int32, (order, order), 0)
     right[...] = jnp.where(across == down, 1.0, 0.0)
     inverse_ref[...] = jnp.zeros_like(inverse_ref)
     eliminate(inverse_ref, left, right)
-    inverse = inverse_ref[...]
-    basis_ref[...] = nt(sketch_ref[...], inverse) * scale
-    out_ref[...] = nt(rows_ref[...], inverse)
-
-
-def basis(core, mine, other, sketch, block_rows, scale):
+    inverse = split(inverse_ref[...])
+    basis_ref[...] = three(split(sketch_ref[...]), inverse, NT) * scale
+    out_ref[...] = three(split(rows[...]), inverse, NT)
+
+
+def basis(slots, mine, other, sketch, parts, scale):
     order = sketch.shape[1]
+    rows = jax.ShapeDtypeStruct((NX * parts[0].shape[0], order), jnp.float32)
     return pl.pallas_call(
         functools.partial(basis_kernel, scale),
         out_shape=(
             jax.ShapeDtypeStruct((order, order), jnp.float32),
             jax.ShapeDtypeStruct(sketch.shape, jnp.float32),
-            jax.ShapeDtypeStruct(block_rows.shape, jnp.float32),
+            rows,
         ),
         in_specs=[pl.BlockSpec(memory_space=pltpu.SMEM)]
-        + [pl.BlockSpec(memory_space=pltpu.VMEM)] * 4,
-        scratch_shapes=[pltpu.VMEM((order, order), jnp.float32)] * 2,
+        + [pl.BlockSpec(memory_space=pltpu.VMEM)] * (3 + NX),
+        scratch_shapes=[pltpu.VMEM((order, order), jnp.float32)] * 2
+        + [pltpu.VMEM(rows.shape, jnp.float32)],
         cost_estimate=pl.CostEstimate(flops=10**10, bytes_accessed=2**21, transcendentals=0),
-    )(core, mine, other, sketch, block_rows)
-
-
-def whiten_kernel(width, core_ref, mine_ref, other_ref, inverse_ref, rows_ref, out_ref, inner):
-    join(core_ref, mine_ref, other_ref, inner)
-    inverse = inverse_ref[...]
-    order = inverse.shape[0]
+    )(slots, mine, other, sketch, *parts)
+
+
+def whiten_kernel(width, slots_ref, mine_ref, other_ref, inverse_ref, rows_ref, out_ref, inner):
+    join(slots_ref, mine_ref, other_ref, inner)
+    inverse = split(inverse_ref[...])
+    order = inverse_ref.shape[0]
     across = lax.broadcasted_iota(jnp.int32, (order, order), 1)
     down = lax.broadcasted_iota(jnp.int32, (order, order), 0)
     diagonal = jnp.where(across == down, 1.5, 0.0)
-    inverse = split(inverse)
     cross = three(split(three(inverse, split(inner[...]), NN)), inverse, NT)
     squares = jnp.sum(cross * cross, axis=0, keepdims=True)
     frob = jnp.sqrt(jnp.sum(squares, axis=1, keepdims=True))
@@ -255,12 +266,15 @@
     for step in range(PSTEPS):
         middle = split(diagonal - 0.5 * now)
         if step < PSTEPS - 1:
-            now = three(split(three(middle, split(now), NN)), middle, NN)
+            halves = [now[:LANES], now[LANES:]]
+            for _ in range(2):
+                halves = [three(split(half), middle, NN) for half in halves]
+            now = jnp.concatenate(halves, axis=0)
         projected = three(split(projected), middle, NN)
     out_ref[...] = projected
 
 
-def whiten(core, mine, other, inverse, block_rows, width):
+def whiten(slots, mine, other, inverse, block_rows, width):
     order = inverse.shape[0]
     return pl.pallas_call(
         functools.partial(whiten_kernel, width),
@@ -269,7 +283,7 @@
         + [pl.BlockSpec(memory_space=pltpu.VMEM)] * 4,
         scratch_shapes=[pltpu.VMEM((order, order), jnp.float32)],
         cost_estimate=pl.CostEstimate(flops=10**10, bytes_accessed=2**20, transcendentals=0),
-    )(core, mine, other, inverse, block_rows)
+    )(slots, mine, other, inverse, block_rows)
 
 
 def to_core(block):
@@ -327,7 +341,7 @@
     core = c.reshape(1)
 
     slots = jnp.concatenate(
-        [core] + [ring_slots(k, at) for at in (y, x) for k in (c, 1 - c)]
+        [core] + [ring_slots(k, at) for at in (y, x) for k in (c, 1 - c)] + [x.reshape(1)]
     )
     sketch, keep_a, keep_b, send_a, send_b = products(slots, embeddings, sketch_matrix)
     got_a, got_b = to_core(send_a), to_core(send_b)
@@ -347,24 +361,20 @@
             jnp.where(first_core, from_core, own_product),
         ]
     )
-    around = jnp.stack([pair] + [along_x(pair, r) for r in (1, 2, 3)])
-    block_rows = jnp.concatenate(
-        [lax.dynamic_index_in_dim(around, x ^ r, 0, keepdims=False) for r in range(NX)]
-    )
-
     half = jnp.where(first_core, pair[:, :chips], pair[:, chips:])
     inner = tn(half, pair)
     packet = jnp.concatenate([inner, jnp.broadcast_to(own_gram, inner.shape)], axis=1)
-    packet = exchange(packet, CHIPS)
+    packet, *parts = lax.optimization_barrier(
+        (exchange(packet, CHIPS), pair, *(along_x(pair, r) for r in (1, 2, 3)))
+    )
     gram = packet[:, rank:]
     inner_row = jnp.sum(packet[:, :rank], axis=0, keepdims=True)
     inner = exchange(jnp.broadcast_to(inner_row, inner.shape), CHIPS)
-
     inverse, left_basis, projected = basis(
-        core, gram, to_core(gram), sketch, block_rows, math.sqrt(total_rows)
+        slots, gram, to_core(gram), sketch, parts, math.sqrt(total_rows)
     )
     inner, inverse = lax.optimization_barrier((inner, inverse))
-    right_basis = whiten(core, inner, to_core(inner), inverse, projected, width)
+    right_basis = whiten(slots, inner, to_core(inner), inverse, projected, width)
     return (left_basis, right_basis)
 
 

time: 126 us -> 125 us (level)
  Pallas kernels: 29.8 us -> 27 us
  waiting for transfers between devices: 34.9 us -> 36.5 us
    all_to_all x2, waiting for transfers between devices: 7.61 us -> 13 us  [exchange(): return lax.all_to_all(blocks, axes, 0, 0, tiled=True)]
    ppermute x3, waiting for transfers between devices: 3.9 us -> 0.01 us  [along_x(): return lax.ppermute(block, 'x', [(x, x ^ flip) for x in range(NX)])]
    pallas_call x1, Pallas kernels: 10.9 us -> 8.79 us  [basis(): pl.pallas_call(functools.partial(basis_kernel, scale), out_shape=(jax.Sha...]
  transfers between devices with their start and end apart: 18 -> 18, of which waited for: 13 -> 11; matrix products, arithmetic and copies ran while one was open for 1% -> 1% of each run, Pallas kernels for 9% -> 7%
where the time goes in v4:
time: 125 us; the launch traced here: 124 us
  starting transfers between devices  39.2 us (31%)
  waiting for transfers between devices  36.5 us (29%)
  Pallas kernels  27 us (22%)
  blocking collectives  16.6 us (13%)
  local copies, waits for them, and re-layouts  3.13 us (3%)
    all_to_all x1, blocking collectives, exchange(): return lax.all_to_all(blocks, axes, 0, 0, tiled=True)  16.6 us
    ppermute x5, starting transfers between devices, to_core(): return lax.ppermute(block, 'c', [(0, 1), (1, 0)])  14.7 us
    all_to_all x2, waiting for transfers between devices, exchange(): return lax.all_to_all(blocks, axes, 0, 0, tiled=True)  13 us
    pallas_call x1, Pallas kernels, products(): pl.pallas_call(products_kernel, grid_spec=pltpu.PrefetchScalarGridSpec(nu...  12.9 us
    ppermute x4, waiting for transfers between devices, ring_pairs(): return lax.ppermute(block, ('x', 'c'), pairs)  12.6 us
    all_to_all x2, starting transfers between devices, exchange(): return lax.all_to_all(blocks, axes, 0, 0, tiled=True)  12.5 us
    pallas_call x1, Pallas kernels, basis(): pl.pallas_call(functools.partial(basis_kernel, scale), out_shape=(jax.Sha...  8.79 us
    ppermute x4, waiting for transfers between devices, ring_pairs(): return lax.ppermute(block, ('c', 'y'), pairs)  6.3 us
  transfers between devices with their start and end apart: 18, of which 11 were waited for; matrix products, arithmetic and copies ran while one was open for 1% of the time, Pallas kernels for 7%

profile of v4, /device:TPU:1, one launch (start us, length us, event | category | flops | bytes accessed | tf_op | source)
XLA Modules:
  0.0 124.3 jit_solution(4667336371215125297)
XLA Ops:
  0.7 0.1 concatenate.15.slots_ref
  0.8 12.9 %shard_map.41 = (f32[512,256]{1,0:T(8,128)S(1)}, f32[4,4,72,256]{3,2,1,0:T(8,128)S(1)}, f32[4,4,64,256]{3,2,1,0:T(8,128)S(1)}, f32[4,4,72,256]{3,2,1,0:T(8,128)S(1)}, f32[4,4,64,256]{3,2,1,0:T(8,128)S(1)}) custom-call(s32[18]{0:T(128)S(1)} %concatenate.15.slots_ref, f32[512,4096]{1,0:T(8,128)} %emb_ref.1, f32[4096,256]{1,0:T(8,128)} %matrix_ref.1), custom_call_target="tpu_custom_call" | custom-call | flops 6442450944 | bytes 25165824 | tf_op jit(solution)/shard_map/pallas_call | solution.py:123
  13.7 3.3 %collective-permute-start = (f32[4,4,72,256]{3,2,1,0:T(8,128)S(1)}, f32[4,4,72,256]{3,2,1,0:T(8,128)S(1)}, u32[]{:S(2)}, u32[]{:S(2)}) collective-permute-start(f32[4,4,72,256]{3,2,1,0:T(8,128)S(1)} %get-tuple-element.26), channel_id=1, source_target_pairs={{0,32},{32,0},{1,33},{33,1},{2,34},{34,2},{3,35},{35,3},{4,36},{36... | collective-permute-start | bytes 3538952 | tf_op jit(solution)/shard_map/ppermute | solution.py:290
  17.0 0.1 collective-permute-start.2
  17.1 2.4 %collective-permute-done = f32[4,4,72,256]{3,2,1,0:T(8,128)S(1)} collective-permute-done((f32[4,4,72,256]{3,2,1,0:T(8,128)S(1)}, f32[4,4,72,256]{3,2,1,0:T(8,128)S(1)}, u32[]{:S(2)}, u32[]{:S(2)}) %collective-permute-start) | collective-permute-done | bytes 1179680 | tf_op jit(solution)/shard_map/ppermute | solution.py:290
  19.5 0.1 slice_add_fusion
  19.6 1.1 collective-permute-start.1
  20.7 0.3 collective-permute-done.2
  21.0 0.1 slice_add_fusion.1
  21.1 2.2 %collective-permute-start.3 = (f32[2,4,64,256]{3,2,1,0:T(8,128)S(1)}, f32[2,4,64,256]{3,2,1,0:T(8,128)S(1)}, u32[]{:S(2)}, u32[]{:S(2)}) collective-permute-start(f32[2,4,64,256]{3,2,1,0:T(8,128)S(1)} %slice_add_fusion.1), channel_id=1, source_target_pairs={{0,64},{64,0},{128,192},{192,128},{32,224},{96,160},{160,96},{224,... | collective-permute-start | bytes 1572872 | tf_op jit(solution)/shard_map/ppermute | solution.py:309
  23.3 7.1 %collective-permute-done.3 = f32[2,4,64,256]{3,2,1,0:T(8,128)S(1)} collective-permute-done((f32[2,4,64,256]{3,2,1,0:T(8,128)S(1)}, f32[2,4,64,256]{3,2,1,0:T(8,128)S(1)}, u32[]{:S(2)}, u32[]{:S(2)}) %collective-permute-start.3) | collective-permute-done | bytes 524320 | tf_op jit(solution)/shard_map/ppermute | solution.py:309
  30.4 0.1 fusion.1
  30.5 0.1 collective-permute-start.4
  30.6 0.1 slice_add_fusion.4
  30.7 0.1 collective-permute-start.5
  30.8 5.5 %collective-permute-done.5 = f32[4,64,256]{2,1,0:T(8,128)S(1)} collective-permute-done((f32[4,64,256]{2,1,0:T(8,128)S(1)}, f32[4,64,256]{2,1,0:T(8,128)S(1)}, u32[]{:S(2)}, u32[]{:S(2)}) %collective-permute-start.5) | collective-permute-done | bytes 262176 | tf_op jit(solution)/shard_map/ppermute | solution.py:309
  36.3 0.2 collective-permute-done.4
  36.5 2.2 %collective-permute-start.6 = (f32[2,72,256]{2,1,0:T(8,128)S(1)}, f32[2,72,256]{2,1,0:T(8,128)S(1)}, u32[]{:S(2)}, u32[]{:S(2)}) collective-permute-start(f32[2,72,256]{2,1,0:T(8,128)S(1)} %fusion.5), channel_id=1, source_target_pairs={{0,64},{64,0},{128,192},{192,128},{32,224},{96,160},{160,96},{224,... | collective-permute-start | bytes 442376 | tf_op jit(solution)/shard_map/ppermute | solution.py:309
  38.8 1.7 %collective-permute-start.7 = (f32[2,64,256]{2,1,0:T(8,128)S(1)}, f32[2,64,256]{2,1,0:T(8,128)S(1)}, u32[]{:S(2)}, u32[]{:S(2)}) collective-permute-start(f32[2,64,256]{2,1,0:T(8,128)S(1)} %fusion.7), channel_id=1, source_target_pairs={{0,8},{8,0},{16,24},{24,16},{32,56},{40,48},{48,40},{56,32},{1,9},... | collective-permute-start | bytes 393224 | tf_op jit(solution)/shard_map/ppermute | solution.py:307
  40.5 3.4 %collective-permute-done.7 = f32[2,64,256]{2,1,0:T(8,128)S(1)} collective-permute-done((f32[2,64,256]{2,1,0:T(8,128)S(1)}, f32[2,64,256]{2,1,0:T(8,128)S(1)}, u32[]{:S(2)}, u32[]{:S(2)}) %collective-permute-start.7) | collective-permute-done | bytes 131104 | tf_op jit(solution)/shard_map/ppermute | solution.py:307
  43.9 0.0 collective-permute-done.6
  43.9 0.1 collective-permute-start.8
  44.1 0.5 collective-permute-start.9
  44.5 2.7 %collective-permute-done.9 = f32[64,256]{1,0:T(8,128)S(1)} collective-permute-done((f32[64,256]{1,0:T(8,128)S(1)}, f32[64,256]{1,0:T(8,128)S(1)}, u32[]{:S(2)}, u32[]{:S(2)}) %collective-permute-start.9) | collective-permute-done | bytes 65568 | tf_op jit(solution)/shard_map/ppermute | solution.py:307
  47.3 0.0 collective-permute-done.8
  47.4 16.6 %all_to_all.26 = f32[8,17,256]{2,1,0:T(8,128)S(1)} all-to-all(f32[8,17,256]{2,1,0:T(8,128)S(1)} %pad_maximum_fusion), channel_id=1, replica_groups=mesh['x'=4,'c'=2,'y'=4,'z'=8] {'z'}, dimensions={0} | all-to-all | bytes 278528 | tf_op jit(solution)/shard_map/all_to_all | solution.py:298
  64.1 8.3 %collective-permute-start.10 = (f32[16,256]{1,0:T(8,128)S(1)}, f32[16,256]{1,0:T(8,128)S(1)}, u32[]{:S(2)}, u32[]{:S(2)}) collective-permute-start(f32[16,256]{1,0:T(8,128)S(1)} %slice.210), channel_id=1, source_target_pairs={{0,32},{32,0},{1,33},{33,1},{2,34},{34,2},{3,35},{35,3},{4,36},{36... | collective-permute-start | bytes 49160 | tf_op jit(solution)/shard_map/ppermute | solution.py:290
  72.4 0.8 collective-permute-done.10
  73.2 0.3 fusion.24
  73.6 1.0 copy.6
  74.6 6.4 %all-to-all-start.1 = ((f32[128,1,512]{2,1,0:T(1,128)}), f32[128,1,512]{2,1,0:T(1,128)S(1)}, u32[]{:S(2)}, u32[]{:S(2)}) async-start(f32[128,1,512]{2,1,0:T(1,128)} %copy.6), calls=%async_computation.1 | async-start | bytes 524288 | tf_op jit(solution)/shard_map/all_to_all | solution.py:298
  80.9 0.8 collective-permute-start.11
  81.7 2.8 %collective-permute-start.12 = (f32[32,256]{1,0:T(8,128)S(1)}, f32[32,256]{1,0:T(8,128)S(1)}, u32[]{:S(2)}, u32[]{:S(2)}) collective-permute-start(f32[32,256]{1,0:T(8,128)S(1)} %pad_maximum_fusion.2.part_0), channel_id=1, source_target_pairs={{0,128},{64,192},{128,0},{192,64},{1,129},{65,193},{129,1},{193,65... | collective-permute-start | bytes 98312 | tf_op jit(solution)/shard_map/ppermute | solution.py:294
  84.5 0.4 collective-permute-start.13
  84.9 10.4 %all-to-all-done.1 = f32[128,1,512]{2,1,0:T(1,128)S(1)} async-done(((f32[128,1,512]{2,1,0:T(1,128)}), f32[128,1,512]{2,1,0:T(1,128)S(1)}, u32[]{:S(2)}, u32[]{:S(2)}) %all-to-all-start.1) | async-done | bytes 262176 | tf_op jit(solution)/shard_map/all_to_all | solution.py:298
  95.4 0.0 collective-permute-done.12.part_2
  95.4 0.0 collective-permute-done.13.part_3
  95.5 0.0 copy-start.2
  95.5 1.7 %collective-permute-start.14 = (f32[128,256]{1,0:T(8,128)S(1)}, f32[128,256]{1,0:T(8,128)S(1)}, u32[]{:S(2)}, u32[]{:S(2)}) collective-permute-start(f32[128,256]{1,0:T(8,128)S(1)} %get-tuple-element.53.mine_ref), channel_id=1, source_target_pairs={{0,32},{32,0},{1,33},{33,1},{2,34},{34,2},{3,35},{35,3},{4,36},{36... | collective-permute-start | bytes 393224 | tf_op jit(solution)/shard_map/ppermute | solution.py:290
  97.2 0.7 broadcast_in_dim.19
  97.9 6.2 %all-to-all-start.2 = ((f32[128,1,256]{2,1,0:T(1,128)}), f32[128,1,256]{2,1,0:T(1,128)S(1)}, u32[]{:S(2)}, u32[]{:S(2)}) async-start(f32[128,1,256]{2,1,0:T(1,128)} %broadcast_in_dim.19), calls=%async_computation.2 | async-start | bytes 262144 | tf_op jit(solution)/shard_map/all_to_all | solution.py:298
  104.1 0.6 copy-done.5
  104.7 8.8 %shard_map.42 = (f32[256,256]{1,0:T(8,128)}, f32[512,256]{1,0:T(8,128)}, f32[128,256]{1,0:T(8,128)}) custom-call(s32[18]{0:T(128)} %copy-done, f32[128,256]{1,0:T(8,128)} %copy-done.2, f32[128,256]{1,0:T(8,128)} %copy-done.5, f32[512,256]{1,0:T(8,128)} %copy-done.1, f32[32,256]{1,0:T(8,128)} %copy-done.4, f32[32,256]{1,0:T(8,128)} %copy-done.7, ...), custom_call_target="tpu_custom_call" | custom-call | flops 10000000000 | bytes 2097152 | tf_op jit(solution)/shard_map/pallas_call | solution.py:239
  113.5 2.6 %all-to-all-done.2 = f32[128,1,256]{2,1,0:T(1,128)S(1)} async-done(((f32[128,1,256]{2,1,0:T(1,128)}), f32[128,1,256]{2,1,0:T(1,128)S(1)}, u32[]{:S(2)}, u32[]{:S(2)}) %all-to-all-start.2) | async-done | bytes 131104 | tf_op jit(solution)/shard_map/all_to_all | solution.py:298
  116.1 1.2 %collective-permute-start.15 = (f32[128,256]{1,0:T(8,128)S(1)}, f32[128,256]{1,0:T(8,128)S(1)}, u32[]{:S(2)}, u32[]{:S(2)}) collective-permute-start(f32[128,256]{1,0:T(8,128)S(1)} %bitcast.72), channel_id=1, source_target_pairs={{0,32},{32,0},{1,33},{33,1},{2,34},{34,2},{3,35},{35,3},{4,36},{36... | collective-permute-start | bytes 393224 | tf_op jit(solution)/shard_map/ppermute | solution.py:290
  117.4 1.0 collective-permute-done.15.other_ref
  118.4 0.6 copy-done.6
  119.0 5.3 %shard_map.43 = f32[128,256]{1,0:T(8,128)} custom-call(s32[18]{0:T(128)} %copy-done, f32[128,256]{1,0:T(8,128)} %bitcast.73, f32[128,256]{1,0:T(8,128)} %copy-done.6, f32[256,256]{1,0:T(8,128)} %get-tuple-element.46.inverse_ref, f32[128,256]{1,0:T(8,128)} %get-tuple-element.47.rows_ref), custom_call_target="tpu_custom_call" | custom-call | flops 10000000000 | bytes 1048576 | tf_op jit(solution)/shard_map/pallas_call | solution.py:279
  (43 shorter events, 0.4 us)
Async XLA Ops:
  0.8 12.9 %copy-start = (s32[18]{0:T(128)}, s32[18]{0:T(128)S(1)}, u32[]{:S(2)}) copy-start(s32[18]{0:T(128)S(1)} %concatenate.15.slots_ref) | copy-start | bytes 220
  13.7 7.4 %copy-start.1 = (f32[512,256]{1,0:T(8,128)}, f32[512,256]{1,0:T(8,128)S(1)}, u32[]{:S(2)}) copy-start(f32[512,256]{1,0:T(8,128)S(1)} %get-tuple-element.38.sketch_ref) | copy-start | bytes 1572868
  13.7 5.8 %collective-permute-start = (f32[4,4,72,256]{3,2,1,0:T(8,128)S(1)}, f32[4,4,72,256]{3,2,1,0:T(8,128)S(1)}, u32[]{:S(2)}, u32[]{:S(2)}) collective-permute-start(f32[4,4,72,256]{3,2,1,0:T(8,128)S(1)} %get-tuple-element.26), channel_id=1, source_target_pairs={{0,32},{32,0},{1,33},{33,1},{2,34},{34,2},{3,35},{35,3},{4,36},{36... | collective-permute-start | bytes 3538952 | tf_op jit(solution)/shard_map/ppermute | solution.py:290
  17.0 4.0 %collective-permute-start.2 = (f32[4,4,64,256]{3,2,1,0:T(8,128)S(1)}, f32[4,4,64,256]{3,2,1,0:T(8,128)S(1)}, u32[]{:S(2)}, u32[]{:S(2)}) collective-permute-start(f32[4,4,64,256]{3,2,1,0:T(8,128)S(1)} %get-tuple-element.28), channel_id=1, source_target_pairs={{0,32},{32,0},{1,33},{33,1},{2,34},{34,2},{3,35},{35,3},{4,36},{36... | collective-permute-start | bytes 3145736 | tf_op jit(solution)/shard_map/ppermute | solution.py:290
  19.6 10.8 %collective-permute-start.1 = (f32[2,4,72,256]{3,2,1,0:T(8,128)S(1)}, f32[2,4,72,256]{3,2,1,0:T(8,128)S(1)}, u32[]{:S(2)}, u32[]{:S(2)}) collective-permute-start(f32[2,4,72,256]{3,2,1,0:T(8,128)S(1)} %slice_add_fusion), channel_id=1, source_target_pairs={{0,8},{8,0},{16,24},{24,16},{32,56},{40,48},{48,40},{56,32},{1,9},... | collective-permute-start | bytes 1769480 | tf_op jit(solution)/shard_map/ppermute | solution.py:307
  21.1 9.3 %collective-permute-start.3 = (f32[2,4,64,256]{3,2,1,0:T(8,128)S(1)}, f32[2,4,64,256]{3,2,1,0:T(8,128)S(1)}, u32[]{:S(2)}, u32[]{:S(2)}) collective-permute-start(f32[2,4,64,256]{3,2,1,0:T(8,128)S(1)} %slice_add_fusion.1), channel_id=1, source_target_pairs={{0,64},{64,0},{128,192},{192,128},{32,224},{96,160},{160,96},{224,... | collective-permute-start | bytes 1572872 | tf_op jit(solution)/shard_map/ppermute | solution.py:309
  30.5 6.0 %collective-permute-start.4 = (f32[4,72,256]{2,1,0:T(8,128)S(1)}, f32[4,72,256]{2,1,0:T(8,128)S(1)}, u32[]{:S(2)}, u32[]{:S(2)}) collective-permute-start(f32[4,72,256]{2,1,0:T(8,128)S(1)} %get-tuple-element.48), channel_id=1, source_target_pairs={{0,24},{8,16},{16,8},{24,0},{32,40},{40,32},{48,56},{56,48},{1,25}... | collective-permute-start | bytes 884744 | tf_op jit(solution)/shard_map/ppermute | solution.py:307
  30.7 5.6 %collective-permute-start.5 = (f32[4,64,256]{2,1,0:T(8,128)S(1)}, f32[4,64,256]{2,1,0:T(8,128)S(1)}, u32[]{:S(2)}, u32[]{:S(2)}) collective-permute-start(f32[4,64,256]{2,1,0:T(8,128)S(1)} %get-tuple-element.51), channel_id=1, source_target_pairs={{0,192},{64,128},{128,64},{192,0},{32,96},{96,32},{160,224},{224,1... | collective-permute-start | bytes 786440 | tf_op jit(solution)/shard_map/ppermute | solution.py:309
  36.5 7.4 %collective-permute-start.6 = (f32[2,72,256]{2,1,0:T(8,128)S(1)}, f32[2,72,256]{2,1,0:T(8,128)S(1)}, u32[]{:S(2)}, u32[]{:S(2)}) collective-permute-start(f32[2,72,256]{2,1,0:T(8,128)S(1)} %fusion.5), channel_id=1, source_target_pairs={{0,64},{64,0},{128,192},{192,128},{32,224},{96,160},{160,96},{224,... | collective-permute-start | bytes 442376 | tf_op jit(solution)/shard_map/ppermute | solution.py:309
  38.8 5.1 %collective-permute-start.7 = (f32[2,64,256]{2,1,0:T(8,128)S(1)}, f32[2,64,256]{2,1,0:T(8,128)S(1)}, u32[]{:S(2)}, u32[]{:S(2)}) collective-permute-start(f32[2,64,256]{2,1,0:T(8,128)S(1)} %fusion.7), channel_id=1, source_target_pairs={{0,8},{8,0},{16,24},{24,16},{32,56},{40,48},{48,40},{56,32},{1,9},... | collective-permute-start | bytes 393224 | tf_op jit(solution)/shard_map/ppermute | solution.py:307
  43.9 3.3 %collective-permute-start.8 = (f32[72,256]{1,0:T(8,128)S(1)}, f32[72,256]{1,0:T(8,128)S(1)}, u32[]{:S(2)}, u32[]{:S(2)}) collective-permute-start(f32[72,256]{1,0:T(8,128)S(1)} %fusion.10), channel_id=1, source_target_pairs={{0,192},{64,128},{128,64},{192,0},{32,96},{96,32},{160,224},{224,1... | collective-permute-start | bytes 221192 | tf_op jit(solution)/shard_map/ppermute | solution.py:309
  44.1 3.2 %collective-permute-start.9 = (f32[64,256]{1,0:T(8,128)S(1)}, f32[64,256]{1,0:T(8,128)S(1)}, u32[]{:S(2)}, u32[]{:S(2)}) collective-permute-start(f32[64,256]{1,0:T(8,128)S(1)} %fusion.21), channel_id=1, source_target_pairs={{0,24},{8,16},{16,8},{24,0},{32,40},{40,32},{48,56},{56,48},{1,25}... | collective-permute-start | bytes 196616 | tf_op jit(solution)/shard_map/ppermute | solution.py:307
  64.1 9.2 %collective-permute-start.10 = (f32[16,256]{1,0:T(8,128)S(1)}, f32[16,256]{1,0:T(8,128)S(1)}, u32[]{:S(2)}, u32[]{:S(2)}) collective-permute-start(f32[16,256]{1,0:T(8,128)S(1)} %slice.210), channel_id=1, source_target_pairs={{0,32},{32,0},{1,33},{33,1},{2,34},{34,2},{3,35},{35,3},{4,36},{36... | collective-permute-start | bytes 49160 | tf_op jit(solution)/shard_map/ppermute | solution.py:290
  74.6 20.8 %all-to-all-start.1 = ((f32[128,1,512]{2,1,0:T(1,128)}), f32[128,1,512]{2,1,0:T(1,128)S(1)}, u32[]{:S(2)}, u32[]{:S(2)}) async-start(f32[128,1,512]{2,1,0:T(1,128)} %copy.6), calls=%async_computation.1 | async-start | bytes 524288 | tf_op jit(solution)/shard_map/all_to_all | solution.py:298
  80.9 23.2 %copy-start.4 = (f32[32,256]{1,0:T(8,128)}, f32[32,256]{1,0:T(8,128)S(1)}, u32[]{:S(2)}) copy-start(f32[32,256]{1,0:T(8,128)S(1)} %pad_maximum_fusion.2.part_0) | copy-start | bytes 98308
  80.9 14.4 %collective-permute-start.11 = (f32[32,256]{1,0:T(8,128)S(1)}, f32[32,256]{1,0:T(8,128)S(1)}, u32[]{:S(2)}, u32[]{:S(2)}) collective-permute-start(f32[32,256]{1,0:T(8,128)S(1)} %pad_maximum_fusion.2.part_0), channel_id=1, source_target_pairs={{0,64},{64,0},{128,192},{192,128},{1,65},{65,1},{129,193},{193,129... | collective-permute-start | bytes 98312 | tf_op jit(solution)/shard_map/ppermute | solution.py:294
  81.7 13.7 %collective-permute-start.12 = (f32[32,256]{1,0:T(8,128)S(1)}, f32[32,256]{1,0:T(8,128)S(1)}, u32[]{:S(2)}, u32[]{:S(2)}) collective-permute-start(f32[32,256]{1,0:T(8,128)S(1)} %pad_maximum_fusion.2.part_0), channel_id=1, source_target_pairs={{0,128},{64,192},{128,0},{192,64},{1,129},{65,193},{129,1},{193,65... | collective-permute-start | bytes 98312 | tf_op jit(solution)/shard_map/ppermute | solution.py:294
  84.5 10.9 %collective-permute-start.13 = (f32[32,256]{1,0:T(8,128)S(1)}, f32[32,256]{1,0:T(8,128)S(1)}, u32[]{:S(2)}, u32[]{:S(2)}) collective-permute-start(f32[32,256]{1,0:T(8,128)S(1)} %pad_maximum_fusion.2.part_0), channel_id=1, source_target_pairs={{0,192},{64,128},{128,64},{192,0},{1,193},{65,129},{129,65},{193,1... | collective-permute-start | bytes 98312 | tf_op jit(solution)/shard_map/ppermute | solution.py:294
  95.4 8.7 %copy-start.7 = (f32[32,256]{1,0:T(8,128)}, f32[32,256]{1,0:T(8,128)S(1)}, u32[]{:S(2)}) copy-start(f32[32,256]{1,0:T(8,128)S(1)} %collective-permute-done.11.part_1) | copy-start | bytes 98308
  95.4 8.7 %copy-start.8 = (f32[32,256]{1,0:T(8,128)}, f32[32,256]{1,0:T(8,128)S(1)}, u32[]{:S(2)}) copy-start(f32[32,256]{1,0:T(8,128)S(1)} %collective-permute-done.12.part_2) | copy-start | bytes 98308
  95.4 8.7 %copy-start.9 = (f32[32,256]{1,0:T(8,128)}, f32[32,256]{1,0:T(8,128)S(1)}, u32[]{:S(2)}) copy-start(f32[32,256]{1,0:T(8,128)S(1)} %collective-permute-done.13.part_3) | copy-start | bytes 98308
  95.5 8.7 %copy-start.2 = (f32[128,256]{1,0:T(8,128)}, f32[128,256]{1,0:T(8,128)S(1)}, u32[]{:S(2)}) copy-start(f32[128,256]{1,0:T(8,128)S(1)} %get-tuple-element.53.mine_ref) | copy-start | bytes 393220
  95.5 8.6 %collective-permute-start.14 = (f32[128,256]{1,0:T(8,128)S(1)}, f32[128,256]{1,0:T(8,128)S(1)}, u32[]{:S(2)}, u32[]{:S(2)}) collective-permute-start(f32[128,256]{1,0:T(8,128)S(1)} %get-tuple-element.53.mine_ref), channel_id=1, source_target_pairs={{0,32},{32,0},{1,33},{33,1},{2,34},{34,2},{3,35},{35,3},{4,36},{36... | collective-permute-start | bytes 393224 | tf_op jit(solution)/shard_map/ppermute | solution.py:290
  97.9 18.2 %all-to-all-start.2 = ((f32[128,1,256]{2,1,0:T(1,128)}), f32[128,1,256]{2,1,0:T(1,128)S(1)}, u32[]{:S(2)}, u32[]{:S(2)}) async-start(f32[128,1,256]{2,1,0:T(1,128)} %broadcast_in_dim.19), calls=%async_computation.2 | async-start | bytes 262144 | tf_op jit(solution)/shard_map/all_to_all | solution.py:298
  104.1 0.6 copy-start.5
  116.1 2.3 %copy-start.3 = (f32[128,1,256]{2,0,1:T(8,128)}, f32[128,1,256]{2,0,1:T(8,128)S(1)}, u32[]{:S(2)}) copy-start(f32[128,1,256]{2,0,1:T(8,128)S(1)} %copy.12) | copy-start | bytes 393220
  116.1 2.2 %collective-permute-start.15 = (f32[128,256]{1,0:T(8,128)S(1)}, f32[128,256]{1,0:T(8,128)S(1)}, u32[]{:S(2)}, u32[]{:S(2)}) collective-permute-start(f32[128,256]{1,0:T(8,128)S(1)} %bitcast.72), channel_id=1, source_target_pairs={{0,32},{32,0},{1,33},{33,1},{2,34},{34,2},{3,35},{35,3},{4,36},{36... | collective-permute-start | bytes 393224 | tf_op jit(solution)/shard_map/ppermute | solution.py:290
  118.4 0.7 copy-start.6

commit v5 on v4

--- a/solution.py
+++ b/solution.py
@@ -17,6 +17,7 @@
 PANEL, GROUP, LANES = 64, 16, 128
 HIGHEST = lax.Precision.HIGHEST
 VMEM_LIMIT = 48 * 2**20
+SMALL_LIMIT = 16 * 2**20
 NN, TN, NT = ((1,), (0,)), ((0,), (0,)), ((1,), (1,))
 
 
@@ -247,6 +248,7 @@
         + [pl.BlockSpec(memory_space=pltpu.VMEM)] * (3 + NX),
         scratch_shapes=[pltpu.VMEM((order, order), jnp.float32)] * 2
         + [pltpu.VMEM(rows.shape, jnp.float32)],
+        compiler_params=pltpu.CompilerParams(vmem_limit_bytes=SMALL_LIMIT),
         cost_estimate=pl.CostEstimate(flops=10**10, bytes_accessed=2**21, transcendentals=0),
     )(slots, mine, other, sketch, *parts)
 
@@ -282,6 +284,7 @@
         in_specs=[pl.BlockSpec(memory_space=pltpu.SMEM)]
         + [pl.BlockSpec(memory_space=pltpu.VMEM)] * 4,
         scratch_shapes=[pltpu.VMEM((order, order), jnp.float32)],
+        compiler_params=pltpu.CompilerParams(vmem_limit_bytes=SMALL_LIMIT),
         cost_estimate=pl.CostEstimate(flops=10**10, bytes_accessed=2**20, transcendentals=0),
     )(slots, mine, other, inverse, block_rows)
 

time: 125 us -> 123 us (0.984)
  waiting for transfers between devices: 36.5 us -> 37.9 us
  Pallas kernels: 27 us -> 25.7 us
  local copies, waits for them, and re-layouts: 3.13 us -> 1.84 us
    all_to_all x2, waiting for transfers between devices: 13 us -> 14.5 us  [exchange(): return lax.all_to_all(blocks, axes, 0, 0, tiled=True)]
    unnamed x22 -> x2, local copies, waits for them, and re-layouts: 1.3 us -> 0.03 us
where the time goes in v5:
time: 123 us
  starting transfers between devices  39.2 us (32%)
  waiting for transfers between devices  37.9 us (31%)
  Pallas kernels  25.7 us (21%)
  blocking collectives  16.6 us (13%)
  local copies, waits for them, and re-layouts  1.84 us (1%)
    all_to_all x1, blocking collectives, exchange(): return lax.all_to_all(blocks, axes, 0, 0, tiled=True)  16.6 us
    ppermute x5, starting transfers between devices, to_core(): return lax.ppermute(block, 'c', [(0, 1), (1, 0)])  14.7 us
    all_to_all x2, waiting for transfers between devices, exchange(): return lax.all_to_all(blocks, axes, 0, 0, tiled=True)  14.5 us
    pallas_call x1, Pallas kernels, products(): pl.pallas_call(products_kernel, grid_spec=pltpu.PrefetchScalarGridSpec(nu...  12.9 us
    ppermute x4, waiting for transfers between devices, ring_pairs(): return lax.ppermute(block, ('x', 'c'), pairs)  12.6 us
    all_to_all x2, starting transfers between devices, exchange(): return lax.all_to_all(blocks, axes, 0, 0, tiled=True)  12.5 us
    pallas_call x1, Pallas kernels, basis(): pl.pallas_call(functools.partial(basis_kernel, scale), out_shape=(jax.Sha...  8.04 us
    ppermute x4, waiting for transfers between devices, ring_pairs(): return lax.ppermute(block, ('c', 'y'), pairs)  6.3 us
  transfers between devices with their start and end apart: 18, of which 11 were waited for; matrix products, arithmetic and copies ran while one was open for 1% of the time, Pallas kernels for 7%

profile of v5, /device:TPU:1, one launch (start us, length us, event | category | flops | bytes accessed | tf_op | source)
XLA Modules:
  0.0 123.0 jit_solution(17977626622822507730)
XLA Ops:
  0.7 0.1 concatenate.15.slots_ref
  0.8 12.9 %shard_map.41 = (f32[512,256]{1,0:T(8,128)S(1)}, f32[4,4,72,256]{3,2,1,0:T(8,128)S(1)}, f32[4,4,64,256]{3,2,1,0:T(8,128)S(1)}, f32[4,4,72,256]{3,2,1,0:T(8,128)S(1)}, f32[4,4,64,256]{3,2,1,0:T(8,128)S(1)}) custom-call(s32[18]{0:T(128)S(1)} %concatenate.15.slots_ref, f32[512,4096]{1,0:T(8,128)} %emb_ref.1, f32[4096,256]{1,0:T(8,128)} %matrix_ref.1), custom_call_target="tpu_custom_call" | custom-call | flops 6442450944 | bytes 25165824 | tf_op jit(solution)/shard_map/pallas_call | solution.py:124
  13.7 3.3 %collective-permute-start = (f32[4,4,72,256]{3,2,1,0:T(8,128)S(1)}, f32[4,4,72,256]{3,2,1,0:T(8,128)S(1)}, u32[]{:S(2)}, u32[]{:S(2)}) collective-permute-start(f32[4,4,72,256]{3,2,1,0:T(8,128)S(1)} %get-tuple-element.26), channel_id=1, source_target_pairs={{0,32},{32,0},{1,33},{33,1},{2,34},{34,2},{3,35},{35,3},{4,36},{36... | collective-permute-start | bytes 3538952 | tf_op jit(solution)/shard_map/ppermute | solution.py:293
  17.0 0.1 collective-permute-start.2
  17.1 2.4 %collective-permute-done = f32[4,4,72,256]{3,2,1,0:T(8,128)S(1)} collective-permute-done((f32[4,4,72,256]{3,2,1,0:T(8,128)S(1)}, f32[4,4,72,256]{3,2,1,0:T(8,128)S(1)}, u32[]{:S(2)}, u32[]{:S(2)}) %collective-permute-start) | collective-permute-done | bytes 1179680 | tf_op jit(solution)/shard_map/ppermute | solution.py:293
  19.5 0.1 slice_add_fusion
  19.6 1.1 collective-permute-start.1
  20.6 0.3 collective-permute-done.2
  21.0 0.1 slice_add_fusion.1
  21.1 2.2 %collective-permute-start.3 = (f32[2,4,64,256]{3,2,1,0:T(8,128)S(1)}, f32[2,4,64,256]{3,2,1,0:T(8,128)S(1)}, u32[]{:S(2)}, u32[]{:S(2)}) collective-permute-start(f32[2,4,64,256]{3,2,1,0:T(8,128)S(1)} %slice_add_fusion.1), channel_id=1, source_target_pairs={{0,64},{64,0},{128,192},{192,128},{32,224},{96,160},{160,96},{224,... | collective-permute-start | bytes 1572872 | tf_op jit(solution)/shard_map/ppermute | solution.py:312
  23.3 7.1 %collective-permute-done.3 = f32[2,4,64,256]{3,2,1,0:T(8,128)S(1)} collective-permute-done((f32[2,4,64,256]{3,2,1,0:T(8,128)S(1)}, f32[2,4,64,256]{3,2,1,0:T(8,128)S(1)}, u32[]{:S(2)}, u32[]{:S(2)}) %collective-permute-start.3) | collective-permute-done | bytes 524320 | tf_op jit(solution)/shard_map/ppermute | solution.py:312
  30.4 0.0 collective-permute-done.1
  30.4 0.1 fusion.1
  30.5 0.1 collective-permute-start.4
  30.6 0.1 slice_add_fusion.4
  30.7 0.1 collective-permute-start.5
  30.8 5.5 %collective-permute-done.5 = f32[4,64,256]{2,1,0:T(8,128)S(1)} collective-permute-done((f32[4,64,256]{2,1,0:T(8,128)S(1)}, f32[4,64,256]{2,1,0:T(8,128)S(1)}, u32[]{:S(2)}, u32[]{:S(2)}) %collective-permute-start.5) | collective-permute-done | bytes 262176 | tf_op jit(solution)/shard_map/ppermute | solution.py:312
  36.3 0.2 collective-permute-done.4
  36.5 2.2 %collective-permute-start.6 = (f32[2,72,256]{2,1,0:T(8,128)S(1)}, f32[2,72,256]{2,1,0:T(8,128)S(1)}, u32[]{:S(2)}, u32[]{:S(2)}) collective-permute-start(f32[2,72,256]{2,1,0:T(8,128)S(1)} %fusion.5), channel_id=1, source_target_pairs={{0,64},{64,0},{128,192},{192,128},{32,224},{96,160},{160,96},{224,... | collective-permute-start | bytes 442376 | tf_op jit(solution)/shard_map/ppermute | solution.py:312
  38.7 1.7 %collective-permute-start.7 = (f32[2,64,256]{2,1,0:T(8,128)S(1)}, f32[2,64,256]{2,1,0:T(8,128)S(1)}, u32[]{:S(2)}, u32[]{:S(2)}) collective-permute-start(f32[2,64,256]{2,1,0:T(8,128)S(1)} %fusion.7), channel_id=1, source_target_pairs={{0,8},{8,0},{16,24},{24,16},{32,56},{40,48},{48,40},{56,32},{1,9},... | collective-permute-start | bytes 393224 | tf_op jit(solution)/shard_map/ppermute | solution.py:310
  40.4 3.4 %collective-permute-done.7 = f32[2,64,256]{2,1,0:T(8,128)S(1)} collective-permute-done((f32[2,64,256]{2,1,0:T(8,128)S(1)}, f32[2,64,256]{2,1,0:T(8,128)S(1)}, u32[]{:S(2)}, u32[]{:S(2)}) %collective-permute-start.7) | collective-permute-done | bytes 131104 | tf_op jit(solution)/shard_map/ppermute | solution.py:310
  43.9 0.0 collective-permute-done.6
  43.9 0.1 collective-permute-start.8
  44.0 0.5 collective-permute-start.9
  44.5 2.7 %collective-permute-done.9 = f32[64,256]{1,0:T(8,128)S(1)} collective-permute-done((f32[64,256]{1,0:T(8,128)S(1)}, f32[64,256]{1,0:T(8,128)S(1)}, u32[]{:S(2)}, u32[]{:S(2)}) %collective-permute-start.9) | collective-permute-done | bytes 65568 | tf_op jit(solution)/shard_map/ppermute | solution.py:310
  47.2 0.0 collective-permute-done.8
  47.4 16.6 %all_to_all.26 = f32[8,17,256]{2,1,0:T(8,128)S(1)} all-to-all(f32[8,17,256]{2,1,0:T(8,128)S(1)} %pad_maximum_fusion), channel_id=1, replica_groups=mesh['x'=4,'c'=2,'y'=4,'z'=8] {'z'}, dimensions={0} | all-to-all | bytes 278528 | tf_op jit(solution)/shard_map/all_to_all | solution.py:301
  64.0 8.3 %collective-permute-start.10 = (f32[16,256]{1,0:T(8,128)S(1)}, f32[16,256]{1,0:T(8,128)S(1)}, u32[]{:S(2)}, u32[]{:S(2)}) collective-permute-start(f32[16,256]{1,0:T(8,128)S(1)} %slice.210), channel_id=1, source_target_pairs={{0,32},{32,0},{1,33},{33,1},{2,34},{34,2},{3,35},{35,3},{4,36},{36... | collective-permute-start | bytes 49160 | tf_op jit(solution)/shard_map/ppermute | solution.py:293
  72.4 0.8 collective-permute-done.10
  73.2 0.3 fusion.24
  73.5 1.0 copy.6
  74.5 6.4 %all-to-all-start.1 = ((f32[128,1,512]{2,1,0:T(1,128)}), f32[128,1,512]{2,1,0:T(1,128)S(1)}, u32[]{:S(2)}, u32[]{:S(2)}) async-start(f32[128,1,512]{2,1,0:T(1,128)} %copy.6), calls=%async_computation.1 | async-start | bytes 524288 | tf_op jit(solution)/shard_map/all_to_all | solution.py:301
  80.9 0.8 collective-permute-start.11
  81.6 2.8 %collective-permute-start.12 = (f32[32,256]{1,0:T(8,128)S(1)}, f32[32,256]{1,0:T(8,128)S(1)}, u32[]{:S(2)}, u32[]{:S(2)}) collective-permute-start(f32[32,256]{1,0:T(8,128)S(1)} %pad_maximum_fusion.2.part_0), channel_id=1, source_target_pairs={{0,128},{64,192},{128,0},{192,64},{1,129},{65,193},{129,1},{193,65... | collective-permute-start | bytes 98312 | tf_op jit(solution)/shard_map/ppermute | solution.py:297
  84.5 0.4 collective-permute-start.13
  84.8 10.5 %all-to-all-done.1 = f32[128,1,512]{2,1,0:T(1,128)S(1)} async-done(((f32[128,1,512]{2,1,0:T(1,128)}), f32[128,1,512]{2,1,0:T(1,128)S(1)}, u32[]{:S(2)}, u32[]{:S(2)}) %all-to-all-start.1) | async-done | bytes 262176 | tf_op jit(solution)/shard_map/all_to_all | solution.py:301
  95.3 0.0 collective-permute-done.11.part_1
  95.3 0.0 collective-permute-done.12.part_2
  95.3 0.0 collective-permute-done.13.part_3
  95.4 1.7 %collective-permute-start.14 = (f32[128,256]{1,0:T(8,128)S(1)}, f32[128,256]{1,0:T(8,128)S(1)}, u32[]{:S(2)}, u32[]{:S(2)}) collective-permute-start(f32[128,256]{1,0:T(8,128)S(1)} %get-tuple-element.53.mine_ref), channel_id=1, source_target_pairs={{0,32},{32,0},{1,33},{33,1},{2,34},{34,2},{3,35},{35,3},{4,36},{36... | collective-permute-start | bytes 393224 | tf_op jit(solution)/shard_map/ppermute | solution.py:293
  97.1 0.7 broadcast_in_dim.19
  97.8 6.2 %all-to-all-start.2 = ((f32[128,1,256]{2,1,0:T(1,128)}), f32[128,1,256]{2,1,0:T(1,128)S(1)}, u32[]{:S(2)}, u32[]{:S(2)}) async-start(f32[128,1,256]{2,1,0:T(1,128)} %broadcast_in_dim.19), calls=%async_computation.2 | async-start | bytes 262144 | tf_op jit(solution)/shard_map/all_to_all | solution.py:301
  104.0 0.0 collective-permute-done.14.other_ref
  104.0 8.0 %shard_map.42 = (f32[256,256]{1,0:T(8,128)S(1)}, f32[512,256]{1,0:T(8,128)}, f32[128,256]{1,0:T(8,128)S(1)}) custom-call(s32[18]{0:T(128)S(1)} %concatenate.15.slots_ref, f32[128,256]{1,0:T(8,128)S(1)} %get-tuple-element.53.mine_ref, f32[128,256]{1,0:T(8,128)S(1)} %collective-permute-done.14.other_ref, f32[512,256]{1,0:T(8,128)S(1)} %get-tuple-element.38.sketch_ref, ...), custom_call_target="tpu_custom_call" | custom-call | flops 10000000000 | bytes 2097152 | tf_op jit(solution)/shard_map/pallas_call | solution.py:240
  112.0 4.0 %all-to-all-done.2 = f32[128,1,256]{2,1,0:T(1,128)S(1)} async-done(((f32[128,1,256]{2,1,0:T(1,128)}), f32[128,1,256]{2,1,0:T(1,128)S(1)}, u32[]{:S(2)}, u32[]{:S(2)}) %all-to-all-start.2) | async-done | bytes 131104 | tf_op jit(solution)/shard_map/all_to_all | solution.py:301
  116.0 1.2 %collective-permute-start.15 = (f32[128,256]{1,0:T(8,128)S(1)}, f32[128,256]{1,0:T(8,128)S(1)}, u32[]{:S(2)}, u32[]{:S(2)}) collective-permute-start(f32[128,256]{1,0:T(8,128)S(1)} %bitcast.70), channel_id=1, source_target_pairs={{0,32},{32,0},{1,33},{33,1},{2,34},{34,2},{3,35},{35,3},{4,36},{36... | collective-permute-start | bytes 393224 | tf_op jit(solution)/shard_map/ppermute | solution.py:293
  117.3 1.0 collective-permute-done.15.other_ref
  118.3 4.7 %shard_map.43 = f32[128,256]{1,0:T(8,128)} custom-call(s32[18]{0:T(128)S(1)} %concatenate.15.slots_ref, f32[128,256]{1,0:T(8,128)S(1)} %bitcast.71, f32[128,256]{1,0:T(8,128)S(1)} %collective-permute-done.15.other_ref, f32[256,256]{1,0:T(8,128)S(1)} %get-tuple-element.46.inverse_ref, f32[128,256]{1,0:T(8,128)S(1)} %get-tuple-element.47.rows_ref), custom_call_target="tpu_custom_call" | custom-call | flops 10000000000 | bytes 1048576 | tf_op jit(solution)/shard_map/pallas_call | solution.py:281
  (23 shorter events, 0.3 us)
Async XLA Ops:
  13.7 5.8 %collective-permute-start = (f32[4,4,72,256]{3,2,1,0:T(8,128)S(1)}, f32[4,4,72,256]{3,2,1,0:T(8,128)S(1)}, u32[]{:S(2)}, u32[]{:S(2)}) collective-permute-start(f32[4,4,72,256]{3,2,1,0:T(8,128)S(1)} %get-tuple-element.26), channel_id=1, source_target_pairs={{0,32},{32,0},{1,33},{33,1},{2,34},{34,2},{3,35},{35,3},{4,36},{36... | collective-permute-start | bytes 3538952 | tf_op jit(solution)/shard_map/ppermute | solution.py:293
  17.0 4.0 %collective-permute-start.2 = (f32[4,4,64,256]{3,2,1,0:T(8,128)S(1)}, f32[4,4,64,256]{3,2,1,0:T(8,128)S(1)}, u32[]{:S(2)}, u32[]{:S(2)}) collective-permute-start(f32[4,4,64,256]{3,2,1,0:T(8,128)S(1)} %get-tuple-element.28), channel_id=1, source_target_pairs={{0,32},{32,0},{1,33},{33,1},{2,34},{34,2},{3,35},{35,3},{4,36},{36... | collective-permute-start | bytes 3145736 | tf_op jit(solution)/shard_map/ppermute | solution.py:293
  19.6 10.8 %collective-permute-start.1 = (f32[2,4,72,256]{3,2,1,0:T(8,128)S(1)}, f32[2,4,72,256]{3,2,1,0:T(8,128)S(1)}, u32[]{:S(2)}, u32[]{:S(2)}) collective-permute-start(f32[2,4,72,256]{3,2,1,0:T(8,128)S(1)} %slice_add_fusion), channel_id=1, source_target_pairs={{0,8},{8,0},{16,24},{24,16},{32,56},{40,48},{48,40},{56,32},{1,9},... | collective-permute-start | bytes 1769480 | tf_op jit(solution)/shard_map/ppermute | solution.py:310
  21.1 9.3 %collective-permute-start.3 = (f32[2,4,64,256]{3,2,1,0:T(8,128)S(1)}, f32[2,4,64,256]{3,2,1,0:T(8,128)S(1)}, u32[]{:S(2)}, u32[]{:S(2)}) collective-permute-start(f32[2,4,64,256]{3,2,1,0:T(8,128)S(1)} %slice_add_fusion.1), channel_id=1, source_target_pairs={{0,64},{64,0},{128,192},{192,128},{32,224},{96,160},{160,96},{224,... | collective-permute-start | bytes 1572872 | tf_op jit(solution)/shard_map/ppermute | solution.py:312
  30.5 6.0 %collective-permute-start.4 = (f32[4,72,256]{2,1,0:T(8,128)S(1)}, f32[4,72,256]{2,1,0:T(8,128)S(1)}, u32[]{:S(2)}, u32[]{:S(2)}) collective-permute-start(f32[4,72,256]{2,1,0:T(8,128)S(1)} %get-tuple-element.48), channel_id=1, source_target_pairs={{0,24},{8,16},{16,8},{24,0},{32,40},{40,32},{48,56},{56,48},{1,25}... | collective-permute-start | bytes 884744 | tf_op jit(solution)/shard_map/ppermute | solution.py:310
  30.7 5.6 %collective-permute-start.5 = (f32[4,64,256]{2,1,0:T(8,128)S(1)}, f32[4,64,256]{2,1,0:T(8,128)S(1)}, u32[]{:S(2)}, u32[]{:S(2)}) collective-permute-start(f32[4,64,256]{2,1,0:T(8,128)S(1)} %get-tuple-element.51), channel_id=1, source_target_pairs={{0,192},{64,128},{128,64},{192,0},{32,96},{96,32},{160,224},{224,1... | collective-permute-start | bytes 786440 | tf_op jit(solution)/shard_map/ppermute | solution.py:312
  36.5 7.4 %collective-permute-start.6 = (f32[2,72,256]{2,1,0:T(8,128)S(1)}, f32[2,72,256]{2,1,0:T(8,128)S(1)}, u32[]{:S(2)}, u32[]{:S(2)}) collective-permute-start(f32[2,72,256]{2,1,0:T(8,128)S(1)} %fusion.5), channel_id=1, source_target_pairs={{0,64},{64,0},{128,192},{192,128},{32,224},{96,160},{160,96},{224,... | collective-permute-start | bytes 442376 | tf_op jit(solution)/shard_map/ppermute | solution.py:312
  38.7 5.1 %collective-permute-start.7 = (f32[2,64,256]{2,1,0:T(8,128)S(1)}, f32[2,64,256]{2,1,0:T(8,128)S(1)}, u32[]{:S(2)}, u32[]{:S(2)}) collective-permute-start(f32[2,64,256]{2,1,0:T(8,128)S(1)} %fusion.7), channel_id=1, source_target_pairs={{0,8},{8,0},{16,24},{24,16},{32,56},{40,48},{48,40},{56,32},{1,9},... | collective-permute-start | bytes 393224 | tf_op jit(solution)/shard_map/ppermute | solution.py:310
  43.9 3.3 %collective-permute-start.8 = (f32[72,256]{1,0:T(8,128)S(1)}, f32[72,256]{1,0:T(8,128)S(1)}, u32[]{:S(2)}, u32[]{:S(2)}) collective-permute-start(f32[72,256]{1,0:T(8,128)S(1)} %fusion.10), channel_id=1, source_target_pairs={{0,192},{64,128},{128,64},{192,0},{32,96},{96,32},{160,224},{224,1... | collective-permute-start | bytes 221192 | tf_op jit(solution)/shard_map/ppermute | solution.py:312
  44.0 3.2 %collective-permute-start.9 = (f32[64,256]{1,0:T(8,128)S(1)}, f32[64,256]{1,0:T(8,128)S(1)}, u32[]{:S(2)}, u32[]{:S(2)}) collective-permute-start(f32[64,256]{1,0:T(8,128)S(1)} %fusion.21), channel_id=1, source_target_pairs={{0,24},{8,16},{16,8},{24,0},{32,40},{40,32},{48,56},{56,48},{1,25}... | collective-permute-start | bytes 196616 | tf_op jit(solution)/shard_map/ppermute | solution.py:310
  64.0 9.2 %collective-permute-start.10 = (f32[16,256]{1,0:T(8,128)S(1)}, f32[16,256]{1,0:T(8,128)S(1)}, u32[]{:S(2)}, u32[]{:S(2)}) collective-permute-start(f32[16,256]{1,0:T(8,128)S(1)} %slice.210), channel_id=1, source_target_pairs={{0,32},{32,0},{1,33},{33,1},{2,34},{34,2},{3,35},{35,3},{4,36},{36... | collective-permute-start | bytes 49160 | tf_op jit(solution)/shard_map/ppermute | solution.py:293
  74.5 20.8 %all-to-all-start.1 = ((f32[128,1,512]{2,1,0:T(1,128)}), f32[128,1,512]{2,1,0:T(1,128)S(1)}, u32[]{:S(2)}, u32[]{:S(2)}) async-start(f32[128,1,512]{2,1,0:T(1,128)} %copy.6), calls=%async_computation.1 | async-start | bytes 524288 | tf_op jit(solution)/shard_map/all_to_all | solution.py:301
  80.9 14.4 %collective-permute-start.11 = (f32[32,256]{1,0:T(8,128)S(1)}, f32[32,256]{1,0:T(8,128)S(1)}, u32[]{:S(2)}, u32[]{:S(2)}) collective-permute-start(f32[32,256]{1,0:T(8,128)S(1)} %pad_maximum_fusion.2.part_0), channel_id=1, source_target_pairs={{0,64},{64,0},{128,192},{192,128},{1,65},{65,1},{129,193},{193,129... | collective-permute-start | bytes 98312 | tf_op jit(solution)/shard_map/ppermute | solution.py:297
  81.6 13.7 %collective-permute-start.12 = (f32[32,256]{1,0:T(8,128)S(1)}, f32[32,256]{1,0:T(8,128)S(1)}, u32[]{:S(2)}, u32[]{:S(2)}) collective-permute-start(f32[32,256]{1,0:T(8,128)S(1)} %pad_maximum_fusion.2.part_0), channel_id=1, source_target_pairs={{0,128},{64,192},{128,0},{192,64},{1,129},{65,193},{129,1},{193,65... | collective-permute-start | bytes 98312 | tf_op jit(solution)/shard_map/ppermute | solution.py:297
  84.5 10.9 %collective-permute-start.13 = (f32[32,256]{1,0:T(8,128)S(1)}, f32[32,256]{1,0:T(8,128)S(1)}, u32[]{:S(2)}, u32[]{:S(2)}) collective-permute-start(f32[32,256]{1,0:T(8,128)S(1)} %pad_maximum_fusion.2.part_0), channel_id=1, source_target_pairs={{0,192},{64,128},{128,64},{192,0},{1,193},{65,129},{129,65},{193,1... | collective-permute-start | bytes 98312 | tf_op jit(solution)/shard_map/ppermute | solution.py:297
  95.4 8.6 %collective-permute-start.14 = (f32[128,256]{1,0:T(8,128)S(1)}, f32[128,256]{1,0:T(8,128)S(1)}, u32[]{:S(2)}, u32[]{:S(2)}) collective-permute-start(f32[128,256]{1,0:T(8,128)S(1)} %get-tuple-element.53.mine_ref), channel_id=1, source_target_pairs={{0,32},{32,0},{1,33},{33,1},{2,34},{34,2},{3,35},{35,3},{4,36},{36... | collective-permute-start | bytes 393224 | tf_op jit(solution)/shard_map/ppermute | solution.py:293
  97.8 18.2 %all-to-all-start.2 = ((f32[128,1,256]{2,1,0:T(1,128)}), f32[128,1,256]{2,1,0:T(1,128)S(1)}, u32[]{:S(2)}, u32[]{:S(2)}) async-start(f32[128,1,256]{2,1,0:T(1,128)} %broadcast_in_dim.19), calls=%async_computation.2 | async-start | bytes 262144 | tf_op jit(solution)/shard_map/all_to_all | solution.py:301
  116.0 2.2 %collective-permute-start.15 = (f32[128,256]{1,0:T(8,128)S(1)}, f32[128,256]{1,0:T(8,128)S(1)}, u32[]{:S(2)}, u32[]{:S(2)}) collective-permute-start(f32[128,256]{1,0:T(8,128)S(1)} %bitcast.70), channel_id=1, source_target_pairs={{0,32},{32,0},{1,33},{33,1},{2,34},{34,2},{3,35},{35,3},{4,36},{36... | collective-permute-start | bytes 393224 | tf_op jit(solution)/shard_map/ppermute | solution.py:293

commit v6 on v5

--- a/solution.py
+++ b/solution.py
@@ -324,10 +324,8 @@
     out = []
     sent = [sum(t[1:3] for t in terms) for terms in (terms_a, terms_b)]
     got = [ring_pairs(v, axis, 0) for v, axis in zip(sent, (axis_a, axis_b))]
-    got = lax.optimization_barrier(tuple(got))
     sent = [first(terms, 3) + g[1] for terms, g in zip((terms_a, terms_b), got)]
     more = [ring_pairs(v, axis, 1) for v, axis in zip(sent, (axis_a, axis_b))]
-    more = lax.optimization_barrier(tuple(more))
     for terms, g, m in zip((terms_a, terms_b), got, more):
         out.append([first(terms, 0), g[0], m])
     return out

time: 123 us -> 121 us (0.984)
  starting transfers between devices: 39.2 us -> 36.7 us
    ppermute x4, starting transfers between devices: 4.65 us -> 2.27 us  [ring_pairs(): return lax.ppermute(block, ('x', 'c'), pairs)]
    ppermute x5, starting transfers between devices: 14.7 us -> 13.2 us  [to_core(): return lax.ppermute(block, 'c', [(0, 1), (1, 0)])]
    all_to_all x2, starting transfers between devices: 12.5 us -> 14 us  [exchange(): return lax.all_to_all(blocks, axes, 0, 0, tiled=True)]
  transfers between devices with their start and end apart: 18 -> 18, of which waited for: 11 -> 14; matrix products, arithmetic and copies ran while one was open for 1% -> 1% of each run, Pallas kernels for 7% -> 7%
where the time goes in v6:
time: 121 us
  waiting for transfers between devices  38.6 us (32%)
  starting transfers between devices  36.7 us (30%)
  Pallas kernels  25.7 us (21%)
  blocking collectives  16.2 us (13%)
  local copies, waits for them, and re-layouts  1.84 us (2%)
    all_to_all x1, blocking collectives, exchange(): return lax.all_to_all(blocks, axes, 0, 0, tiled=True)  16.2 us
    all_to_all x2, waiting for transfers between devices, exchange(): return lax.all_to_all(blocks, axes, 0, 0, tiled=True)  14.2 us
    all_to_all x2, starting transfers between devices, exchange(): return lax.all_to_all(blocks, axes, 0, 0, tiled=True)  14 us
    ppermute x5, starting transfers between devices, to_core(): return lax.ppermute(block, 'c', [(0, 1), (1, 0)])  13.2 us
    pallas_call x1, Pallas kernels, products(): pl.pallas_call(products_kernel, grid_spec=pltpu.PrefetchScalarGridSpec(nu...  12.9 us
    ppermute x4, waiting for transfers between devices, ring_pairs(): return lax.ppermute(block, ('x', 'c'), pairs)  12.8 us
    pallas_call x1, Pallas kernels, basis(): pl.pallas_call(functools.partial(basis_kernel, scale), out_shape=(jax.Sha...  8.05 us
    ppermute x4, waiting for transfers between devices, ring_pairs(): return lax.ppermute(block, ('c', 'y'), pairs)  6.83 us
  transfers between devices with their start and end apart: 18, of which 14 were waited for; matrix products, arithmetic and copies ran while one was open for 1% of the time, Pallas kernels for 7%

profile of v6, /device:TPU:1, one launch (start us, length us, event | category | flops | bytes accessed | tf_op | source)
XLA Modules:
  0.0 120.8 jit_solution(494455748004194286)
XLA Ops:
  0.7 0.1 concatenate.15.slots_ref
  0.8 12.9 %shard_map.41 = (f32[512,256]{1,0:T(8,128)S(1)}, f32[4,4,72,256]{3,2,1,0:T(8,128)S(1)}, f32[4,4,64,256]{3,2,1,0:T(8,128)S(1)}, f32[4,4,72,256]{3,2,1,0:T(8,128)S(1)}, f32[4,4,64,256]{3,2,1,0:T(8,128)S(1)}) custom-call(s32[18]{0:T(128)S(1)} %concatenate.15.slots_ref, f32[512,4096]{1,0:T(8,128)} %emb_ref.1, f32[4096,256]{1,0:T(8,128)} %matrix_ref.1), custom_call_target="tpu_custom_call" | custom-call | flops 6442450944 | bytes 25165824 | tf_op jit(solution)/shard_map/pallas_call | solution.py:124
  13.7 3.3 %collective-permute-start.5 = (f32[4,4,64,256]{3,2,1,0:T(8,128)S(1)}, f32[4,4,64,256]{3,2,1,0:T(8,128)S(1)}, u32[]{:S(2)}, u32[]{:S(2)}) collective-permute-start(f32[4,4,64,256]{3,2,1,0:T(8,128)S(1)} %get-tuple-element.20), channel_id=1, source_target_pairs={{0,32},{32,0},{1,33},{33,1},{2,34},{34,2},{3,35},{35,3},{4,36},{36... | collective-permute-start | bytes 3145736 | tf_op jit(solution)/shard_map/ppermute | solution.py:293
  17.0 0.1 collective-permute-start
  17.1 2.2 %collective-permute-done.5 = f32[4,4,64,256]{3,2,1,0:T(8,128)S(1)} collective-permute-done((f32[4,4,64,256]{3,2,1,0:T(8,128)S(1)}, f32[4,4,64,256]{3,2,1,0:T(8,128)S(1)}, u32[]{:S(2)}, u32[]{:S(2)}) %collective-permute-start.5) | collective-permute-done | bytes 1048608 | tf_op jit(solution)/shard_map/ppermute | solution.py:293
  19.3 0.1 slice_add_fusion.1
  19.4 0.8 collective-permute-start.6
  20.2 0.8 collective-permute-done
  21.0 0.1 slice_add_fusion
  21.1 2.0 %collective-permute-start.1 = (f32[2,4,72,256]{3,2,1,0:T(8,128)S(1)}, f32[2,4,72,256]{3,2,1,0:T(8,128)S(1)}, u32[]{:S(2)}, u32[]{:S(2)}) collective-permute-start(f32[2,4,72,256]{3,2,1,0:T(8,128)S(1)} %slice_add_fusion), channel_id=1, source_target_pairs={{0,8},{8,0},{16,24},{24,16},{32,56},{40,48},{48,40},{56,32},{1,9},... | collective-permute-start | bytes 1769480 | tf_op jit(solution)/shard_map/ppermute | solution.py:310
  23.1 5.6 %collective-permute-done.6 = f32[2,4,64,256]{3,2,1,0:T(8,128)S(1)} collective-permute-done((f32[2,4,64,256]{3,2,1,0:T(8,128)S(1)}, f32[2,4,64,256]{3,2,1,0:T(8,128)S(1)}, u32[]{:S(2)}, u32[]{:S(2)}) %collective-permute-start.6) | collective-permute-done | bytes 524320 | tf_op jit(solution)/shard_map/ppermute | solution.py:312
  28.7 0.1 slice_add_fusion.7
  28.8 0.1 collective-permute-start.7
  28.9 2.2 %collective-permute-done.1 = f32[2,4,72,256]{3,2,1,0:T(8,128)S(1)} collective-permute-done((f32[2,4,72,256]{3,2,1,0:T(8,128)S(1)}, f32[2,4,72,256]{3,2,1,0:T(8,128)S(1)}, u32[]{:S(2)}, u32[]{:S(2)}) %collective-permute-start.1) | collective-permute-done | bytes 589856 | tf_op jit(solution)/shard_map/ppermute | solution.py:310
  31.1 0.1 slice_add_fusion.4
  31.2 0.1 collective-permute-start.2
  31.3 3.1 %collective-permute-done.7 = f32[4,64,256]{2,1,0:T(8,128)S(1)} collective-permute-done((f32[4,64,256]{2,1,0:T(8,128)S(1)}, f32[4,64,256]{2,1,0:T(8,128)S(1)}, u32[]{:S(2)}, u32[]{:S(2)}) %collective-permute-start.7) | collective-permute-done | bytes 262176 | tf_op jit(solution)/shard_map/ppermute | solution.py:312
  34.4 1.1 collective-permute-start.8
  35.5 1.6 %collective-permute-done.2 = f32[4,72,256]{2,1,0:T(8,128)S(1)} collective-permute-done((f32[4,72,256]{2,1,0:T(8,128)S(1)}, f32[4,72,256]{2,1,0:T(8,128)S(1)}, u32[]{:S(2)}, u32[]{:S(2)}) %collective-permute-start.2) | collective-permute-done | bytes 294944 | tf_op jit(solution)/shard_map/ppermute | solution.py:310
  37.2 1.2 %collective-permute-start.3 = (f32[2,72,256]{2,1,0:T(8,128)S(1)}, f32[2,72,256]{2,1,0:T(8,128)S(1)}, u32[]{:S(2)}, u32[]{:S(2)}) collective-permute-start(f32[2,72,256]{2,1,0:T(8,128)S(1)} %slice_add_fusion.8), channel_id=1, source_target_pairs={{0,64},{64,0},{128,192},{192,128},{32,224},{96,160},{160,96},{224,... | collective-permute-start | bytes 442376 | tf_op jit(solution)/shard_map/ppermute | solution.py:312
  38.4 1.8 %collective-permute-done.8 = f32[2,64,256]{2,1,0:T(8,128)S(1)} collective-permute-done((f32[2,64,256]{2,1,0:T(8,128)S(1)}, f32[2,64,256]{2,1,0:T(8,128)S(1)}, u32[]{:S(2)}, u32[]{:S(2)}) %collective-permute-start.8) | collective-permute-done | bytes 131104 | tf_op jit(solution)/shard_map/ppermute | solution.py:310
  40.3 0.1 collective-permute-start.9
  40.4 2.1 %collective-permute-done.3 = f32[2,72,256]{2,1,0:T(8,128)S(1)} collective-permute-done((f32[2,72,256]{2,1,0:T(8,128)S(1)}, f32[2,72,256]{2,1,0:T(8,128)S(1)}, u32[]{:S(2)}, u32[]{:S(2)}) %collective-permute-start.3) | collective-permute-done | bytes 147488 | tf_op jit(solution)/shard_map/ppermute | solution.py:312
  42.5 0.1 collective-permute-start.4
  42.6 1.2 collective-permute-done.9
  43.8 2.0 %collective-permute-done.4 = f32[72,256]{1,0:T(8,128)S(1)} collective-permute-done((f32[72,256]{1,0:T(8,128)S(1)}, f32[72,256]{1,0:T(8,128)S(1)}, u32[]{:S(2)}, u32[]{:S(2)}) %collective-permute-start.4) | collective-permute-done | bytes 73760 | tf_op jit(solution)/shard_map/ppermute | solution.py:312
  45.9 16.2 %all_to_all.26 = f32[8,17,256]{2,1,0:T(8,128)S(1)} all-to-all(f32[8,17,256]{2,1,0:T(8,128)S(1)} %pad_maximum_fusion), channel_id=1, replica_groups=mesh['x'=4,'c'=2,'y'=4,'z'=8] {'z'}, dimensions={0} | all-to-all | bytes 278528 | tf_op jit(solution)/shard_map/all_to_all | solution.py:301
  62.1 6.5 %collective-permute-start.10 = (f32[16,256]{1,0:T(8,128)S(1)}, f32[16,256]{1,0:T(8,128)S(1)}, u32[]{:S(2)}, u32[]{:S(2)}) collective-permute-start(f32[16,256]{1,0:T(8,128)S(1)} %slice.228), channel_id=1, source_target_pairs={{0,32},{32,0},{1,33},{33,1},{2,34},{34,2},{3,35},{35,3},{4,36},{36... | collective-permute-start | bytes 49160 | tf_op jit(solution)/shard_map/ppermute | solution.py:293
  68.7 0.8 collective-permute-done.10
  69.5 0.3 fusion.20
  69.9 1.0 copy.6
  70.8 7.8 %all-to-all-start.1 = ((f32[128,1,512]{2,1,0:T(1,128)}), f32[128,1,512]{2,1,0:T(1,128)S(1)}, u32[]{:S(2)}, u32[]{:S(2)}) async-start(f32[128,1,512]{2,1,0:T(1,128)} %copy.6), calls=%async_computation.1 | async-start | bytes 524288 | tf_op jit(solution)/shard_map/all_to_all | solution.py:301
  78.7 0.8 collective-permute-start.11
  79.4 2.8 %collective-permute-start.12 = (f32[32,256]{1,0:T(8,128)S(1)}, f32[32,256]{1,0:T(8,128)S(1)}, u32[]{:S(2)}, u32[]{:S(2)}) collective-permute-start(f32[32,256]{1,0:T(8,128)S(1)} %pad_maximum_fusion.2.part_0), channel_id=1, source_target_pairs={{0,128},{64,192},{128,0},{192,64},{1,129},{65,193},{129,1},{193,65... | collective-permute-start | bytes 98312 | tf_op jit(solution)/shard_map/ppermute | solution.py:297
  82.2 0.4 collective-permute-start.13
  82.6 10.2 %all-to-all-done.1 = f32[128,1,512]{2,1,0:T(1,128)S(1)} async-done(((f32[128,1,512]{2,1,0:T(1,128)}), f32[128,1,512]{2,1,0:T(1,128)S(1)}, u32[]{:S(2)}, u32[]{:S(2)}) %all-to-all-start.1) | async-done | bytes 262176 | tf_op jit(solution)/shard_map/all_to_all | solution.py:301
  92.8 0.0 collective-permute-done.11.part_1
  92.8 0.0 collective-permute-done.12.part_2
  92.8 0.0 collective-permute-done.13.part_3
  92.9 2.0 %collective-permute-start.14 = (f32[128,256]{1,0:T(8,128)S(1)}, f32[128,256]{1,0:T(8,128)S(1)}, u32[]{:S(2)}, u32[]{:S(2)}) collective-permute-start(f32[128,256]{1,0:T(8,128)S(1)} %get-tuple-element.37.mine_ref), channel_id=1, source_target_pairs={{0,32},{32,0},{1,33},{33,1},{2,34},{34,2},{3,35},{35,3},{4,36},{36... | collective-permute-start | bytes 393224 | tf_op jit(solution)/shard_map/ppermute | solution.py:293
  94.8 0.7 broadcast_in_dim.19
  95.6 6.2 %all-to-all-start.2 = ((f32[128,1,256]{2,1,0:T(1,128)}), f32[128,1,256]{2,1,0:T(1,128)S(1)}, u32[]{:S(2)}, u32[]{:S(2)}) async-start(f32[128,1,256]{2,1,0:T(1,128)} %broadcast_in_dim.19), calls=%async_computation.2 | async-start | bytes 262144 | tf_op jit(solution)/shard_map/all_to_all | solution.py:301
  101.7 0.0 collective-permute-done.14.other_ref
  101.8 8.0 %shard_map.42 = (f32[256,256]{1,0:T(8,128)S(1)}, f32[512,256]{1,0:T(8,128)}, f32[128,256]{1,0:T(8,128)S(1)}) custom-call(s32[18]{0:T(128)S(1)} %concatenate.15.slots_ref, f32[128,256]{1,0:T(8,128)S(1)} %get-tuple-element.37.mine_ref, f32[128,256]{1,0:T(8,128)S(1)} %collective-permute-done.14.other_ref, f32[512,256]{1,0:T(8,128)S(1)} %get-tuple-element.22.sketch_ref, ...), custom_call_target="tpu_custom_call" | custom-call | flops 10000000000 | bytes 2097152 | tf_op jit(solution)/shard_map/pallas_call | solution.py:240
  109.8 4.0 %all-to-all-done.2 = f32[128,1,256]{2,1,0:T(1,128)S(1)} async-done(((f32[128,1,256]{2,1,0:T(1,128)}), f32[128,1,256]{2,1,0:T(1,128)S(1)}, u32[]{:S(2)}, u32[]{:S(2)}) %all-to-all-start.2) | async-done | bytes 131104 | tf_op jit(solution)/shard_map/all_to_all | solution.py:301
  113.8 1.2 %collective-permute-start.15 = (f32[128,256]{1,0:T(8,128)S(1)}, f32[128,256]{1,0:T(8,128)S(1)}, u32[]{:S(2)}, u32[]{:S(2)}) collective-permute-start(f32[128,256]{1,0:T(8,128)S(1)} %bitcast.86), channel_id=1, source_target_pairs={{0,32},{32,0},{1,33},{33,1},{2,34},{34,2},{3,35},{35,3},{4,36},{36... | collective-permute-start | bytes 393224 | tf_op jit(solution)/shard_map/ppermute | solution.py:293
  115.1 1.0 collective-permute-done.15.other_ref
  116.0 4.7 %shard_map.43 = f32[128,256]{1,0:T(8,128)} custom-call(s32[18]{0:T(128)S(1)} %concatenate.15.slots_ref, f32[128,256]{1,0:T(8,128)S(1)} %bitcast.87, f32[128,256]{1,0:T(8,128)S(1)} %collective-permute-done.15.other_ref, f32[256,256]{1,0:T(8,128)S(1)} %get-tuple-element.30.inverse_ref, f32[128,256]{1,0:T(8,128)S(1)} %get-tuple-element.31.rows_ref), custom_call_target="tpu_custom_call" | custom-call | flops 10000000000 | bytes 1048576 | tf_op jit(solution)/shard_map/pallas_call | solution.py:281
  (23 shorter events, 0.3 us)
Async XLA Ops:
  13.7 5.6 %collective-permute-start.5 = (f32[4,4,64,256]{3,2,1,0:T(8,128)S(1)}, f32[4,4,64,256]{3,2,1,0:T(8,128)S(1)}, u32[]{:S(2)}, u32[]{:S(2)}) collective-permute-start(f32[4,4,64,256]{3,2,1,0:T(8,128)S(1)} %get-tuple-element.20), channel_id=1, source_target_pairs={{0,32},{32,0},{1,33},{33,1},{2,34},{34,2},{3,35},{35,3},{4,36},{36... | collective-permute-start | bytes 3145736 | tf_op jit(solution)/shard_map/ppermute | solution.py:293
  17.0 4.0 %collective-permute-start = (f32[4,4,72,256]{3,2,1,0:T(8,128)S(1)}, f32[4,4,72,256]{3,2,1,0:T(8,128)S(1)}, u32[]{:S(2)}, u32[]{:S(2)}) collective-permute-start(f32[4,4,72,256]{3,2,1,0:T(8,128)S(1)} %get-tuple-element.18), channel_id=1, source_target_pairs={{0,32},{32,0},{1,33},{33,1},{2,34},{34,2},{3,35},{35,3},{4,36},{36... | collective-permute-start | bytes 3538952 | tf_op jit(solution)/shard_map/ppermute | solution.py:293
  19.4 9.3 %collective-permute-start.6 = (f32[2,4,64,256]{3,2,1,0:T(8,128)S(1)}, f32[2,4,64,256]{3,2,1,0:T(8,128)S(1)}, u32[]{:S(2)}, u32[]{:S(2)}) collective-permute-start(f32[2,4,64,256]{3,2,1,0:T(8,128)S(1)} %slice_add_fusion.1), channel_id=1, source_target_pairs={{0,64},{64,0},{128,192},{192,128},{32,224},{96,160},{160,96},{224,... | collective-permute-start | bytes 1572872 | tf_op jit(solution)/shard_map/ppermute | solution.py:312
  21.1 10.0 %collective-permute-start.1 = (f32[2,4,72,256]{3,2,1,0:T(8,128)S(1)}, f32[2,4,72,256]{3,2,1,0:T(8,128)S(1)}, u32[]{:S(2)}, u32[]{:S(2)}) collective-permute-start(f32[2,4,72,256]{3,2,1,0:T(8,128)S(1)} %slice_add_fusion), channel_id=1, source_target_pairs={{0,8},{8,0},{16,24},{24,16},{32,56},{40,48},{48,40},{56,32},{1,9},... | collective-permute-start | bytes 1769480 | tf_op jit(solution)/shard_map/ppermute | solution.py:310
  28.8 5.6 %collective-permute-start.7 = (f32[4,64,256]{2,1,0:T(8,128)S(1)}, f32[4,64,256]{2,1,0:T(8,128)S(1)}, u32[]{:S(2)}, u32[]{:S(2)}) collective-permute-start(f32[4,64,256]{2,1,0:T(8,128)S(1)} %get-tuple-element.35), channel_id=1, source_target_pairs={{0,192},{64,128},{128,64},{192,0},{32,96},{96,32},{160,224},{224,1... | collective-permute-start | bytes 786440 | tf_op jit(solution)/shard_map/ppermute | solution.py:312
  31.2 6.0 %collective-permute-start.2 = (f32[4,72,256]{2,1,0:T(8,128)S(1)}, f32[4,72,256]{2,1,0:T(8,128)S(1)}, u32[]{:S(2)}, u32[]{:S(2)}) collective-permute-start(f32[4,72,256]{2,1,0:T(8,128)S(1)} %get-tuple-element.33), channel_id=1, source_target_pairs={{0,24},{8,16},{16,8},{24,0},{32,40},{40,32},{48,56},{56,48},{1,25}... | collective-permute-start | bytes 884744 | tf_op jit(solution)/shard_map/ppermute | solution.py:310
  34.4 5.8 %collective-permute-start.8 = (f32[2,64,256]{2,1,0:T(8,128)S(1)}, f32[2,64,256]{2,1,0:T(8,128)S(1)}, u32[]{:S(2)}, u32[]{:S(2)}) collective-permute-start(f32[2,64,256]{2,1,0:T(8,128)S(1)} %slice_add_fusion.10), channel_id=1, source_target_pairs={{0,8},{8,0},{16,24},{24,16},{32,56},{40,48},{48,40},{56,32},{1,9},... | collective-permute-start | bytes 393224 | tf_op jit(solution)/shard_map/ppermute | solution.py:310
  37.2 5.3 %collective-permute-start.3 = (f32[2,72,256]{2,1,0:T(8,128)S(1)}, f32[2,72,256]{2,1,0:T(8,128)S(1)}, u32[]{:S(2)}, u32[]{:S(2)}) collective-permute-start(f32[2,72,256]{2,1,0:T(8,128)S(1)} %slice_add_fusion.8), channel_id=1, source_target_pairs={{0,64},{64,0},{128,192},{192,128},{32,224},{96,160},{160,96},{224,... | collective-permute-start | bytes 442376 | tf_op jit(solution)/shard_map/ppermute | solution.py:312
  40.3 3.5 %collective-permute-start.9 = (f32[64,256]{1,0:T(8,128)S(1)}, f32[64,256]{1,0:T(8,128)S(1)}, u32[]{:S(2)}, u32[]{:S(2)}) collective-permute-start(f32[64,256]{1,0:T(8,128)S(1)} %fusion.11), channel_id=1, source_target_pairs={{0,24},{8,16},{16,8},{24,0},{32,40},{40,32},{48,56},{56,48},{1,25}... | collective-permute-start | bytes 196616 | tf_op jit(solution)/shard_map/ppermute | solution.py:310
  42.5 3.3 %collective-permute-start.4 = (f32[72,256]{1,0:T(8,128)S(1)}, f32[72,256]{1,0:T(8,128)S(1)}, u32[]{:S(2)}, u32[]{:S(2)}) collective-permute-start(f32[72,256]{1,0:T(8,128)S(1)} %fusion.4), channel_id=1, source_target_pairs={{0,192},{64,128},{128,64},{192,0},{32,96},{96,32},{160,224},{224,1... | collective-permute-start | bytes 221192 | tf_op jit(solution)/shard_map/ppermute | solution.py:312
  62.1 7.4 %collective-permute-start.10 = (f32[16,256]{1,0:T(8,128)S(1)}, f32[16,256]{1,0:T(8,128)S(1)}, u32[]{:S(2)}, u32[]{:S(2)}) collective-permute-start(f32[16,256]{1,0:T(8,128)S(1)} %slice.228), channel_id=1, source_target_pairs={{0,32},{32,0},{1,33},{33,1},{2,34},{34,2},{3,35},{35,3},{4,36},{36... | collective-permute-start | bytes 49160 | tf_op jit(solution)/shard_map/ppermute | solution.py:293
  70.8 21.9 %all-to-all-start.1 = ((f32[128,1,512]{2,1,0:T(1,128)}), f32[128,1,512]{2,1,0:T(1,128)S(1)}, u32[]{:S(2)}, u32[]{:S(2)}) async-start(f32[128,1,512]{2,1,0:T(1,128)} %copy.6), calls=%async_computation.1 | async-start | bytes 524288 | tf_op jit(solution)/shard_map/all_to_all | solution.py:301
  78.7 14.2 %collective-permute-start.11 = (f32[32,256]{1,0:T(8,128)S(1)}, f32[32,256]{1,0:T(8,128)S(1)}, u32[]{:S(2)}, u32[]{:S(2)}) collective-permute-start(f32[32,256]{1,0:T(8,128)S(1)} %pad_maximum_fusion.2.part_0), channel_id=1, source_target_pairs={{0,64},{64,0},{128,192},{192,128},{1,65},{65,1},{129,193},{193,129... | collective-permute-start | bytes 98312 | tf_op jit(solution)/shard_map/ppermute | solution.py:297
  79.4 13.4 %collective-permute-start.12 = (f32[32,256]{1,0:T(8,128)S(1)}, f32[32,256]{1,0:T(8,128)S(1)}, u32[]{:S(2)}, u32[]{:S(2)}) collective-permute-start(f32[32,256]{1,0:T(8,128)S(1)} %pad_maximum_fusion.2.part_0), channel_id=1, source_target_pairs={{0,128},{64,192},{128,0},{192,64},{1,129},{65,193},{129,1},{193,65... | collective-permute-start | bytes 98312 | tf_op jit(solution)/shard_map/ppermute | solution.py:297
  82.2 10.6 %collective-permute-start.13 = (f32[32,256]{1,0:T(8,128)S(1)}, f32[32,256]{1,0:T(8,128)S(1)}, u32[]{:S(2)}, u32[]{:S(2)}) collective-permute-start(f32[32,256]{1,0:T(8,128)S(1)} %pad_maximum_fusion.2.part_0), channel_id=1, source_target_pairs={{0,192},{64,128},{128,64},{192,0},{1,193},{65,129},{129,65},{193,1... | collective-permute-start | bytes 98312 | tf_op jit(solution)/shard_map/ppermute | solution.py:297
  92.9 8.9 %collective-permute-start.14 = (f32[128,256]{1,0:T(8,128)S(1)}, f32[128,256]{1,0:T(8,128)S(1)}, u32[]{:S(2)}, u32[]{:S(2)}) collective-permute-start(f32[128,256]{1,0:T(8,128)S(1)} %get-tuple-element.37.mine_ref), channel_id=1, source_target_pairs={{0,32},{32,0},{1,33},{33,1},{2,34},{34,2},{3,35},{35,3},{4,36},{36... | collective-permute-start | bytes 393224 | tf_op jit(solution)/shard_map/ppermute | solution.py:293
  95.6 18.2 %all-to-all-start.2 = ((f32[128,1,256]{2,1,0:T(1,128)}), f32[128,1,256]{2,1,0:T(1,128)S(1)}, u32[]{:S(2)}, u32[]{:S(2)}) async-start(f32[128,1,256]{2,1,0:T(1,128)} %broadcast_in_dim.19), calls=%async_computation.2 | async-start | bytes 262144 | tf_op jit(solution)/shard_map/all_to_all | solution.py:301
  113.8 2.2 %collective-permute-start.15 = (f32[128,256]{1,0:T(8,128)S(1)}, f32[128,256]{1,0:T(8,128)S(1)}, u32[]{:S(2)}, u32[]{:S(2)}) collective-permute-start(f32[128,256]{1,0:T(8,128)S(1)} %bitcast.86), channel_id=1, source_target_pairs={{0,32},{32,0},{1,33},{33,1},{2,34},{34,2},{3,35},{35,3},{4,36},{36... | collective-permute-start | bytes 393224 | tf_op jit(solution)/shard_map/ppermute | solution.py:293

commit v7 on v6

--- a/solution.py
+++ b/solution.py
@@ -317,17 +317,16 @@
     return jnp.where((core == 1) & (apart % 2 == 1), 4 - apart, apart)
 
 
+def by_slot(blocks):
+    return blocks[1:3], blocks[3], blocks[0]
+
+
 def ring_sums(terms_a, terms_b, axis_a, axis_b):
-    def first(terms, slot):
-        return functools.reduce(lambda p, q: p + q, [t[slot] for t in terms])
-
     out = []
-    sent = [sum(t[1:3] for t in terms) for terms in (terms_a, terms_b)]
-    got = [ring_pairs(v, axis, 0) for v, axis in zip(sent, (axis_a, axis_b))]
-    sent = [first(terms, 3) + g[1] for terms, g in zip((terms_a, terms_b), got)]
-    more = [ring_pairs(v, axis, 1) for v, axis in zip(sent, (axis_a, axis_b))]
-    for terms, g, m in zip((terms_a, terms_b), got, more):
-        out.append([first(terms, 0), g[0], m])
+    for terms, axis in ((terms_a, axis_a), (terms_b, axis_b)):
+        middle, third, own = (sum(t[k] for t in terms) for k in range(3))
+        got = ring_pairs(middle, axis, 0)
+        out.append([own, got[0], ring_pairs(third + got[1], axis, 1)])
     return out
 
 
@@ -345,8 +344,13 @@
         [core] + [ring_slots(k, at) for at in (y, x) for k in (c, 1 - c)] + [x.reshape(1)]
     )
     sketch, keep_a, keep_b, send_a, send_b = products(slots, embeddings, sketch_matrix)
-    got_a, got_b = to_core(send_a), to_core(send_b)
-    line_a, line_b = ring_sums([keep_a, got_a], [keep_b, got_b], "y", "x")
+    terms = []
+    for keep, send in ((keep_a, send_a), (keep_b, send_b)):
+        middle, third, own = by_slot(send)
+        rest = to_core(jnp.stack([third, own]))
+        terms.append([by_slot(keep), (to_core(middle), rest[0], rest[1])])
+    line_a, line_b = ring_sums(*terms, "y", "x")
+    line_a, line_b = ([by_slot(v) for v in line] for line in (line_a, line_b))
     own_a, own_b = ring_sums(line_a, line_b, "x", "y")
     own_a, own_b = sum(own_a), sum(own_b)
     size = own_b.shape[0]

time: 121 us -> 120 us (level)
  waiting for transfers between devices: 38.6 us -> 36.4 us
    ppermute x5 -> x7, waiting for transfers between devices: 4.78 us -> 3.03 us  [to_core(): return lax.ppermute(block, 'c', [(0, 1), (1, 0)])]
    ppermute x5 -> x7, starting transfers between devices: 13.2 us -> 14.1 us  [to_core(): return lax.ppermute(block, 'c', [(0, 1), (1, 0)])]
  transfers between devices with their start and end apart: 18 -> 20, of which waited for: 14 -> 14; matrix products, arithmetic and copies ran while one was open for 1% -> 1% of each run, Pallas kernels for 7% -> 7%
where the time goes in v7:
time: 120 us
  starting transfers between devices  37.7 us (31%)
  waiting for transfers between devices  36.4 us (30%)
  Pallas kernels  25.7 us (21%)
  blocking collectives  16.3 us (14%)
  local copies, waits for them, and re-layouts  1.99 us (2%)
    all_to_all x1, blocking collectives, exchange(): return lax.all_to_all(blocks, axes, 0, 0, tiled=True)  16.3 us
    ppermute x7, starting transfers between devices, to_core(): return lax.ppermute(block, 'c', [(0, 1), (1, 0)])  14.1 us
    all_to_all x2, waiting for transfers between devices, exchange(): return lax.all_to_all(blocks, axes, 0, 0, tiled=True)  14 us
    all_to_all x2, starting transfers between devices, exchange(): return lax.all_to_all(blocks, axes, 0, 0, tiled=True)  13.9 us
    pallas_call x1, Pallas kernels, products(): pl.pallas_call(products_kernel, grid_spec=pltpu.PrefetchScalarGridSpec(nu...  12.9 us
    ppermute x4, waiting for transfers between devices, ring_pairs(): return lax.ppermute(block, ('x', 'c'), pairs)  12.9 us
    pallas_call x1, Pallas kernels, basis(): pl.pallas_call(functools.partial(basis_kernel, scale), out_shape=(jax.Sha...  8.04 us
    ppermute x4, waiting for transfers between devices, ring_pairs(): return lax.ppermute(block, ('c', 'y'), pairs)  6.55 us
  transfers between devices with their start and end apart: 20, of which 14 were waited for; matrix products, arithmetic and copies ran while one was open for 1% of the time, Pallas kernels for 7%

profile of v7, /device:TPU:1, one launch (start us, length us, event | category | flops | bytes accessed | tf_op | source)
XLA Modules:
  0.0 120.0 jit_solution(17461082296762413640)
XLA Ops:
  0.7 0.1 concatenate.15.slots_ref
  0.8 12.9 %shard_map.41 = (f32[512,256]{1,0:T(8,128)S(1)}, f32[4,4,72,256]{3,2,1,0:T(8,128)S(1)}, f32[4,4,64,256]{3,2,1,0:T(8,128)S(1)}, f32[4,4,72,256]{3,2,1,0:T(8,128)S(1)}, f32[4,4,64,256]{3,2,1,0:T(8,128)S(1)}) custom-call(s32[18]{0:T(128)S(1)} %concatenate.15.slots_ref, f32[512,4096]{1,0:T(8,128)} %emb_ref.1, f32[4096,256]{1,0:T(8,128)} %matrix_ref.1), custom_call_target="tpu_custom_call" | custom-call | flops 6442450944 | bytes 25165824 | tf_op jit(solution)/shard_map/pallas_call | solution.py:124
  13.7 3.3 %collective-permute-start.7 = (f32[2,4,64,256]{3,2,1,0:T(8,128)S(1)}, f32[2,4,64,256]{3,2,1,0:T(8,128)S(1)}, u32[]{:S(2)}, u32[]{:S(2)}) collective-permute-start(f32[2,4,64,256]{3,2,1,0:T(8,128)S(1)} %slice.191), channel_id=1, source_target_pairs={{0,32},{32,0},{1,33},{33,1},{2,34},{34,2},{3,35},{35,3},{4,36},{36... | collective-permute-start | bytes 1572872 | tf_op jit(solution)/shard_map/ppermute | solution.py:293
  17.1 0.1 collective-permute-start.6
  17.3 0.6 collective-permute-start.1
  18.0 0.1 collective-permute-start
  18.1 0.5 collective-permute-done.7
  18.6 0.1 slice_add_fusion.1
  18.7 0.8 collective-permute-start.8
  19.5 0.7 collective-permute-done.1
  20.2 0.1 slice_add_fusion
  20.3 2.1 %collective-permute-start.2 = (f32[2,4,72,256]{3,2,1,0:T(8,128)S(1)}, f32[2,4,72,256]{3,2,1,0:T(8,128)S(1)}, u32[]{:S(2)}, u32[]{:S(2)}) collective-permute-start(f32[2,4,72,256]{3,2,1,0:T(8,128)S(1)} %slice_add_fusion), channel_id=1, source_target_pairs={{0,8},{8,0},{16,24},{24,16},{32,56},{40,48},{48,40},{56,32},{1,9},... | collective-permute-start | bytes 1769480 | tf_op jit(solution)/shard_map/ppermute | solution.py:310
  22.4 0.0 collective-permute-done.6
  22.4 5.6 %collective-permute-done.8 = f32[2,4,64,256]{3,2,1,0:T(8,128)S(1)} collective-permute-done((f32[2,4,64,256]{3,2,1,0:T(8,128)S(1)}, f32[2,4,64,256]{3,2,1,0:T(8,128)S(1)}, u32[]{:S(2)}, u32[]{:S(2)}) %collective-permute-start.8) | collective-permute-done | bytes 524320 | tf_op jit(solution)/shard_map/ppermute | solution.py:312
  28.0 0.1 slice_add_fusion.7
  28.1 0.1 collective-permute-start.9
  28.2 2.1 %collective-permute-done.2 = f32[2,4,72,256]{3,2,1,0:T(8,128)S(1)} collective-permute-done((f32[2,4,72,256]{3,2,1,0:T(8,128)S(1)}, f32[2,4,72,256]{3,2,1,0:T(8,128)S(1)}, u32[]{:S(2)}, u32[]{:S(2)}) %collective-permute-start.2) | collective-permute-done | bytes 589856 | tf_op jit(solution)/shard_map/ppermute | solution.py:310
  30.3 0.1 slice_add_fusion.4
  30.4 0.1 collective-permute-start.3
  30.5 3.2 %collective-permute-done.9 = f32[4,64,256]{2,1,0:T(8,128)S(1)} collective-permute-done((f32[4,64,256]{2,1,0:T(8,128)S(1)}, f32[4,64,256]{2,1,0:T(8,128)S(1)}, u32[]{:S(2)}, u32[]{:S(2)}) %collective-permute-start.9) | collective-permute-done | bytes 262176 | tf_op jit(solution)/shard_map/ppermute | solution.py:312
  33.7 1.1 collective-permute-start.10
  34.8 1.6 %collective-permute-done.3 = f32[4,72,256]{2,1,0:T(8,128)S(1)} collective-permute-done((f32[4,72,256]{2,1,0:T(8,128)S(1)}, f32[4,72,256]{2,1,0:T(8,128)S(1)}, u32[]{:S(2)}, u32[]{:S(2)}) %collective-permute-start.3) | collective-permute-done | bytes 294944 | tf_op jit(solution)/shard_map/ppermute | solution.py:310
  36.4 1.3 %collective-permute-start.4 = (f32[2,72,256]{2,1,0:T(8,128)S(1)}, f32[2,72,256]{2,1,0:T(8,128)S(1)}, u32[]{:S(2)}, u32[]{:S(2)}) collective-permute-start(f32[2,72,256]{2,1,0:T(8,128)S(1)} %slice_add_fusion.8), channel_id=1, source_target_pairs={{0,64},{64,0},{128,192},{192,128},{32,224},{96,160},{160,96},{224,... | collective-permute-start | bytes 442376 | tf_op jit(solution)/shard_map/ppermute | solution.py:312
  37.7 1.7 %collective-permute-done.10 = f32[2,64,256]{2,1,0:T(8,128)S(1)} collective-permute-done((f32[2,64,256]{2,1,0:T(8,128)S(1)}, f32[2,64,256]{2,1,0:T(8,128)S(1)}, u32[]{:S(2)}, u32[]{:S(2)}) %collective-permute-start.10) | collective-permute-done | bytes 131104 | tf_op jit(solution)/shard_map/ppermute | solution.py:310
  39.5 0.1 collective-permute-start.11
  39.6 2.1 %collective-permute-done.4 = f32[2,72,256]{2,1,0:T(8,128)S(1)} collective-permute-done((f32[2,72,256]{2,1,0:T(8,128)S(1)}, f32[2,72,256]{2,1,0:T(8,128)S(1)}, u32[]{:S(2)}, u32[]{:S(2)}) %collective-permute-start.4) | collective-permute-done | bytes 147488 | tf_op jit(solution)/shard_map/ppermute | solution.py:312
  41.7 0.1 collective-permute-start.5
  41.8 1.2 collective-permute-done.11
  43.0 2.0 %collective-permute-done.5 = f32[72,256]{1,0:T(8,128)S(1)} collective-permute-done((f32[72,256]{1,0:T(8,128)S(1)}, f32[72,256]{1,0:T(8,128)S(1)}, u32[]{:S(2)}, u32[]{:S(2)}) %collective-permute-start.5) | collective-permute-done | bytes 73760 | tf_op jit(solution)/shard_map/ppermute | solution.py:312
  45.1 16.3 %all_to_all.26 = f32[8,17,256]{2,1,0:T(8,128)S(1)} all-to-all(f32[8,17,256]{2,1,0:T(8,128)S(1)} %pad_maximum_fusion.2), channel_id=1, replica_groups=mesh['x'=4,'c'=2,'y'=4,'z'=8] {'z'}, dimensions={0} | all-to-all | bytes 278528 | tf_op jit(solution)/shard_map/all_to_all | solution.py:301
  61.4 6.7 %collective-permute-start.12 = (f32[16,256]{1,0:T(8,128)S(1)}, f32[16,256]{1,0:T(8,128)S(1)}, u32[]{:S(2)}, u32[]{:S(2)}) collective-permute-start(f32[16,256]{1,0:T(8,128)S(1)} %slice.242), channel_id=1, source_target_pairs={{0,32},{32,0},{1,33},{33,1},{2,34},{34,2},{3,35},{35,3},{4,36},{36... | collective-permute-start | bytes 49160 | tf_op jit(solution)/shard_map/ppermute | solution.py:293
  68.2 0.8 collective-permute-done.12
  69.0 0.3 fusion.20
  69.3 1.0 copy.6
  70.3 7.5 %all-to-all-start.1 = ((f32[128,1,512]{2,1,0:T(1,128)}), f32[128,1,512]{2,1,0:T(1,128)S(1)}, u32[]{:S(2)}, u32[]{:S(2)}) async-start(f32[128,1,512]{2,1,0:T(1,128)} %copy.6), calls=%async_computation.1 | async-start | bytes 524288 | tf_op jit(solution)/shard_map/all_to_all | solution.py:301
  77.9 0.8 collective-permute-start.13
  78.6 2.8 %collective-permute-start.14 = (f32[32,256]{1,0:T(8,128)S(1)}, f32[32,256]{1,0:T(8,128)S(1)}, u32[]{:S(2)}, u32[]{:S(2)}) collective-permute-start(f32[32,256]{1,0:T(8,128)S(1)} %pad_maximum_fusion.4.part_0), channel_id=1, source_target_pairs={{0,128},{64,192},{128,0},{192,64},{1,129},{65,193},{129,1},{193,65... | collective-permute-start | bytes 98312 | tf_op jit(solution)/shard_map/ppermute | solution.py:297
  81.5 0.4 collective-permute-start.15
  81.8 10.2 %all-to-all-done.1 = f32[128,1,512]{2,1,0:T(1,128)S(1)} async-done(((f32[128,1,512]{2,1,0:T(1,128)}), f32[128,1,512]{2,1,0:T(1,128)S(1)}, u32[]{:S(2)}, u32[]{:S(2)}) %all-to-all-start.1) | async-done | bytes 262176 | tf_op jit(solution)/shard_map/all_to_all | solution.py:301
  92.0 0.0 collective-permute-done.13.part_1
  92.1 2.0 %collective-permute-start.16 = (f32[128,256]{1,0:T(8,128)S(1)}, f32[128,256]{1,0:T(8,128)S(1)}, u32[]{:S(2)}, u32[]{:S(2)}) collective-permute-start(f32[128,256]{1,0:T(8,128)S(1)} %get-tuple-element.41.mine_ref), channel_id=1, source_target_pairs={{0,32},{32,0},{1,33},{33,1},{2,34},{34,2},{3,35},{35,3},{4,36},{36... | collective-permute-start | bytes 393224 | tf_op jit(solution)/shard_map/ppermute | solution.py:293
  94.1 0.7 broadcast_in_dim.19
  94.8 6.4 %all-to-all-start.2 = ((f32[128,1,256]{2,1,0:T(1,128)}), f32[128,1,256]{2,1,0:T(1,128)S(1)}, u32[]{:S(2)}, u32[]{:S(2)}) async-start(f32[128,1,256]{2,1,0:T(1,128)} %broadcast_in_dim.19), calls=%async_computation.2 | async-start | bytes 262144 | tf_op jit(solution)/shard_map/all_to_all | solution.py:301
  101.2 8.0 %shard_map.42 = (f32[256,256]{1,0:T(8,128)S(1)}, f32[512,256]{1,0:T(8,128)}, f32[128,256]{1,0:T(8,128)S(1)}) custom-call(s32[18]{0:T(128)S(1)} %concatenate.15.slots_ref, f32[128,256]{1,0:T(8,128)S(1)} %get-tuple-element.41.mine_ref, f32[128,256]{1,0:T(8,128)S(1)} %collective-permute-done.16.other_ref, f32[512,256]{1,0:T(8,128)S(1)} %get-tuple-element.22.sketch_ref, ...), custom_call_target="tpu_custom_call" | custom-call | flops 10000000000 | bytes 2097152 | tf_op jit(solution)/shard_map/pallas_call | solution.py:240
  109.2 3.8 %all-to-all-done.2 = f32[128,1,256]{2,1,0:T(1,128)S(1)} async-done(((f32[128,1,256]{2,1,0:T(1,128)}), f32[128,1,256]{2,1,0:T(1,128)S(1)}, u32[]{:S(2)}, u32[]{:S(2)}) %all-to-all-start.2) | async-done | bytes 131104 | tf_op jit(solution)/shard_map/all_to_all | solution.py:301
  113.0 1.2 %collective-permute-start.17 = (f32[128,256]{1,0:T(8,128)S(1)}, f32[128,256]{1,0:T(8,128)S(1)}, u32[]{:S(2)}, u32[]{:S(2)}) collective-permute-start(f32[128,256]{1,0:T(8,128)S(1)} %bitcast.86), channel_id=1, source_target_pairs={{0,32},{32,0},{1,33},{33,1},{2,34},{34,2},{3,35},{35,3},{4,36},{36... | collective-permute-start | bytes 393224 | tf_op jit(solution)/shard_map/ppermute | solution.py:293
  114.3 1.0 collective-permute-done.17.other_ref
  115.3 4.7 %shard_map.43 = f32[128,256]{1,0:T(8,128)} custom-call(s32[18]{0:T(128)S(1)} %concatenate.15.slots_ref, f32[128,256]{1,0:T(8,128)S(1)} %bitcast.87, f32[128,256]{1,0:T(8,128)S(1)} %collective-permute-done.17.other_ref, f32[256,256]{1,0:T(8,128)S(1)} %get-tuple-element.30.inverse_ref, f32[128,256]{1,0:T(8,128)S(1)} %get-tuple-element.31.rows_ref), custom_call_target="tpu_custom_call" | custom-call | flops 10000000000 | bytes 1048576 | tf_op jit(solution)/shard_map/pallas_call | solution.py:281
  (33 shorter events, 0.6 us)
Async XLA Ops:
  13.7 4.9 %collective-permute-start.7 = (f32[2,4,64,256]{3,2,1,0:T(8,128)S(1)}, f32[2,4,64,256]{3,2,1,0:T(8,128)S(1)}, u32[]{:S(2)}, u32[]{:S(2)}) collective-permute-start(f32[2,4,64,256]{3,2,1,0:T(8,128)S(1)} %slice.191), channel_id=1, source_target_pairs={{0,32},{32,0},{1,33},{33,1},{2,34},{34,2},{3,35},{35,3},{4,36},{36... | collective-permute-start | bytes 1572872 | tf_op jit(solution)/shard_map/ppermute | solution.py:293
  17.1 5.3 %collective-permute-start.6 = (f32[2,4,64,256]{3,2,1,0:T(8,128)S(1)}, f32[2,4,64,256]{3,2,1,0:T(8,128)S(1)}, u32[]{:S(2)}, u32[]{:S(2)}) collective-permute-start(f32[2,4,64,256]{3,2,1,0:T(8,128)S(1)} %pad_maximum_fusion.1), channel_id=1, source_target_pairs={{0,32},{32,0},{1,33},{33,1},{2,34},{34,2},{3,35},{35,3},{4,36},{36... | collective-permute-start | bytes 1572872 | tf_op jit(solution)/shard_map/ppermute | solution.py:293
  17.3 2.9 %collective-permute-start.1 = (f32[2,4,72,256]{3,2,1,0:T(8,128)S(1)}, f32[2,4,72,256]{3,2,1,0:T(8,128)S(1)}, u32[]{:S(2)}, u32[]{:S(2)}) collective-permute-start(f32[2,4,72,256]{3,2,1,0:T(8,128)S(1)} %slice.170), channel_id=1, source_target_pairs={{0,32},{32,0},{1,33},{33,1},{2,34},{34,2},{3,35},{35,3},{4,36},{36... | collective-permute-start | bytes 1769480 | tf_op jit(solution)/shard_map/ppermute | solution.py:293
  18.0 10.2 %collective-permute-start = (f32[2,4,72,256]{3,2,1,0:T(8,128)S(1)}, f32[2,4,72,256]{3,2,1,0:T(8,128)S(1)}, u32[]{:S(2)}, u32[]{:S(2)}) collective-permute-start(f32[2,4,72,256]{3,2,1,0:T(8,128)S(1)} %pad_maximum_fusion), channel_id=1, source_target_pairs={{0,32},{32,0},{1,33},{33,1},{2,34},{34,2},{3,35},{35,3},{4,36},{36... | collective-permute-start | bytes 1769480 | tf_op jit(solution)/shard_map/ppermute | solution.py:293
  18.7 9.3 %collective-permute-start.8 = (f32[2,4,64,256]{3,2,1,0:T(8,128)S(1)}, f32[2,4,64,256]{3,2,1,0:T(8,128)S(1)}, u32[]{:S(2)}, u32[]{:S(2)}) collective-permute-start(f32[2,4,64,256]{3,2,1,0:T(8,128)S(1)} %slice_add_fusion.1), channel_id=1, source_target_pairs={{0,64},{64,0},{128,192},{192,128},{32,224},{96,160},{160,96},{224,... | collective-permute-start | bytes 1572872 | tf_op jit(solution)/shard_map/ppermute | solution.py:312
  20.3 10.0 %collective-permute-start.2 = (f32[2,4,72,256]{3,2,1,0:T(8,128)S(1)}, f32[2,4,72,256]{3,2,1,0:T(8,128)S(1)}, u32[]{:S(2)}, u32[]{:S(2)}) collective-permute-start(f32[2,4,72,256]{3,2,1,0:T(8,128)S(1)} %slice_add_fusion), channel_id=1, source_target_pairs={{0,8},{8,0},{16,24},{24,16},{32,56},{40,48},{48,40},{56,32},{1,9},... | collective-permute-start | bytes 1769480 | tf_op jit(solution)/shard_map/ppermute | solution.py:310
  28.1 5.6 %collective-permute-start.9 = (f32[4,64,256]{2,1,0:T(8,128)S(1)}, f32[4,64,256]{2,1,0:T(8,128)S(1)}, u32[]{:S(2)}, u32[]{:S(2)}) collective-permute-start(f32[4,64,256]{2,1,0:T(8,128)S(1)} %get-tuple-element.35), channel_id=1, source_target_pairs={{0,192},{64,128},{128,64},{192,0},{32,96},{96,32},{160,224},{224,1... | collective-permute-start | bytes 786440 | tf_op jit(solution)/shard_map/ppermute | solution.py:312
  30.4 6.0 %collective-permute-start.3 = (f32[4,72,256]{2,1,0:T(8,128)S(1)}, f32[4,72,256]{2,1,0:T(8,128)S(1)}, u32[]{:S(2)}, u32[]{:S(2)}) collective-permute-start(f32[4,72,256]{2,1,0:T(8,128)S(1)} %get-tuple-element.33), channel_id=1, source_target_pairs={{0,24},{8,16},{16,8},{24,0},{32,40},{40,32},{48,56},{56,48},{1,25}... | collective-permute-start | bytes 884744 | tf_op jit(solution)/shard_map/ppermute | solution.py:310
  33.7 5.7 %collective-permute-start.10 = (f32[2,64,256]{2,1,0:T(8,128)S(1)}, f32[2,64,256]{2,1,0:T(8,128)S(1)}, u32[]{:S(2)}, u32[]{:S(2)}) collective-permute-start(f32[2,64,256]{2,1,0:T(8,128)S(1)} %slice_add_fusion.10), channel_id=1, source_target_pairs={{0,8},{8,0},{16,24},{24,16},{32,56},{40,48},{48,40},{56,32},{1,9},... | collective-permute-start | bytes 393224 | tf_op jit(solution)/shard_map/ppermute | solution.py:310
  36.4 5.3 %collective-permute-start.4 = (f32[2,72,256]{2,1,0:T(8,128)S(1)}, f32[2,72,256]{2,1,0:T(8,128)S(1)}, u32[]{:S(2)}, u32[]{:S(2)}) collective-permute-start(f32[2,72,256]{2,1,0:T(8,128)S(1)} %slice_add_fusion.8), channel_id=1, source_target_pairs={{0,64},{64,0},{128,192},{192,128},{32,224},{96,160},{160,96},{224,... | collective-permute-start | bytes 442376 | tf_op jit(solution)/shard_map/ppermute | solution.py:312
  39.5 3.5 %collective-permute-start.11 = (f32[64,256]{1,0:T(8,128)S(1)}, f32[64,256]{1,0:T(8,128)S(1)}, u32[]{:S(2)}, u32[]{:S(2)}) collective-permute-start(f32[64,256]{1,0:T(8,128)S(1)} %fusion.11), channel_id=1, source_target_pairs={{0,24},{8,16},{16,8},{24,0},{32,40},{40,32},{48,56},{56,48},{1,25}... | collective-permute-start | bytes 196616 | tf_op jit(solution)/shard_map/ppermute | solution.py:310
  41.7 3.3 %collective-permute-start.5 = (f32[72,256]{1,0:T(8,128)S(1)}, f32[72,256]{1,0:T(8,128)S(1)}, u32[]{:S(2)}, u32[]{:S(2)}) collective-permute-start(f32[72,256]{1,0:T(8,128)S(1)} %fusion.4), channel_id=1, source_target_pairs={{0,192},{64,128},{128,64},{192,0},{32,96},{96,32},{160,224},{224,1... | collective-permute-start | bytes 221192 | tf_op jit(solution)/shard_map/ppermute | solution.py:312
  61.4 7.6 %collective-permute-start.12 = (f32[16,256]{1,0:T(8,128)S(1)}, f32[16,256]{1,0:T(8,128)S(1)}, u32[]{:S(2)}, u32[]{:S(2)}) collective-permute-start(f32[16,256]{1,0:T(8,128)S(1)} %slice.242), channel_id=1, source_target_pairs={{0,32},{32,0},{1,33},{33,1},{2,34},{34,2},{3,35},{35,3},{4,36},{36... | collective-permute-start | bytes 49160 | tf_op jit(solution)/shard_map/ppermute | solution.py:293
  70.3 21.7 %all-to-all-start.1 = ((f32[128,1,512]{2,1,0:T(1,128)}), f32[128,1,512]{2,1,0:T(1,128)S(1)}, u32[]{:S(2)}, u32[]{:S(2)}) async-start(f32[128,1,512]{2,1,0:T(1,128)} %copy.6), calls=%async_computation.1 | async-start | bytes 524288 | tf_op jit(solution)/shard_map/all_to_all | solution.py:301
  77.9 14.2 %collective-permute-start.13 = (f32[32,256]{1,0:T(8,128)S(1)}, f32[32,256]{1,0:T(8,128)S(1)}, u32[]{:S(2)}, u32[]{:S(2)}) collective-permute-start(f32[32,256]{1,0:T(8,128)S(1)} %pad_maximum_fusion.4.part_0), channel_id=1, source_target_pairs={{0,64},{64,0},{128,192},{192,128},{1,65},{65,1},{129,193},{193,129... | collective-permute-start | bytes 98312 | tf_op jit(solution)/shard_map/ppermute | solution.py:297
  78.6 13.4 %collective-permute-start.14 = (f32[32,256]{1,0:T(8,128)S(1)}, f32[32,256]{1,0:T(8,128)S(1)}, u32[]{:S(2)}, u32[]{:S(2)}) collective-permute-start(f32[32,256]{1,0:T(8,128)S(1)} %pad_maximum_fusion.4.part_0), channel_id=1, source_target_pairs={{0,128},{64,192},{128,0},{192,64},{1,129},{65,193},{129,1},{193,65... | collective-permute-start | bytes 98312 | tf_op jit(solution)/shard_map/ppermute | solution.py:297
  81.5 10.6 %collective-permute-start.15 = (f32[32,256]{1,0:T(8,128)S(1)}, f32[32,256]{1,0:T(8,128)S(1)}, u32[]{:S(2)}, u32[]{:S(2)}) collective-permute-start(f32[32,256]{1,0:T(8,128)S(1)} %pad_maximum_fusion.4.part_0), channel_id=1, source_target_pairs={{0,192},{64,128},{128,64},{192,0},{1,193},{65,129},{129,65},{193,1... | collective-permute-start | bytes 98312 | tf_op jit(solution)/shard_map/ppermute | solution.py:297
  92.1 9.1 %collective-permute-start.16 = (f32[128,256]{1,0:T(8,128)S(1)}, f32[128,256]{1,0:T(8,128)S(1)}, u32[]{:S(2)}, u32[]{:S(2)}) collective-permute-start(f32[128,256]{1,0:T(8,128)S(1)} %get-tuple-element.41.mine_ref), channel_id=1, source_target_pairs={{0,32},{32,0},{1,33},{33,1},{2,34},{34,2},{3,35},{35,3},{4,36},{36... | collective-permute-start | bytes 393224 | tf_op jit(solution)/shard_map/ppermute | solution.py:293
  94.8 18.2 %all-to-all-start.2 = ((f32[128,1,256]{2,1,0:T(1,128)}), f32[128,1,256]{2,1,0:T(1,128)S(1)}, u32[]{:S(2)}, u32[]{:S(2)}) async-start(f32[128,1,256]{2,1,0:T(1,128)} %broadcast_in_dim.19), calls=%async_computation.2 | async-start | bytes 262144 | tf_op jit(solution)/shard_map/all_to_all | solution.py:301
  113.0 2.2 %collective-permute-start.17 = (f32[128,256]{1,0:T(8,128)S(1)}, f32[128,256]{1,0:T(8,128)S(1)}, u32[]{:S(2)}, u32[]{:S(2)}) collective-permute-start(f32[128,256]{1,0:T(8,128)S(1)} %bitcast.86), channel_id=1, source_target_pairs={{0,32},{32,0},{1,33},{33,1},{2,34},{34,2},{3,35},{35,3},{4,36},{36... | collective-permute-start | bytes 393224 | tf_op jit(solution)/shard_map/ppermute | solution.py:293

commit v8 on v7

--- a/solution.py
+++ b/solution.py
@@ -321,12 +321,17 @@
     return blocks[1:3], blocks[3], blocks[0]
 
 
-def ring_sums(terms_a, terms_b, axis_a, axis_b):
+def ring_sums(terms_a, terms_b, axis_a, axis_b, apart=False):
     out = []
     for terms, axis in ((terms_a, axis_a), (terms_b, axis_b)):
         middle, third, own = (sum(t[k] for t in terms) for k in range(3))
-        got = ring_pairs(middle, axis, 0)
-        out.append([own, got[0], ring_pairs(third + got[1], axis, 1)])
+        if apart:
+            far = ring_pairs(middle[1], axis, 0)
+            far, near = lax.optimization_barrier((far, middle[0]))
+            near = ring_pairs(near, axis, 0)
+        else:
+            near, far = ring_pairs(middle, axis, 0)
+        out.append([own, near, ring_pairs(third + far, axis, 1)])
     return out
 
 
@@ -349,7 +354,7 @@
         middle, third, own = by_slot(send)
         rest = to_core(jnp.stack([third, own]))
         terms.append([by_slot(keep), (to_core(middle), rest[0], rest[1])])
-    line_a, line_b = ring_sums(*terms, "y", "x")
+    line_a, line_b = ring_sums(*terms, "y", "x", apart=True)
     line_a, line_b = ([by_slot(v) for v in line] for line in (line_a, line_b))
     own_a, own_b = ring_sums(line_a, line_b, "x", "y")
     own_a, own_b = sum(own_a), sum(own_b)

time: 120 us -> 119 us (level)
  waiting for transfers between devices: 36.4 us -> 34.2 us
    ppermute x7, starting transfers between devices: 14.1 us -> 11.1 us  [to_core(): return lax.ppermute(block, 'c', [(0, 1), (1, 0)])]
    ppermute x4 -> x5, waiting for transfers between devices: 6.55 us -> 3.87 us  [ring_pairs(): return lax.ppermute(block, ('c', 'y'), pairs)]
    ppermute x4 -> x5, starting transfers between devices: 3.4 us -> 5.53 us  [ring_pairs(): return lax.ppermute(block, ('c', 'y'), pairs)]
    ppermute x4 -> x5, starting transfers between devices: 2.35 us -> 3.18 us  [ring_pairs(): return lax.ppermute(block, ('x', 'c'), pairs)]
    ppermute x4 -> x5, waiting for transfers between devices: 12.9 us -> 13.4 us  [ring_pairs(): return lax.ppermute(block, ('x', 'c'), pairs)]
  transfers between devices with their start and end apart: 20 -> 22, of which waited for: 14 -> 14; matrix products, arithmetic and copies ran while one was open for 1% -> 1% of each run, Pallas kernels for 7% -> 7%
where the time goes in v8:
time: 119 us; the launch traced here: 118 us
  starting transfers between devices  37.5 us (32%)
  waiting for transfers between devices  34.2 us (29%)
  Pallas kernels  25.7 us (22%)
  blocking collectives  17 us (14%)
  local copies, waits for them, and re-layouts  2.07 us (2%)
    all_to_all x1, blocking collectives, exchange(): return lax.all_to_all(blocks, axes, 0, 0, tiled=True)  17 us
    all_to_all x2, waiting for transfers between devices, exchange(): return lax.all_to_all(blocks, axes, 0, 0, tiled=True)  13.9 us
    all_to_all x2, starting transfers between devices, exchange(): return lax.all_to_all(blocks, axes, 0, 0, tiled=True)  13.7 us
    ppermute x5, waiting for transfers between devices, ring_pairs(): return lax.ppermute(block, ('x', 'c'), pairs)  13.4 us
    pallas_call x1, Pallas kernels, products(): pl.pallas_call(products_kernel, grid_spec=pltpu.PrefetchScalarGridSpec(nu...  12.9 us
    ppermute x7, starting transfers between devices, to_core(): return lax.ppermute(block, 'c', [(0, 1), (1, 0)])  11.1 us
    pallas_call x1, Pallas kernels, basis(): pl.pallas_call(functools.partial(basis_kernel, scale), out_shape=(jax.Sha...  8.05 us
    ppermute x5, starting transfers between devices, ring_pairs(): return lax.ppermute(block, ('c', 'y'), pairs)  5.53 us
  transfers between devices with their start and end apart: 22, of which 14 were waited for; matrix products, arithmetic and copies ran while one was open for 1% of the time, Pallas kernels for 7%

profile of v8, /device:TPU:1, one launch (start us, length us, event | category | flops | bytes accessed | tf_op | source)
XLA Modules:
  0.0 118.4 jit_solution(8528065279308487049)
XLA Ops:
  0.7 0.1 concatenate.15.slots_ref
  0.8 12.9 %shard_map.41 = (f32[512,256]{1,0:T(8,128)S(1)}, f32[4,4,72,256]{3,2,1,0:T(8,128)S(1)}, f32[4,4,64,256]{3,2,1,0:T(8,128)S(1)}, f32[4,4,72,256]{3,2,1,0:T(8,128)S(1)}, f32[4,4,64,256]{3,2,1,0:T(8,128)S(1)}) custom-call(s32[18]{0:T(128)S(1)} %concatenate.15.slots_ref, f32[512,4096]{1,0:T(8,128)} %emb_ref.1, f32[4096,256]{1,0:T(8,128)} %matrix_ref.1), custom_call_target="tpu_custom_call" | custom-call | flops 6442450944 | bytes 25165824 | tf_op jit(solution)/shard_map/pallas_call | solution.py:124
  13.7 3.3 %collective-permute-start.8 = (f32[2,4,64,256]{3,2,1,0:T(8,128)S(1)}, f32[2,4,64,256]{3,2,1,0:T(8,128)S(1)}, u32[]{:S(2)}, u32[]{:S(2)}) collective-permute-start(f32[2,4,64,256]{3,2,1,0:T(8,128)S(1)} %slice.186), channel_id=1, source_target_pairs={{0,32},{32,0},{1,33},{33,1},{2,34},{34,2},{3,35},{35,3},{4,36},{36... | collective-permute-start | bytes 1572872 | tf_op jit(solution)/shard_map/ppermute | solution.py:293
  17.1 0.1 collective-permute-start.7
  17.3 0.6 collective-permute-start.1
  18.0 0.1 collective-permute-start
  18.1 0.5 collective-permute-done.8
  18.6 0.1 slice_add_fusion.1
  18.7 0.8 collective-permute-start.9
  19.6 0.6 collective-permute-done.1
  20.2 0.1 slice_add_fusion
  20.3 2.2 %collective-permute-start.2 = (f32[4,72,256]{2,1,0:T(8,128)S(1)}, f32[4,72,256]{2,1,0:T(8,128)S(1)}, u32[]{:S(2)}, u32[]{:S(2)}) collective-permute-start(f32[4,72,256]{2,1,0:T(8,128)S(1)} %get-tuple-element.45), channel_id=1, source_target_pairs={{0,8},{8,0},{16,24},{24,16},{32,56},{40,48},{48,40},{56,32},{1,9},... | collective-permute-start | bytes 884744 | tf_op jit(solution)/shard_map/ppermute | solution.py:310
  22.5 2.7 %collective-permute-done.9 = f32[4,64,256]{2,1,0:T(8,128)S(1)} collective-permute-done((f32[4,64,256]{2,1,0:T(8,128)S(1)}, f32[4,64,256]{2,1,0:T(8,128)S(1)}, u32[]{:S(2)}, u32[]{:S(2)}) %collective-permute-start.9) | collective-permute-done | bytes 262176 | tf_op jit(solution)/shard_map/ppermute | solution.py:312
  25.2 0.8 collective-permute-start.10
  26.0 0.1 fusion.3
  26.0 0.1 collective-permute-start.11
  26.1 1.0 collective-permute-done.2
  27.2 2.1 %collective-permute-start.3 = (f32[4,72,256]{2,1,0:T(8,128)S(1)}, f32[4,72,256]{2,1,0:T(8,128)S(1)}, u32[]{:S(2)}, u32[]{:S(2)}) collective-permute-start(f32[4,72,256]{2,1,0:T(8,128)S(1)} %get-tuple-element.23), channel_id=1, source_target_pairs={{0,8},{8,0},{16,24},{24,16},{32,56},{40,48},{48,40},{56,32},{1,9},... | collective-permute-start | bytes 884744 | tf_op jit(solution)/shard_map/ppermute | solution.py:310
  29.3 0.1 fusion.1
  29.3 0.1 collective-permute-start.4
  29.5 4.3 %collective-permute-done.10 = f32[4,64,256]{2,1,0:T(8,128)S(1)} collective-permute-done((f32[4,64,256]{2,1,0:T(8,128)S(1)}, f32[4,64,256]{2,1,0:T(8,128)S(1)}, u32[]{:S(2)}, u32[]{:S(2)}) %collective-permute-start.10) | collective-permute-done | bytes 262176 | tf_op jit(solution)/shard_map/ppermute | solution.py:312
  33.8 0.5 collective-permute-done.11
  34.4 1.1 collective-permute-start.12
  35.4 1.6 %collective-permute-done.4 = f32[4,72,256]{2,1,0:T(8,128)S(1)} collective-permute-done((f32[4,72,256]{2,1,0:T(8,128)S(1)}, f32[4,72,256]{2,1,0:T(8,128)S(1)}, u32[]{:S(2)}, u32[]{:S(2)}) %collective-permute-start.4) | collective-permute-done | bytes 294944 | tf_op jit(solution)/shard_map/ppermute | solution.py:310
  37.1 1.2 %collective-permute-start.5 = (f32[2,72,256]{2,1,0:T(8,128)S(1)}, f32[2,72,256]{2,1,0:T(8,128)S(1)}, u32[]{:S(2)}, u32[]{:S(2)}) collective-permute-start(f32[2,72,256]{2,1,0:T(8,128)S(1)} %slice_add_fusion.6), channel_id=1, source_target_pairs={{0,64},{64,0},{128,192},{192,128},{32,224},{96,160},{160,96},{224,... | collective-permute-start | bytes 442376 | tf_op jit(solution)/shard_map/ppermute | solution.py:312
  38.3 1.2 %collective-permute-done.12 = f32[2,64,256]{2,1,0:T(8,128)S(1)} collective-permute-done((f32[2,64,256]{2,1,0:T(8,128)S(1)}, f32[2,64,256]{2,1,0:T(8,128)S(1)}, u32[]{:S(2)}, u32[]{:S(2)}) %collective-permute-start.12) | collective-permute-done | bytes 131104 | tf_op jit(solution)/shard_map/ppermute | solution.py:310
  39.5 0.1 collective-permute-start.13
  39.6 2.8 %collective-permute-done.5 = f32[2,72,256]{2,1,0:T(8,128)S(1)} collective-permute-done((f32[2,72,256]{2,1,0:T(8,128)S(1)}, f32[2,72,256]{2,1,0:T(8,128)S(1)}, u32[]{:S(2)}, u32[]{:S(2)}) %collective-permute-start.5) | collective-permute-done | bytes 147488 | tf_op jit(solution)/shard_map/ppermute | solution.py:312
  42.4 0.3 collective-permute-start.6
  42.7 3.1 %collective-permute-done.6 = f32[72,256]{1,0:T(8,128)S(1)} collective-permute-done((f32[72,256]{1,0:T(8,128)S(1)}, f32[72,256]{1,0:T(8,128)S(1)}, u32[]{:S(2)}, u32[]{:S(2)}) %collective-permute-start.6) | collective-permute-done | bytes 73760 | tf_op jit(solution)/shard_map/ppermute | solution.py:312
  46.0 17.0 %all_to_all.26 = f32[8,17,256]{2,1,0:T(8,128)S(1)} all-to-all(f32[8,17,256]{2,1,0:T(8,128)S(1)} %pad_maximum_fusion.2), channel_id=1, replica_groups=mesh['x'=4,'c'=2,'y'=4,'z'=8] {'z'}, dimensions={0} | all-to-all | bytes 278528 | tf_op jit(solution)/shard_map/all_to_all | solution.py:301
  63.0 3.7 %collective-permute-start.14 = (f32[16,256]{1,0:T(8,128)S(1)}, f32[16,256]{1,0:T(8,128)S(1)}, u32[]{:S(2)}, u32[]{:S(2)}) collective-permute-start(f32[16,256]{1,0:T(8,128)S(1)} %slice.236), channel_id=1, source_target_pairs={{0,32},{32,0},{1,33},{33,1},{2,34},{34,2},{3,35},{35,3},{4,36},{36... | collective-permute-start | bytes 49160 | tf_op jit(solution)/shard_map/ppermute | solution.py:293
  66.7 0.8 collective-permute-done.14
  67.6 0.3 fusion.12
  67.9 1.0 copy.6
  68.9 7.3 %all-to-all-start.1 = ((f32[128,1,512]{2,1,0:T(1,128)}), f32[128,1,512]{2,1,0:T(1,128)S(1)}, u32[]{:S(2)}, u32[]{:S(2)}) async-start(f32[128,1,512]{2,1,0:T(1,128)} %copy.6), calls=%async_computation.1 | async-start | bytes 524288 | tf_op jit(solution)/shard_map/all_to_all | solution.py:301
  76.3 0.8 collective-permute-start.15
  77.0 2.8 %collective-permute-start.16 = (f32[32,256]{1,0:T(8,128)S(1)}, f32[32,256]{1,0:T(8,128)S(1)}, u32[]{:S(2)}, u32[]{:S(2)}) collective-permute-start(f32[32,256]{1,0:T(8,128)S(1)} %pad_maximum_fusion.4.part_0), channel_id=1, source_target_pairs={{0,128},{64,192},{128,0},{192,64},{1,129},{65,193},{129,1},{193,65... | collective-permute-start | bytes 98312 | tf_op jit(solution)/shard_map/ppermute | solution.py:297
  79.8 0.4 collective-permute-start.17
  80.2 10.2 %all-to-all-done.1 = f32[128,1,512]{2,1,0:T(1,128)S(1)} async-done(((f32[128,1,512]{2,1,0:T(1,128)}), f32[128,1,512]{2,1,0:T(1,128)S(1)}, u32[]{:S(2)}, u32[]{:S(2)}) %all-to-all-start.1) | async-done | bytes 262176 | tf_op jit(solution)/shard_map/all_to_all | solution.py:301
  90.5 2.0 %collective-permute-start.18 = (f32[128,256]{1,0:T(8,128)S(1)}, f32[128,256]{1,0:T(8,128)S(1)}, u32[]{:S(2)}, u32[]{:S(2)}) collective-permute-start(f32[128,256]{1,0:T(8,128)S(1)} %get-tuple-element.49.mine_ref), channel_id=1, source_target_pairs={{0,32},{32,0},{1,33},{33,1},{2,34},{34,2},{3,35},{35,3},{4,36},{36... | collective-permute-start | bytes 393224 | tf_op jit(solution)/shard_map/ppermute | solution.py:293
  92.4 0.7 broadcast_in_dim.19
  93.2 6.4 %all-to-all-start.2 = ((f32[128,1,256]{2,1,0:T(1,128)}), f32[128,1,256]{2,1,0:T(1,128)S(1)}, u32[]{:S(2)}, u32[]{:S(2)}) async-start(f32[128,1,256]{2,1,0:T(1,128)} %broadcast_in_dim.19), calls=%async_computation.2 | async-start | bytes 262144 | tf_op jit(solution)/shard_map/all_to_all | solution.py:301
  99.6 8.1 %shard_map.42 = (f32[256,256]{1,0:T(8,128)S(1)}, f32[512,256]{1,0:T(8,128)}, f32[128,256]{1,0:T(8,128)S(1)}) custom-call(s32[18]{0:T(128)S(1)} %concatenate.15.slots_ref, f32[128,256]{1,0:T(8,128)S(1)} %get-tuple-element.49.mine_ref, f32[128,256]{1,0:T(8,128)S(1)} %collective-permute-done.18.other_ref, f32[512,256]{1,0:T(8,128)S(1)} %get-tuple-element.30.sketch_ref, ...), custom_call_target="tpu_custom_call" | custom-call | flops 10000000000 | bytes 2097152 | tf_op jit(solution)/shard_map/pallas_call | solution.py:240
  107.6 3.8 %all-to-all-done.2 = f32[128,1,256]{2,1,0:T(1,128)S(1)} async-done(((f32[128,1,256]{2,1,0:T(1,128)}), f32[128,1,256]{2,1,0:T(1,128)S(1)}, u32[]{:S(2)}, u32[]{:S(2)}) %all-to-all-start.2) | async-done | bytes 131104 | tf_op jit(solution)/shard_map/all_to_all | solution.py:301
  111.4 1.2 %collective-permute-start.19 = (f32[128,256]{1,0:T(8,128)S(1)}, f32[128,256]{1,0:T(8,128)S(1)}, u32[]{:S(2)}, u32[]{:S(2)}) collective-permute-start(f32[128,256]{1,0:T(8,128)S(1)} %bitcast.66), channel_id=1, source_target_pairs={{0,32},{32,0},{1,33},{33,1},{2,34},{34,2},{3,35},{35,3},{4,36},{36... | collective-permute-start | bytes 393224 | tf_op jit(solution)/shard_map/ppermute | solution.py:293
  112.7 1.0 collective-permute-done.19.other_ref
  113.6 4.7 %shard_map.43 = f32[128,256]{1,0:T(8,128)} custom-call(s32[18]{0:T(128)S(1)} %concatenate.15.slots_ref, f32[128,256]{1,0:T(8,128)S(1)} %bitcast.67, f32[128,256]{1,0:T(8,128)S(1)} %collective-permute-done.19.other_ref, f32[256,256]{1,0:T(8,128)S(1)} %get-tuple-element.38.inverse_ref, f32[128,256]{1,0:T(8,128)S(1)} %get-tuple-element.39.rows_ref), custom_call_target="tpu_custom_call" | custom-call | flops 10000000000 | bytes 1048576 | tf_op jit(solution)/shard_map/pallas_call | solution.py:281
  (41 shorter events, 0.8 us)
Async XLA Ops:
  13.7 4.9 %collective-permute-start.8 = (f32[2,4,64,256]{3,2,1,0:T(8,128)S(1)}, f32[2,4,64,256]{3,2,1,0:T(8,128)S(1)}, u32[]{:S(2)}, u32[]{:S(2)}) collective-permute-start(f32[2,4,64,256]{3,2,1,0:T(8,128)S(1)} %slice.186), channel_id=1, source_target_pairs={{0,32},{32,0},{1,33},{33,1},{2,34},{34,2},{3,35},{35,3},{4,36},{36... | collective-permute-start | bytes 1572872 | tf_op jit(solution)/shard_map/ppermute | solution.py:293
  17.1 5.4 %collective-permute-start.7 = (f32[2,4,64,256]{3,2,1,0:T(8,128)S(1)}, f32[2,4,64,256]{3,2,1,0:T(8,128)S(1)}, u32[]{:S(2)}, u32[]{:S(2)}) collective-permute-start(f32[2,4,64,256]{3,2,1,0:T(8,128)S(1)} %pad_maximum_fusion.1), channel_id=1, source_target_pairs={{0,32},{32,0},{1,33},{33,1},{2,34},{34,2},{3,35},{35,3},{4,36},{36... | collective-permute-start | bytes 1572872 | tf_op jit(solution)/shard_map/ppermute | solution.py:293
  17.3 2.9 %collective-permute-start.1 = (f32[2,4,72,256]{3,2,1,0:T(8,128)S(1)}, f32[2,4,72,256]{3,2,1,0:T(8,128)S(1)}, u32[]{:S(2)}, u32[]{:S(2)}) collective-permute-start(f32[2,4,72,256]{3,2,1,0:T(8,128)S(1)} %slice.163), channel_id=1, source_target_pairs={{0,32},{32,0},{1,33},{33,1},{2,34},{34,2},{3,35},{35,3},{4,36},{36... | collective-permute-start | bytes 1769480 | tf_op jit(solution)/shard_map/ppermute | solution.py:293
  18.0 11.3 %collective-permute-start = (f32[2,4,72,256]{3,2,1,0:T(8,128)S(1)}, f32[2,4,72,256]{3,2,1,0:T(8,128)S(1)}, u32[]{:S(2)}, u32[]{:S(2)}) collective-permute-start(f32[2,4,72,256]{3,2,1,0:T(8,128)S(1)} %pad_maximum_fusion), channel_id=1, source_target_pairs={{0,32},{32,0},{1,33},{33,1},{2,34},{34,2},{3,35},{35,3},{4,36},{36... | collective-permute-start | bytes 1769480 | tf_op jit(solution)/shard_map/ppermute | solution.py:293
  18.7 6.5 %collective-permute-start.9 = (f32[4,64,256]{2,1,0:T(8,128)S(1)}, f32[4,64,256]{2,1,0:T(8,128)S(1)}, u32[]{:S(2)}, u32[]{:S(2)}) collective-permute-start(f32[4,64,256]{2,1,0:T(8,128)S(1)} %get-tuple-element.47), channel_id=1, source_target_pairs={{0,64},{64,0},{128,192},{192,128},{32,224},{96,160},{160,96},{224,... | collective-permute-start | bytes 786440 | tf_op jit(solution)/shard_map/ppermute | solution.py:312
  20.3 6.9 %collective-permute-start.2 = (f32[4,72,256]{2,1,0:T(8,128)S(1)}, f32[4,72,256]{2,1,0:T(8,128)S(1)}, u32[]{:S(2)}, u32[]{:S(2)}) collective-permute-start(f32[4,72,256]{2,1,0:T(8,128)S(1)} %get-tuple-element.45), channel_id=1, source_target_pairs={{0,8},{8,0},{16,24},{24,16},{32,56},{40,48},{48,40},{56,32},{1,9},... | collective-permute-start | bytes 884744 | tf_op jit(solution)/shard_map/ppermute | solution.py:310
  25.2 8.6 %collective-permute-start.10 = (f32[4,64,256]{2,1,0:T(8,128)S(1)}, f32[4,64,256]{2,1,0:T(8,128)S(1)}, u32[]{:S(2)}, u32[]{:S(2)}) collective-permute-start(f32[4,64,256]{2,1,0:T(8,128)S(1)} %get-tuple-element.27), channel_id=1, source_target_pairs={{0,64},{64,0},{128,192},{192,128},{32,224},{96,160},{160,96},{224,... | collective-permute-start | bytes 786440 | tf_op jit(solution)/shard_map/ppermute | solution.py:312
  26.0 8.3 %collective-permute-start.11 = (f32[4,64,256]{2,1,0:T(8,128)S(1)}, f32[4,64,256]{2,1,0:T(8,128)S(1)}, u32[]{:S(2)}, u32[]{:S(2)}) collective-permute-start(f32[4,64,256]{2,1,0:T(8,128)S(1)} %fusion.3), channel_id=1, source_target_pairs={{0,192},{64,128},{128,64},{192,0},{32,96},{96,32},{160,224},{224,1... | collective-permute-start | bytes 786440 | tf_op jit(solution)/shard_map/ppermute | solution.py:312
  27.2 8.3 %collective-permute-start.3 = (f32[4,72,256]{2,1,0:T(8,128)S(1)}, f32[4,72,256]{2,1,0:T(8,128)S(1)}, u32[]{:S(2)}, u32[]{:S(2)}) collective-permute-start(f32[4,72,256]{2,1,0:T(8,128)S(1)} %get-tuple-element.23), channel_id=1, source_target_pairs={{0,8},{8,0},{16,24},{24,16},{32,56},{40,48},{48,40},{56,32},{1,9},... | collective-permute-start | bytes 884744 | tf_op jit(solution)/shard_map/ppermute | solution.py:310
  29.3 7.7 %collective-permute-start.4 = (f32[4,72,256]{2,1,0:T(8,128)S(1)}, f32[4,72,256]{2,1,0:T(8,128)S(1)}, u32[]{:S(2)}, u32[]{:S(2)}) collective-permute-start(f32[4,72,256]{2,1,0:T(8,128)S(1)} %fusion.1), channel_id=1, source_target_pairs={{0,24},{8,16},{16,8},{24,0},{32,40},{40,32},{48,56},{56,48},{1,25}... | collective-permute-start | bytes 884744 | tf_op jit(solution)/shard_map/ppermute | solution.py:310
  34.4 5.1 %collective-permute-start.12 = (f32[2,64,256]{2,1,0:T(8,128)S(1)}, f32[2,64,256]{2,1,0:T(8,128)S(1)}, u32[]{:S(2)}, u32[]{:S(2)}) collective-permute-start(f32[2,64,256]{2,1,0:T(8,128)S(1)} %slice_add_fusion.8), channel_id=1, source_target_pairs={{0,8},{8,0},{16,24},{24,16},{32,56},{40,48},{48,40},{56,32},{1,9},... | collective-permute-start | bytes 393224 | tf_op jit(solution)/shard_map/ppermute | solution.py:310
  37.1 5.3 %collective-permute-start.5 = (f32[2,72,256]{2,1,0:T(8,128)S(1)}, f32[2,72,256]{2,1,0:T(8,128)S(1)}, u32[]{:S(2)}, u32[]{:S(2)}) collective-permute-start(f32[2,72,256]{2,1,0:T(8,128)S(1)} %slice_add_fusion.6), channel_id=1, source_target_pairs={{0,64},{64,0},{128,192},{192,128},{32,224},{96,160},{160,96},{224,... | collective-permute-start | bytes 442376 | tf_op jit(solution)/shard_map/ppermute | solution.py:312
  39.5 3.2 %collective-permute-start.13 = (f32[64,256]{1,0:T(8,128)S(1)}, f32[64,256]{1,0:T(8,128)S(1)}, u32[]{:S(2)}, u32[]{:S(2)}) collective-permute-start(f32[64,256]{1,0:T(8,128)S(1)} %fusion.7), channel_id=1, source_target_pairs={{0,24},{8,16},{16,8},{24,0},{32,40},{40,32},{48,56},{56,48},{1,25}... | collective-permute-start | bytes 196616 | tf_op jit(solution)/shard_map/ppermute | solution.py:310
  42.4 3.5 %collective-permute-start.6 = (f32[72,256]{1,0:T(8,128)S(1)}, f32[72,256]{1,0:T(8,128)S(1)}, u32[]{:S(2)}, u32[]{:S(2)}) collective-permute-start(f32[72,256]{1,0:T(8,128)S(1)} %fusion.4), channel_id=1, source_target_pairs={{0,192},{64,128},{128,64},{192,0},{32,96},{96,32},{160,224},{224,1... | collective-permute-start | bytes 221192 | tf_op jit(solution)/shard_map/ppermute | solution.py:312
  63.0 4.6 %collective-permute-start.14 = (f32[16,256]{1,0:T(8,128)S(1)}, f32[16,256]{1,0:T(8,128)S(1)}, u32[]{:S(2)}, u32[]{:S(2)}) collective-permute-start(f32[16,256]{1,0:T(8,128)S(1)} %slice.236), channel_id=1, source_target_pairs={{0,32},{32,0},{1,33},{33,1},{2,34},{34,2},{3,35},{35,3},{4,36},{36... | collective-permute-start | bytes 49160 | tf_op jit(solution)/shard_map/ppermute | solution.py:293
  68.9 21.5 %all-to-all-start.1 = ((f32[128,1,512]{2,1,0:T(1,128)}), f32[128,1,512]{2,1,0:T(1,128)S(1)}, u32[]{:S(2)}, u32[]{:S(2)}) async-start(f32[128,1,512]{2,1,0:T(1,128)} %copy.6), calls=%async_computation.1 | async-start | bytes 524288 | tf_op jit(solution)/shard_map/all_to_all | solution.py:301
  76.3 14.2 %collective-permute-start.15 = (f32[32,256]{1,0:T(8,128)S(1)}, f32[32,256]{1,0:T(8,128)S(1)}, u32[]{:S(2)}, u32[]{:S(2)}) collective-permute-start(f32[32,256]{1,0:T(8,128)S(1)} %pad_maximum_fusion.4.part_0), channel_id=1, source_target_pairs={{0,64},{64,0},{128,192},{192,128},{1,65},{65,1},{129,193},{193,129... | collective-permute-start | bytes 98312 | tf_op jit(solution)/shard_map/ppermute | solution.py:297
  77.0 13.4 %collective-permute-start.16 = (f32[32,256]{1,0:T(8,128)S(1)}, f32[32,256]{1,0:T(8,128)S(1)}, u32[]{:S(2)}, u32[]{:S(2)}) collective-permute-start(f32[32,256]{1,0:T(8,128)S(1)} %pad_maximum_fusion.4.part_0), channel_id=1, source_target_pairs={{0,128},{64,192},{128,0},{192,64},{1,129},{65,193},{129,1},{193,65... | collective-permute-start | bytes 98312 | tf_op jit(solution)/shard_map/ppermute | solution.py:297
  79.8 10.6 %collective-permute-start.17 = (f32[32,256]{1,0:T(8,128)S(1)}, f32[32,256]{1,0:T(8,128)S(1)}, u32[]{:S(2)}, u32[]{:S(2)}) collective-permute-start(f32[32,256]{1,0:T(8,128)S(1)} %pad_maximum_fusion.4.part_0), channel_id=1, source_target_pairs={{0,192},{64,128},{128,64},{192,0},{1,193},{65,129},{129,65},{193,1... | collective-permute-start | bytes 98312 | tf_op jit(solution)/shard_map/ppermute | solution.py:297
  90.5 9.1 %collective-permute-start.18 = (f32[128,256]{1,0:T(8,128)S(1)}, f32[128,256]{1,0:T(8,128)S(1)}, u32[]{:S(2)}, u32[]{:S(2)}) collective-permute-start(f32[128,256]{1,0:T(8,128)S(1)} %get-tuple-element.49.mine_ref), channel_id=1, source_target_pairs={{0,32},{32,0},{1,33},{33,1},{2,34},{34,2},{3,35},{35,3},{4,36},{36... | collective-permute-start | bytes 393224 | tf_op jit(solution)/shard_map/ppermute | solution.py:293
  93.2 18.2 %all-to-all-start.2 = ((f32[128,1,256]{2,1,0:T(1,128)}), f32[128,1,256]{2,1,0:T(1,128)S(1)}, u32[]{:S(2)}, u32[]{:S(2)}) async-start(f32[128,1,256]{2,1,0:T(1,128)} %broadcast_in_dim.19), calls=%async_computation.2 | async-start | bytes 262144 | tf_op jit(solution)/shard_map/all_to_all | solution.py:301
  111.4 2.2 %collective-permute-start.19 = (f32[128,256]{1,0:T(8,128)S(1)}, f32[128,256]{1,0:T(8,128)S(1)}, u32[]{:S(2)}, u32[]{:S(2)}) collective-permute-start(f32[128,256]{1,0:T(8,128)S(1)} %bitcast.66), channel_id=1, source_target_pairs={{0,32},{32,0},{1,33},{33,1},{2,34},{34,2},{3,35},{35,3},{4,36},{36... | collective-permute-start | bytes 393224 | tf_op jit(solution)/shard_map/ppermute | solution.py:293

commit v9 on v8

--- a/solution.py
+++ b/solution.py
@@ -356,7 +356,7 @@
         terms.append([by_slot(keep), (to_core(middle), rest[0], rest[1])])
     line_a, line_b = ring_sums(*terms, "y", "x", apart=True)
     line_a, line_b = ([by_slot(v) for v in line] for line in (line_a, line_b))
-    own_a, own_b = ring_sums(line_a, line_b, "x", "y")
+    own_a, own_b = ring_sums(line_a, line_b, "x", "y", apart=True)
     own_a, own_b = sum(own_a), sum(own_b)
     size = own_b.shape[0]
     line = jnp.concatenate([own_a[:size], own_b]).reshape(NZ, share, rank)

time: 119 us -> 119 us (level)
  starting transfers between devices: 37.5 us -> 40.2 us
  blocking collectives: 17 us -> 15.5 us
    ppermute x5 -> x6, starting transfers between devices: 5.53 us -> 7.74 us  [ring_pairs(): return lax.ppermute(block, ('c', 'y'), pairs)]
    ppermute x5 -> x6, waiting for transfers between devices: 13.4 us -> 11.7 us  [ring_pairs(): return lax.ppermute(block, ('x', 'c'), pairs)]
    all_to_all x1, blocking collectives: 17 us -> 15.5 us  [exchange(): return lax.all_to_all(blocks, axes, 0, 0, tiled=True)]
    ppermute x5 -> x6, waiting for transfers between devices: 3.87 us -> 5.16 us  [ring_pairs(): return lax.ppermute(block, ('c', 'y'), pairs)]
    ppermute x5 -> x6, starting transfers between devices: 3.18 us -> 3.46 us  [ring_pairs(): return lax.ppermute(block, ('x', 'c'), pairs)]
  transfers between devices with their start and end apart: 22 -> 24, of which waited for: 14 -> 15; matrix products, arithmetic and copies ran while one was open for 1% -> 1% of each run, Pallas kernels for 7% -> 7%
where the time goes in v9:
time: 119 us
  starting transfers between devices  40.2 us (34%)
  waiting for transfers between devices  33.8 us (28%)
  Pallas kernels  25.7 us (22%)
  blocking collectives  15.5 us (13%)
  local copies, waits for them, and re-layouts  2.09 us (2%)
    all_to_all x1, blocking collectives, exchange(): return lax.all_to_all(blocks, axes, 0, 0, tiled=True)  15.5 us
    all_to_all x2, waiting for transfers between devices, exchange(): return lax.all_to_all(blocks, axes, 0, 0, tiled=True)  14 us
    all_to_all x2, starting transfers between devices, exchange(): return lax.all_to_all(blocks, axes, 0, 0, tiled=True)  13.5 us
    pallas_call x1, Pallas kernels, products(): pl.pallas_call(products_kernel, grid_spec=pltpu.PrefetchScalarGridSpec(nu...  12.9 us
    ppermute x6, waiting for transfers between devices, ring_pairs(): return lax.ppermute(block, ('x', 'c'), pairs)  11.7 us
    ppermute x7, starting transfers between devices, to_core(): return lax.ppermute(block, 'c', [(0, 1), (1, 0)])  11.6 us
    pallas_call x1, Pallas kernels, basis(): pl.pallas_call(functools.partial(basis_kernel, scale), out_shape=(jax.Sha...  8.05 us
    ppermute x6, starting transfers between devices, ring_pairs(): return lax.ppermute(block, ('c', 'y'), pairs)  7.74 us
  transfers between devices with their start and end apart: 24, of which 15 were waited for; matrix products, arithmetic and copies ran while one was open for 1% of the time, Pallas kernels for 7%

profile of v9, /device:TPU:1, one launch (start us, length us, event | category | flops | bytes accessed | tf_op | source)
XLA Modules:
  0.0 119.2 jit_solution(1494172391362038290)
XLA Ops:
  0.7 0.1 concatenate.15.slots_ref
  0.8 12.9 %shard_map.41 = (f32[512,256]{1,0:T(8,128)S(1)}, f32[4,4,72,256]{3,2,1,0:T(8,128)S(1)}, f32[4,4,64,256]{3,2,1,0:T(8,128)S(1)}, f32[4,4,72,256]{3,2,1,0:T(8,128)S(1)}, f32[4,4,64,256]{3,2,1,0:T(8,128)S(1)}) custom-call(s32[18]{0:T(128)S(1)} %concatenate.15.slots_ref, f32[512,4096]{1,0:T(8,128)} %emb_ref.1, f32[4096,256]{1,0:T(8,128)} %matrix_ref.1), custom_call_target="tpu_custom_call" | custom-call | flops 6442450944 | bytes 25165824 | tf_op jit(solution)/shard_map/pallas_call | solution.py:124
  13.7 3.3 %collective-permute-start.9 = (f32[2,4,64,256]{3,2,1,0:T(8,128)S(1)}, f32[2,4,64,256]{3,2,1,0:T(8,128)S(1)}, u32[]{:S(2)}, u32[]{:S(2)}) collective-permute-start(f32[2,4,64,256]{3,2,1,0:T(8,128)S(1)} %slice.200), channel_id=1, source_target_pairs={{0,32},{32,0},{1,33},{33,1},{2,34},{34,2},{3,35},{35,3},{4,36},{36... | collective-permute-start | bytes 1572872 | tf_op jit(solution)/shard_map/ppermute | solution.py:293
  17.1 0.1 collective-permute-start.8
  17.3 0.6 collective-permute-start.1
  18.0 0.1 collective-permute-start
  18.1 0.5 collective-permute-done.9
  18.7 0.8 collective-permute-start.10
  19.6 0.6 collective-permute-done.1
  20.2 0.1 slice_add_fusion
  20.3 2.2 %collective-permute-start.2 = (f32[4,72,256]{2,1,0:T(8,128)S(1)}, f32[4,72,256]{2,1,0:T(8,128)S(1)}, u32[]{:S(2)}, u32[]{:S(2)}) collective-permute-start(f32[4,72,256]{2,1,0:T(8,128)S(1)} %get-tuple-element.53), channel_id=1, source_target_pairs={{0,8},{8,0},{16,24},{24,16},{32,56},{40,48},{48,40},{56,32},{1,9},... | collective-permute-start | bytes 884744 | tf_op jit(solution)/shard_map/ppermute | solution.py:310
  22.5 2.7 %collective-permute-done.10 = f32[4,64,256]{2,1,0:T(8,128)S(1)} collective-permute-done((f32[4,64,256]{2,1,0:T(8,128)S(1)}, f32[4,64,256]{2,1,0:T(8,128)S(1)}, u32[]{:S(2)}, u32[]{:S(2)}) %collective-permute-start.10) | collective-permute-done | bytes 262176 | tf_op jit(solution)/shard_map/ppermute | solution.py:312
  25.2 0.8 collective-permute-start.11
  26.0 0.1 collective-permute-start.12
  26.2 1.0 collective-permute-done.2
  27.2 2.1 %collective-permute-start.3 = (f32[4,72,256]{2,1,0:T(8,128)S(1)}, f32[4,72,256]{2,1,0:T(8,128)S(1)}, u32[]{:S(2)}, u32[]{:S(2)}) collective-permute-start(f32[4,72,256]{2,1,0:T(8,128)S(1)} %get-tuple-element.27), channel_id=1, source_target_pairs={{0,8},{8,0},{16,24},{24,16},{32,56},{40,48},{48,40},{56,32},{1,9},... | collective-permute-start | bytes 884744 | tf_op jit(solution)/shard_map/ppermute | solution.py:310
  29.3 0.1 collective-permute-start.4
  29.4 4.4 %collective-permute-done.11 = f32[4,64,256]{2,1,0:T(8,128)S(1)} collective-permute-done((f32[4,64,256]{2,1,0:T(8,128)S(1)}, f32[4,64,256]{2,1,0:T(8,128)S(1)}, u32[]{:S(2)}, u32[]{:S(2)}) %collective-permute-start.11) | collective-permute-done | bytes 262176 | tf_op jit(solution)/shard_map/ppermute | solution.py:312
  33.8 0.5 collective-permute-done.12
  34.4 1.1 collective-permute-start.13
  35.5 3.3 %collective-permute-done.13 = f32[64,256]{1,0:T(8,128)S(1)} collective-permute-done((f32[64,256]{1,0:T(8,128)S(1)}, f32[64,256]{1,0:T(8,128)S(1)}, u32[]{:S(2)}, u32[]{:S(2)}) %collective-permute-start.13) | collective-permute-done | bytes 65568 | tf_op jit(solution)/shard_map/ppermute | solution.py:310
  38.9 0.8 collective-permute-start.5
  39.7 0.1 collective-permute-start.15
  39.8 2.2 %collective-permute-start.14 = (f32[64,256]{1,0:T(8,128)S(1)}, f32[64,256]{1,0:T(8,128)S(1)}, u32[]{:S(2)}, u32[]{:S(2)}) collective-permute-start(f32[64,256]{1,0:T(8,128)S(1)} %get-tuple-element.35), channel_id=1, source_target_pairs={{0,8},{8,0},{16,24},{24,16},{32,56},{40,48},{48,40},{56,32},{1,9},... | collective-permute-start | bytes 196616 | tf_op jit(solution)/shard_map/ppermute | solution.py:310
  42.0 1.3 %collective-permute-done.5 = f32[72,256]{1,0:T(8,128)S(1)} collective-permute-done((f32[72,256]{1,0:T(8,128)S(1)}, f32[72,256]{1,0:T(8,128)S(1)}, u32[]{:S(2)}, u32[]{:S(2)}) %collective-permute-start.5) | collective-permute-done | bytes 73760 | tf_op jit(solution)/shard_map/ppermute | solution.py:312
  43.4 0.1 collective-permute-start.7
  43.5 0.8 collective-permute-start.6
  44.3 0.9 collective-permute-done.14
  45.2 1.5 %collective-permute-done.7 = f32[72,256]{1,0:T(8,128)S(1)} collective-permute-done((f32[72,256]{1,0:T(8,128)S(1)}, f32[72,256]{1,0:T(8,128)S(1)}, u32[]{:S(2)}, u32[]{:S(2)}) %collective-permute-start.7) | collective-permute-done | bytes 73760 | tf_op jit(solution)/shard_map/ppermute | solution.py:312
  46.7 1.3 %collective-permute-done.6 = f32[72,256]{1,0:T(8,128)S(1)} collective-permute-done((f32[72,256]{1,0:T(8,128)S(1)}, f32[72,256]{1,0:T(8,128)S(1)}, u32[]{:S(2)}, u32[]{:S(2)}) %collective-permute-start.6) | collective-permute-done | bytes 73760 | tf_op jit(solution)/shard_map/ppermute | solution.py:312
  48.1 15.5 %all_to_all.26 = f32[8,17,256]{2,1,0:T(8,128)S(1)} all-to-all(f32[8,17,256]{2,1,0:T(8,128)S(1)} %pad_maximum_fusion.2), channel_id=1, replica_groups=mesh['x'=4,'c'=2,'y'=4,'z'=8] {'z'}, dimensions={0} | all-to-all | bytes 278528 | tf_op jit(solution)/shard_map/all_to_all | solution.py:301
  63.6 4.2 %collective-permute-start.16 = (f32[16,256]{1,0:T(8,128)S(1)}, f32[16,256]{1,0:T(8,128)S(1)}, u32[]{:S(2)}, u32[]{:S(2)}) collective-permute-start(f32[16,256]{1,0:T(8,128)S(1)} %slice.256), channel_id=1, source_target_pairs={{0,32},{32,0},{1,33},{33,1},{2,34},{34,2},{3,35},{35,3},{4,36},{36... | collective-permute-start | bytes 49160 | tf_op jit(solution)/shard_map/ppermute | solution.py:293
  67.8 0.8 collective-permute-done.16
  68.7 0.3 fusion.16
  69.0 1.0 copy.6
  70.0 7.1 %all-to-all-start.1 = ((f32[128,1,512]{2,1,0:T(1,128)}), f32[128,1,512]{2,1,0:T(1,128)S(1)}, u32[]{:S(2)}, u32[]{:S(2)}) async-start(f32[128,1,512]{2,1,0:T(1,128)} %copy.6), calls=%async_computation.1 | async-start | bytes 524288 | tf_op jit(solution)/shard_map/all_to_all | solution.py:301
  77.1 0.8 collective-permute-start.17
  77.9 2.8 %collective-permute-start.18 = (f32[32,256]{1,0:T(8,128)S(1)}, f32[32,256]{1,0:T(8,128)S(1)}, u32[]{:S(2)}, u32[]{:S(2)}) collective-permute-start(f32[32,256]{1,0:T(8,128)S(1)} %pad_maximum_fusion.4.part_0), channel_id=1, source_target_pairs={{0,128},{64,192},{128,0},{192,64},{1,129},{65,193},{129,1},{193,65... | collective-permute-start | bytes 98312 | tf_op jit(solution)/shard_map/ppermute | solution.py:297
  80.7 0.4 collective-permute-start.19
  81.0 10.2 %all-to-all-done.1 = f32[128,1,512]{2,1,0:T(1,128)S(1)} async-done(((f32[128,1,512]{2,1,0:T(1,128)}), f32[128,1,512]{2,1,0:T(1,128)S(1)}, u32[]{:S(2)}, u32[]{:S(2)}) %all-to-all-start.1) | async-done | bytes 262176 | tf_op jit(solution)/shard_map/all_to_all | solution.py:301
  91.3 2.0 %collective-permute-start.20 = (f32[128,256]{1,0:T(8,128)S(1)}, f32[128,256]{1,0:T(8,128)S(1)}, u32[]{:S(2)}, u32[]{:S(2)}) collective-permute-start(f32[128,256]{1,0:T(8,128)S(1)} %get-tuple-element.57.mine_ref), channel_id=1, source_target_pairs={{0,32},{32,0},{1,33},{33,1},{2,34},{34,2},{3,35},{35,3},{4,36},{36... | collective-permute-start | bytes 393224 | tf_op jit(solution)/shard_map/ppermute | solution.py:293
  93.3 0.7 broadcast_in_dim.19
  94.0 6.4 %all-to-all-start.2 = ((f32[128,1,256]{2,1,0:T(1,128)}), f32[128,1,256]{2,1,0:T(1,128)S(1)}, u32[]{:S(2)}, u32[]{:S(2)}) async-start(f32[128,1,256]{2,1,0:T(1,128)} %broadcast_in_dim.19), calls=%async_computation.2 | async-start | bytes 262144 | tf_op jit(solution)/shard_map/all_to_all | solution.py:301
  100.4 8.1 %shard_map.42 = (f32[256,256]{1,0:T(8,128)S(1)}, f32[512,256]{1,0:T(8,128)}, f32[128,256]{1,0:T(8,128)S(1)}) custom-call(s32[18]{0:T(128)S(1)} %concatenate.15.slots_ref, f32[128,256]{1,0:T(8,128)S(1)} %get-tuple-element.57.mine_ref, f32[128,256]{1,0:T(8,128)S(1)} %collective-permute-done.20.other_ref, f32[512,256]{1,0:T(8,128)S(1)} %get-tuple-element.38.sketch_ref, ...), custom_call_target="tpu_custom_call" | custom-call | flops 10000000000 | bytes 2097152 | tf_op jit(solution)/shard_map/pallas_call | solution.py:240
  108.5 3.8 %all-to-all-done.2 = f32[128,1,256]{2,1,0:T(1,128)S(1)} async-done(((f32[128,1,256]{2,1,0:T(1,128)}), f32[128,1,256]{2,1,0:T(1,128)S(1)}, u32[]{:S(2)}, u32[]{:S(2)}) %all-to-all-start.2) | async-done | bytes 131104 | tf_op jit(solution)/shard_map/all_to_all | solution.py:301
  112.3 1.2 %collective-permute-start.21 = (f32[128,256]{1,0:T(8,128)S(1)}, f32[128,256]{1,0:T(8,128)S(1)}, u32[]{:S(2)}, u32[]{:S(2)}) collective-permute-start(f32[128,256]{1,0:T(8,128)S(1)} %bitcast.82), channel_id=1, source_target_pairs={{0,32},{32,0},{1,33},{33,1},{2,34},{34,2},{3,35},{35,3},{4,36},{36... | collective-permute-start | bytes 393224 | tf_op jit(solution)/shard_map/ppermute | solution.py:293
  113.5 1.0 collective-permute-done.21.other_ref
  114.5 4.7 %shard_map.43 = f32[128,256]{1,0:T(8,128)} custom-call(s32[18]{0:T(128)S(1)} %concatenate.15.slots_ref, f32[128,256]{1,0:T(8,128)S(1)} %bitcast.83, f32[128,256]{1,0:T(8,128)S(1)} %collective-permute-done.21.other_ref, f32[256,256]{1,0:T(8,128)S(1)} %get-tuple-element.46.inverse_ref, f32[128,256]{1,0:T(8,128)S(1)} %get-tuple-element.47.rows_ref), custom_call_target="tpu_custom_call" | custom-call | flops 10000000000 | bytes 1048576 | tf_op jit(solution)/shard_map/pallas_call | solution.py:281
  (47 shorter events, 1.0 us)
Async XLA Ops:
  13.7 4.9 %collective-permute-start.9 = (f32[2,4,64,256]{3,2,1,0:T(8,128)S(1)}, f32[2,4,64,256]{3,2,1,0:T(8,128)S(1)}, u32[]{:S(2)}, u32[]{:S(2)}) collective-permute-start(f32[2,4,64,256]{3,2,1,0:T(8,128)S(1)} %slice.200), channel_id=1, source_target_pairs={{0,32},{32,0},{1,33},{33,1},{2,34},{34,2},{3,35},{35,3},{4,36},{36... | collective-permute-start | bytes 1572872 | tf_op jit(solution)/shard_map/ppermute | solution.py:293
  17.1 8.8 %collective-permute-start.8 = (f32[2,4,64,256]{3,2,1,0:T(8,128)S(1)}, f32[2,4,64,256]{3,2,1,0:T(8,128)S(1)}, u32[]{:S(2)}, u32[]{:S(2)}) collective-permute-start(f32[2,4,64,256]{3,2,1,0:T(8,128)S(1)} %pad_maximum_fusion.1), channel_id=1, source_target_pairs={{0,32},{32,0},{1,33},{33,1},{2,34},{34,2},{3,35},{35,3},{4,36},{36... | collective-permute-start | bytes 1572872 | tf_op jit(solution)/shard_map/ppermute | solution.py:293
  17.3 2.9 %collective-permute-start.1 = (f32[2,4,72,256]{3,2,1,0:T(8,128)S(1)}, f32[2,4,72,256]{3,2,1,0:T(8,128)S(1)}, u32[]{:S(2)}, u32[]{:S(2)}) collective-permute-start(f32[2,4,72,256]{3,2,1,0:T(8,128)S(1)} %slice.175), channel_id=1, source_target_pairs={{0,32},{32,0},{1,33},{33,1},{2,34},{34,2},{3,35},{35,3},{4,36},{36... | collective-permute-start | bytes 1769480 | tf_op jit(solution)/shard_map/ppermute | solution.py:293
  18.0 11.3 %collective-permute-start = (f32[2,4,72,256]{3,2,1,0:T(8,128)S(1)}, f32[2,4,72,256]{3,2,1,0:T(8,128)S(1)}, u32[]{:S(2)}, u32[]{:S(2)}) collective-permute-start(f32[2,4,72,256]{3,2,1,0:T(8,128)S(1)} %pad_maximum_fusion), channel_id=1, source_target_pairs={{0,32},{32,0},{1,33},{33,1},{2,34},{34,2},{3,35},{35,3},{4,36},{36... | collective-permute-start | bytes 1769480 | tf_op jit(solution)/shard_map/ppermute | solution.py:293
  18.7 6.5 %collective-permute-start.10 = (f32[4,64,256]{2,1,0:T(8,128)S(1)}, f32[4,64,256]{2,1,0:T(8,128)S(1)}, u32[]{:S(2)}, u32[]{:S(2)}) collective-permute-start(f32[4,64,256]{2,1,0:T(8,128)S(1)} %get-tuple-element.55), channel_id=1, source_target_pairs={{0,64},{64,0},{128,192},{192,128},{32,224},{96,160},{160,96},{224,... | collective-permute-start | bytes 786440 | tf_op jit(solution)/shard_map/ppermute | solution.py:312
  20.3 6.9 %collective-permute-start.2 = (f32[4,72,256]{2,1,0:T(8,128)S(1)}, f32[4,72,256]{2,1,0:T(8,128)S(1)}, u32[]{:S(2)}, u32[]{:S(2)}) collective-permute-start(f32[4,72,256]{2,1,0:T(8,128)S(1)} %get-tuple-element.53), channel_id=1, source_target_pairs={{0,8},{8,0},{16,24},{24,16},{32,56},{40,48},{48,40},{56,32},{1,9},... | collective-permute-start | bytes 884744 | tf_op jit(solution)/shard_map/ppermute | solution.py:310
  25.2 8.6 %collective-permute-start.11 = (f32[4,64,256]{2,1,0:T(8,128)S(1)}, f32[4,64,256]{2,1,0:T(8,128)S(1)}, u32[]{:S(2)}, u32[]{:S(2)}) collective-permute-start(f32[4,64,256]{2,1,0:T(8,128)S(1)} %get-tuple-element.33), channel_id=1, source_target_pairs={{0,64},{64,0},{128,192},{192,128},{32,224},{96,160},{160,96},{224,... | collective-permute-start | bytes 786440 | tf_op jit(solution)/shard_map/ppermute | solution.py:312
  26.0 8.3 %collective-permute-start.12 = (f32[4,64,256]{2,1,0:T(8,128)S(1)}, f32[4,64,256]{2,1,0:T(8,128)S(1)}, u32[]{:S(2)}, u32[]{:S(2)}) collective-permute-start(f32[4,64,256]{2,1,0:T(8,128)S(1)} %fusion.3), channel_id=1, source_target_pairs={{0,192},{64,128},{128,64},{192,0},{32,96},{96,32},{160,224},{224,1... | collective-permute-start | bytes 786440 | tf_op jit(solution)/shard_map/ppermute | solution.py:312
  27.2 11.6 %collective-permute-start.3 = (f32[4,72,256]{2,1,0:T(8,128)S(1)}, f32[4,72,256]{2,1,0:T(8,128)S(1)}, u32[]{:S(2)}, u32[]{:S(2)}) collective-permute-start(f32[4,72,256]{2,1,0:T(8,128)S(1)} %get-tuple-element.27), channel_id=1, source_target_pairs={{0,8},{8,0},{16,24},{24,16},{32,56},{40,48},{48,40},{56,32},{1,9},... | collective-permute-start | bytes 884744 | tf_op jit(solution)/shard_map/ppermute | solution.py:310
  29.3 9.5 %collective-permute-start.4 = (f32[4,72,256]{2,1,0:T(8,128)S(1)}, f32[4,72,256]{2,1,0:T(8,128)S(1)}, u32[]{:S(2)}, u32[]{:S(2)}) collective-permute-start(f32[4,72,256]{2,1,0:T(8,128)S(1)} %fusion.1), channel_id=1, source_target_pairs={{0,24},{8,16},{16,8},{24,0},{32,40},{40,32},{48,56},{56,48},{1,25}... | collective-permute-start | bytes 884744 | tf_op jit(solution)/shard_map/ppermute | solution.py:310
  34.4 4.4 %collective-permute-start.13 = (f32[64,256]{1,0:T(8,128)S(1)}, f32[64,256]{1,0:T(8,128)S(1)}, u32[]{:S(2)}, u32[]{:S(2)}) collective-permute-start(f32[64,256]{1,0:T(8,128)S(1)} %get-tuple-element.61), channel_id=1, source_target_pairs={{0,8},{8,0},{16,24},{24,16},{32,56},{40,48},{48,40},{56,32},{1,9},... | collective-permute-start | bytes 196616 | tf_op jit(solution)/shard_map/ppermute | solution.py:310
  38.9 4.5 %collective-permute-start.5 = (f32[72,256]{1,0:T(8,128)S(1)}, f32[72,256]{1,0:T(8,128)S(1)}, u32[]{:S(2)}, u32[]{:S(2)}) collective-permute-start(f32[72,256]{1,0:T(8,128)S(1)} %get-tuple-element.59), channel_id=1, source_target_pairs={{0,64},{64,0},{128,192},{192,128},{32,224},{96,160},{160,96},{224,... | collective-permute-start | bytes 221192 | tf_op jit(solution)/shard_map/ppermute | solution.py:312
  39.7 4.6 %collective-permute-start.15 = (f32[64,256]{1,0:T(8,128)S(1)}, f32[64,256]{1,0:T(8,128)S(1)}, u32[]{:S(2)}, u32[]{:S(2)}) collective-permute-start(f32[64,256]{1,0:T(8,128)S(1)} %fusion.10), channel_id=1, source_target_pairs={{0,24},{8,16},{16,8},{24,0},{32,40},{40,32},{48,56},{56,48},{1,25}... | collective-permute-start | bytes 196616 | tf_op jit(solution)/shard_map/ppermute | solution.py:310
  39.8 5.4 %collective-permute-start.14 = (f32[64,256]{1,0:T(8,128)S(1)}, f32[64,256]{1,0:T(8,128)S(1)}, u32[]{:S(2)}, u32[]{:S(2)}) collective-permute-start(f32[64,256]{1,0:T(8,128)S(1)} %get-tuple-element.35), channel_id=1, source_target_pairs={{0,8},{8,0},{16,24},{24,16},{32,56},{40,48},{48,40},{56,32},{1,9},... | collective-permute-start | bytes 196616 | tf_op jit(solution)/shard_map/ppermute | solution.py:310
  43.4 3.3 %collective-permute-start.7 = (f32[72,256]{1,0:T(8,128)S(1)}, f32[72,256]{1,0:T(8,128)S(1)}, u32[]{:S(2)}, u32[]{:S(2)}) collective-permute-start(f32[72,256]{1,0:T(8,128)S(1)} %fusion.5), channel_id=1, source_target_pairs={{0,192},{64,128},{128,64},{192,0},{32,96},{96,32},{160,224},{224,1... | collective-permute-start | bytes 221192 | tf_op jit(solution)/shard_map/ppermute | solution.py:312
  43.5 4.5 %collective-permute-start.6 = (f32[72,256]{1,0:T(8,128)S(1)}, f32[72,256]{1,0:T(8,128)S(1)}, u32[]{:S(2)}, u32[]{:S(2)}) collective-permute-start(f32[72,256]{1,0:T(8,128)S(1)} %get-tuple-element.29), channel_id=1, source_target_pairs={{0,64},{64,0},{128,192},{192,128},{32,224},{96,160},{160,96},{224,... | collective-permute-start | bytes 221192 | tf_op jit(solution)/shard_map/ppermute | solution.py:312
  63.6 5.1 %collective-permute-start.16 = (f32[16,256]{1,0:T(8,128)S(1)}, f32[16,256]{1,0:T(8,128)S(1)}, u32[]{:S(2)}, u32[]{:S(2)}) collective-permute-start(f32[16,256]{1,0:T(8,128)S(1)} %slice.256), channel_id=1, source_target_pairs={{0,32},{32,0},{1,33},{33,1},{2,34},{34,2},{3,35},{35,3},{4,36},{36... | collective-permute-start | bytes 49160 | tf_op jit(solution)/shard_map/ppermute | solution.py:293
  70.0 21.2 %all-to-all-start.1 = ((f32[128,1,512]{2,1,0:T(1,128)}), f32[128,1,512]{2,1,0:T(1,128)S(1)}, u32[]{:S(2)}, u32[]{:S(2)}) async-start(f32[128,1,512]{2,1,0:T(1,128)} %copy.6), calls=%async_computation.1 | async-start | bytes 524288 | tf_op jit(solution)/shard_map/all_to_all | solution.py:301
  77.1 14.2 %collective-permute-start.17 = (f32[32,256]{1,0:T(8,128)S(1)}, f32[32,256]{1,0:T(8,128)S(1)}, u32[]{:S(2)}, u32[]{:S(2)}) collective-permute-start(f32[32,256]{1,0:T(8,128)S(1)} %pad_maximum_fusion.4.part_0), channel_id=1, source_target_pairs={{0,64},{64,0},{128,192},{192,128},{1,65},{65,1},{129,193},{193,129... | collective-permute-start | bytes 98312 | tf_op jit(solution)/shard_map/ppermute | solution.py:297
  77.9 13.4 %collective-permute-start.18 = (f32[32,256]{1,0:T(8,128)S(1)}, f32[32,256]{1,0:T(8,128)S(1)}, u32[]{:S(2)}, u32[]{:S(2)}) collective-permute-start(f32[32,256]{1,0:T(8,128)S(1)} %pad_maximum_fusion.4.part_0), channel_id=1, source_target_pairs={{0,128},{64,192},{128,0},{192,64},{1,129},{65,193},{129,1},{193,65... | collective-permute-start | bytes 98312 | tf_op jit(solution)/shard_map/ppermute | solution.py:297
  80.7 10.6 %collective-permute-start.19 = (f32[32,256]{1,0:T(8,128)S(1)}, f32[32,256]{1,0:T(8,128)S(1)}, u32[]{:S(2)}, u32[]{:S(2)}) collective-permute-start(f32[32,256]{1,0:T(8,128)S(1)} %pad_maximum_fusion.4.part_0), channel_id=1, source_target_pairs={{0,192},{64,128},{128,64},{192,0},{1,193},{65,129},{129,65},{193,1... | collective-permute-start | bytes 98312 | tf_op jit(solution)/shard_map/ppermute | solution.py:297
  91.3 9.1 %collective-permute-start.20 = (f32[128,256]{1,0:T(8,128)S(1)}, f32[128,256]{1,0:T(8,128)S(1)}, u32[]{:S(2)}, u32[]{:S(2)}) collective-permute-start(f32[128,256]{1,0:T(8,128)S(1)} %get-tuple-element.57.mine_ref), channel_id=1, source_target_pairs={{0,32},{32,0},{1,33},{33,1},{2,34},{34,2},{3,35},{35,3},{4,36},{36... | collective-permute-start | bytes 393224 | tf_op jit(solution)/shard_map/ppermute | solution.py:293
  94.0 18.2 %all-to-all-start.2 = ((f32[128,1,256]{2,1,0:T(1,128)}), f32[128,1,256]{2,1,0:T(1,128)S(1)}, u32[]{:S(2)}, u32[]{:S(2)}) async-start(f32[128,1,256]{2,1,0:T(1,128)} %broadcast_in_dim.19), calls=%async_computation.2 | async-start | bytes 262144 | tf_op jit(solution)/shard_map/all_to_all | solution.py:301
  112.3 2.2 %collective-permute-start.21 = (f32[128,256]{1,0:T(8,128)S(1)}, f32[128,256]{1,0:T(8,128)S(1)}, u32[]{:S(2)}, u32[]{:S(2)}) collective-permute-start(f32[128,256]{1,0:T(8,128)S(1)} %bitcast.82), channel_id=1, source_target_pairs={{0,32},{32,0},{1,33},{33,1},{2,34},{34,2},{3,35},{35,3},{4,36},{36... | collective-permute-start | bytes 393224 | tf_op jit(solution)/shard_map/ppermute | solution.py:293
